TPU v7x, 32 devices: a whole 2x2x4 slice. The times are simulated.
32 devices in a mesh: geo: 4 (over x, core), spec: 8 (over z, y).
Axes of the slice: x: 2, y: 2, z: 4, core: 2. Of those that a mesh axis runs over, the one named last changes fastest.
Arguments:
- spectrum: float32 [32, 36, 128, 512], P('spec', None, 'geo'), may hold values from 0.01 to 50, as said below
- land_sea: int32 [128, 512], P('geo'), may hold values from 0 to 1, as said below
- sea_index: int32 [4, 12288], P('geo'), may hold values from 0 to 16383, as said below
- sea_count: int32 [4], P('geo'), may hold values from 4096 to 12288, as said below
- wind_speed: float32 [128, 512], P('geo'), may hold values from 4 to 24
- wind_dir: float32 [128, 512], P('geo'), may hold values from -3.140625 to 3.140625
- slope_x: float32 [128, 512], P('geo'), may hold values from -0.5 to 0.5
- slope_y: float32 [128, 512], P('geo'), may hold values from -0.5 to 0.5
Outputs:
- next_spectrum: float32 [32, 36, 128, 512], P('spec', None, 'geo')
Inputs may be any that keep to these rules, and one draw needn't show every extreme that they name: `spectrum`: A positive energy density. `land_sea`: land comes in aligned 8 x 8 blocks of cells. `sea_index`: row t lists the sea cells of tile t in increasing position, then its land cells in increasing position, all distinct; its first sea_count[t] entries are exactly the tile's sea cells. `sea_count`: the number of sea cells of each tile; at least one tile has exactly 12288.
All inputs are finite; a program needn't handle non-finite values.
Results may differ from a plain program's by a relative error of at most 0.0003.
Values sent between devices are 32-bit elements; how exact they have to be, the bound alone decides.
No kernel may reach another device: no remote copies, remote signals or barrier semaphores. Data moves between devices by JAX's collectives and lax.ppermute only.
A program may use at most 128 MiB of HBM per device.

v0:
```python
import math

import jax
import jax.numpy as jnp
from jax import lax
from jax.sharding import PartitionSpec as P

GRAVITY = 9.81
BASE_FREQ = 0.035
GROWTH = 1.1
COURANT_TOP = 0.9
TURN_TOP = 1.2
SPACING = 0.1
USTAR_RATIO = 0.035
WIND_COEF = 0.0375
WHITECAP = 0.36
STEEP_REF = 1.6
EPSILON = 1e-06
QUAD_COEF = 100.0


def extended(cells, sides, width):
    for axis, dim in sides:
        count = lax.axis_size(axis)
        ends = count - 1
        head = lax.slice_in_dim(cells, 0, width, axis=dim)
        tail = lax.slice_in_dim(cells, cells.shape[dim] - width, cells.shape[dim], axis=dim)
        cells = jnp.concatenate(
            [
                lax.ppermute(tail, axis, [(i, (i + 1) % count) for i in range(ends)]),
                cells,
                lax.ppermute(head, axis, [((i + 1) % count, i) for i in range(ends)]),
            ],
            axis=dim,
        )
    return cells


def band_table(band_ids):
    growth_factor = jnp.power(GROWTH, band_ids)
    radian_freq = 2.0 * math.pi * BASE_FREQ * growth_factor
    wavenum = radian_freq * radian_freq / GRAVITY
    return (
        radian_freq,
        wavenum,
        COURANT_TOP / growth_factor,
        TURN_TOP / growth_factor,
        SPACING * radian_freq,
    )


def quick_flux(far_left, near_left, near_right, far_right, courant):
    forward = courant >= 0
    upwind = jnp.where(forward, far_left, far_right)
    center = jnp.where(forward, near_left, near_right)
    downwind = jnp.where(forward, near_right, near_left)
    face_value = (
        0.5 * (center + downwind)
        - 0.5 * jnp.abs(courant) * (downwind - center)
        - (1.0 - courant * courant) / 6.0 * (downwind - 2.0 * center + upwind)
    )
    return courant * face_value


def advect(padded, courant, along):
    face_count = padded.shape[along] - 4
    shifted = [
        lax.slice_in_dim(padded, offset, offset + face_count + 1, axis=along) for offset in range(4)
    ]
    face_flux = quick_flux(shifted[0], shifted[1], shifted[2], shifted[3], courant)
    centre_cells = lax.slice_in_dim(padded, 2, 2 + face_count, axis=along)
    upper_flux = lax.slice_in_dim(face_flux, 1, face_count + 1, axis=along)
    lower_flux = lax.slice_in_dim(face_flux, 0, face_count, axis=along)
    return centre_cells - (upper_flux - lower_flux)


def quad_delta(center, above, below, energy, dir_axis):
    plus = jnp.roll(above, -1, axis=dir_axis)
    minus = jnp.roll(below, 3, axis=dir_axis)
    return (
        QUAD_COEF
        * (center * center * (plus + minus) - 2.0 * center * plus * minus)
        / (energy * energy)
    )


def quad_term(delta, delta_above, delta_below, dir_axis):
    return (
        -2.0 * delta
        + jnp.roll(delta_below, 1, axis=dir_axis)
        + jnp.roll(delta_above, -3, axis=dir_axis)
    )


def band_neighbours(values):
    empty = jnp.zeros((1,) + values.shape[1:], jnp.float32)
    return (
        jnp.concatenate([values[1:], empty], axis=0),
        jnp.concatenate([empty, values[:-1]], axis=0),
    )


def sources(density, energy_sum, first_sum, root_sum, radian_freq, wavenum, cosine, wind_speed):
    energy = energy_sum + EPSILON
    mean_sigma = energy / (first_sum + EPSILON)
    ratio_k = energy / (root_sum + EPSILON)
    mean_k = ratio_k * ratio_k
    steepness = energy * mean_k * mean_k / STEEP_REF
    decay_rate = WHITECAP * mean_sigma * (wavenum / mean_k) * steepness * steepness
    growth_rate = (
        WIND_COEF
        * radian_freq
        * jnp.maximum(28.0 * USTAR_RATIO * wind_speed * radian_freq / GRAVITY * cosine - 1.0, 0.0)
    )
    return density * (1.0 + growth_rate) / (1.0 + decay_rate)


def local_sources(point_block, wind_block, wind_angle, angles, dtheta):
    band_total = point_block.shape[0]
    band_ids = jnp.arange(band_total).astype(jnp.float32)
    radian_freq, wavenum, courant, turn_rate, band_spread = band_table(band_ids)
    scaled = point_block * (band_spread * dtheta)[:, None, None]
    energy_sum = jnp.sum(scaled, axis=(0, 1))
    first_sum = jnp.sum(scaled / radian_freq[:, None, None], axis=(0, 1))
    root_sum = jnp.sum(scaled / jnp.sqrt(wavenum)[:, None, None], axis=(0, 1))
    energy = energy_sum + EPSILON
    above, below = band_neighbours(point_block)
    delta = quad_delta(point_block, above, below, energy, 1)
    delta_above, delta_below = band_neighbours(delta)
    extra = quad_term(delta, delta_above, delta_below, 1)
    cosine = jnp.cos(angles[:, None] - wind_angle[None, :])
    return (
        sources(
            point_block,
            energy_sum,
            first_sum,
            root_sum,
            radian_freq[:, None, None],
            wavenum[:, None, None],
            cosine,
            wind_block,
        )
        + extra
    )


def shards(spectrum, land_sea, sea_index, sea_count, wind_speed, wind_dir, slope_x, slope_y):
    local_bands, dir_count, row_count, col_count = spectrum.shape
    spec_count = lax.axis_size("spec")
    spec_pos = lax.axis_index("spec")
    band_total = local_bands * spec_count
    tile_cells = row_count * col_count
    dtheta = 2.0 * math.pi / dir_count
    angles = (jnp.arange(dir_count).astype(jnp.float32) + 0.5) * dtheta
    face_angles = jnp.arange(dir_count + 1).astype(jnp.float32) * dtheta
    band_ids = (spec_pos * local_bands + jnp.arange(local_bands)).astype(jnp.float32)
    radian_freq, wavenum, courant, turn_rate, band_spread = band_table(band_ids)
    wet_mask = land_sea.astype(jnp.float32)
    density = spectrum * wet_mask
    padded = extended(density, (("geo", 2),), 2)
    density = (
        advect(padded, (courant[:, None] * jnp.cos(angles)[None, :])[:, :, None, None], 2)
        * wet_mask
    )
    padded = jnp.pad(density, ((0, 0), (0, 0), (0, 0), (2, 2)))
    density = (
        advect(padded, (courant[:, None] * jnp.sin(angles)[None, :])[:, :, None, None], 3)
        * wet_mask
    )
    turning = turn_rate[:, None, None, None] * (
        jnp.sin(face_angles)[None, :, None, None] * slope_x
        - jnp.cos(face_angles)[None, :, None, None] * slope_y
    )
    padded = jnp.concatenate([density[:, -2:], density, density[:, :2]], axis=1)
    floored = jnp.maximum(advect(padded, turning, 1), 0.0)
    per_device = tile_cells // spec_count
    outgoing = floored.reshape(local_bands, dir_count, spec_count, per_device)
    point_block = lax.all_to_all(outgoing, "spec", split_axis=2, concat_axis=0, tiled=True).reshape(
        band_total, dir_count, per_device
    )
    wind_block = lax.dynamic_slice_in_dim(
        wind_speed.reshape(tile_cells), spec_pos * per_device, per_device
    )
    wind_angle = lax.dynamic_slice_in_dim(
        wind_dir.reshape(tile_cells), spec_pos * per_device, per_device
    )
    wet_block = lax.dynamic_slice_in_dim(
        wet_mask.reshape(tile_cells), spec_pos * per_device, per_device
    )
    updated = local_sources(point_block, wind_block, wind_angle, angles, dtheta) * wet_block
    returned = lax.all_to_all(
        updated.reshape(band_total, dir_count, 1, per_device),
        "spec",
        split_axis=0,
        concat_axis=2,
        tiled=True,
    )
    return returned.reshape(local_bands, dir_count, row_count, col_count)


def solution(mesh):
    placed = (
        P("spec", None, "geo", None),
        P("geo", None),
        P("geo", None),
        P("geo"),
        P("geo", None),
        P("geo", None),
        P("geo", None),
        P("geo", None),
    )
    return jax.shard_map(
        shards, mesh=mesh, in_specs=placed, out_specs=P("spec", None, "geo", None), check_vma=False
    )
```

profile of v0, /device:TPU:0, one launch (start us, length us, event | category | flops | bytes accessed | tf_op | source)
XLA Modules:
  0.0 737.1 jit_solution(15412723203871536779)
XLA Ops:
  0.0 0.8 convert_bitcast_fusion
  0.9 0.0 copy-start.4
  0.9 9.2 %copy_multiply_fusion = f32[4,36,32,512]{3,1,2,0:T(8,128)S(1)} fusion(f32[4,36,32,512]{3,2,1,0:T(8,128)} %param.8, f32[32,512]{1,0:T(8,128)S(1)} %get-tuple-element.23), kind=kLoop, calls=%fused_computation.50 | loop fusion | flops 2359296 | bytes 18939904 | tf_op jit(solution)/shard_map/mul | solution.py:159
  10.1 3.8 copy-done.1
  13.9 1.0 fusion.64
  14.9 1.3 collective-permute-start.1
  16.2 3.6 collective-permute-start
  19.9 0.1 multiply_compare_fusion.1
  20.0 0.1 broadcast_multiply_fusion
  20.1 1.3 multiply_subtract_fusion
  21.4 0.0 collective-permute-done.1
  21.4 21.1 %fusion.14 = f32[4,36,33,512]{3,1,2,0:T(8,128)} fusion(f32[4,36,2,512]{3,1,2,0:T(8,128)S(1)} %collective-permute-done.1, f32[4,36,32,512]{3,1,2,0:T(8,128)} %copy-done.1, f32[4,36,2,512]{3,1,2,0:T(8,128)S(1)} %collective-permute-done, f32[4,36]{1,0:T(4,128)S(1)} %get-tuple-element.37, f32[4,36]{1,0:T(4,128)S(1)} %get-tuple-element.36, ...), kind=kLoop, calls=%fused_computation.27 | loop fusion | flops 43794432 | bytes 20350800 | tf_op jit(solution)/shard_map/mul | solution.py:62
  42.5 13.9 %fusion.28 = f32[4,36,32,512]{3,1,2,0:T(8,128)S(1)} fusion(f32[4,36,33,512]{3,1,2,0:T(8,128)} %fusion.14, f32[32,512]{1,0:T(8,128)S(1)} %get-tuple-element.23, f32[4,36,32,512]{3,2,1,0:T(8,128)} %param.8), kind=kLoop, calls=%fused_computation.49 | loop fusion | flops 9437184 | bytes 37814272 | tf_op jit(solution)/shard_map/mul | solution.py:162
  56.4 12.7 %fusion.4 = f32[4,36,32,513]{3,1,2,0:T(8,128)} fusion(f32[4,36,32,512]{3,1,2,0:T(8,128)S(1)} %fusion.28, f32[4,36]{1,0:T(4,128)S(1)} %get-tuple-element.29, f32[4,36]{1,0:T(4,128)S(1)} %get-tuple-element.30, f32[4,36]{1,0:T(4,128)S(1)} %get-tuple-element.28, pred[4,36]{1,0:T(4,128)(4,1)S(1)} %get-tuple-element.34), kind=kLoop, calls=%fused_computation.12 | loop fusion | flops 33094656 | bytes 18894672 | tf_op jit(solution)/shard_map/mul | solution.py:62
  69.1 9.4 %fusion.26 = f32[4,36,32,512]{3,1,2,0:T(8,128)S(1)} fusion(f32[4,36,32,512]{3,1,2,0:T(8,128)S(1)} %fusion.28, f32[4,36,32,513]{3,1,2,0:T(8,128)} %fusion.4, f32[32,512]{1,0:T(8,128)S(1)} %get-tuple-element.23), kind=kLoop, calls=%fused_computation.46 | loop fusion | flops 7077888 | bytes 37814272 | tf_op jit(solution)/shard_map/mul | solution.py:167
  78.4 0.5 fusion.63
  79.0 11.0 %multiply_multiply_fusion = f32[4,37,32,512]{3,1,2,0:T(8,128)S(1)} fusion(f32[4,2,32,512]{3,1,2,0:T(2,128)S(1)} %get-tuple-element.9, f32[4,36,32,512]{3,1,2,0:T(8,128)S(1)} %fusion.26, f32[4,2,32,512]{3,1,2,0:T(2,128)S(1)} %get-tuple-element.8, f32[37,32,512]{2,0,1:T(8,128)S(1)} %multiply_subtract_fusion, f32[4]{0:T(128)S(1)} %broadcast_multiply_fusion.2), kind=kLoop, calls=%fused_computation | loop fusion | flops 60620800 | bytes 22609936 | tf_op jit(solution)/shard_map/mul | solution.py:62
  90.0 6.0 fusion.24
  96.0 13.2 %copy.129 = f32[4,36,32,512]{3,2,1,0:T(8,128)} copy(f32[4,36,32,512]{3,1,2,0:T(8,128)} %fusion.24) | data formatting | bytes 18874368 | tf_op jit(solution)/shard_map/max | solution.py:175
  109.2 12.6 %reshape.740 = f32[4,36,8,2048]{3,2,1,0:T(8,128)} reshape(f32[4,36,32,512]{3,2,1,0:T(8,128)} %copy.129) | data formatting | bytes 18874368 | tf_op jit(solution)/shard_map/reshape | solution.py:177
  121.8 13.5 %copy.130 = f32[4,36,8,2048]{3,0,1,2:T(4,128)} copy(f32[4,36,8,2048]{3,2,1,0:T(8,128)} %reshape.740) | data formatting | bytes 18874368 | tf_op jit(solution)/shard_map/reshape | solution.py:177
  135.3 7.7 %all-to-all-start = ((f32[4,36,8,2048]{3,0,1,2:T(4,128)}), f32[4,36,8,2048]{3,0,1,2:T(4,128)}, u32[]{:S(2)}, u32[]{:S(2)}) async-start(f32[4,36,8,2048]{3,0,1,2:T(4,128)} %copy.130), calls=%async_computation | async-start | bytes 18874368 | tf_op jit(solution)/shard_map/all_to_all | solution.py:178
  143.2 0.8 multiply_multiply_fusion.2
  144.0 1.1 subtract_cosine_fusion
  145.1 200.0 %all-to-all-done = f32[4,36,8,2048]{3,0,1,2:T(4,128)} async-done(((f32[4,36,8,2048]{3,0,1,2:T(4,128)}), f32[4,36,8,2048]{3,0,1,2:T(4,128)}, u32[]{:S(2)}, u32[]{:S(2)}) %all-to-all-start) | async-done | bytes 9437216 | tf_op jit(solution)/shard_map/all_to_all | solution.py:178
  345.1 11.7 %copy.135 = f32[8,4,36,1,2048]{4,1,0,2,3:T(4,128)} copy(f32[8,4,36,1,2048]{4,1,2,0,3:T(4,128)} %bitcast.1) | data formatting | bytes 18874368 | tf_op jit(solution)/shard_map/all_to_all | solution.py:178
  356.8 11.9 %reshape.744 = f32[32,36,2048]{2,0,1:T(8,128)} reshape(f32[8,4,36,1,2048]{4,1,0,2,3:T(4,128)} %copy.135) | data formatting | bytes 18874368 | tf_op jit(solution)/shard_map/reshape | solution.py:178
  368.7 11.5 %fusion.66 = (f32[31,36,2048]{2,0,1:T(8,128)S(1)}, f32[31,36,2048]{2,0,1:T(8,128)}) fusion(f32[32,36,2048]{2,0,1:T(8,128)} %reshape.744), kind=kLoop, calls=%fused_computation.133 | loop fusion | bytes 36569088 | tf_op jit(solution)/shard_map/slice | solution.py:98
  380.3 11.7 %fusion.61 = (f32[32,33,1,2048]{3,0,1,2:T(8,128)}, f32[32,33,2048]{2,0,1:T(8,128)}) fusion(f32[31,36,2048]{2,0,1:T(8,128)} %get-tuple-element.21), kind=kLoop, calls=%fused_computation.128 | loop fusion | bytes 26443776 | tf_op jit(solution)/shard_map/jit(_roll_static)/concatenate | solution.py:79
  392.0 2.7 fusion.60
  394.7 0.7 pad_slice_fusion.13
  395.4 8.0 %fusion.62 = (f32[32,35,1,2048]{3,0,1,2:T(8,128)}, f32[32,35,2048]{2,0,1:T(8,128)}) fusion(f32[31,36,2048]{2,0,1:T(8,128)S(1)} %get-tuple-element.20), kind=kLoop, calls=%fused_computation.129 | loop fusion | bytes 27492352 | tf_op jit(solution)/shard_map/jit(_roll_static)/concatenate | solution.py:78
  403.4 8.7 %divide_reduce_fusion.1 = (f32[2048]{0:T(1024)S(1)}, f32[2048]{0:T(1024)S(1)}, f32[2048]{0:T(1024)S(1)}) fusion(f32[8,4]{1,0:T(8,128)S(1)} %get-tuple-element.44, f32[8,4]{1,0:T(8,128)S(1)} %fusion.46, f32[4,36,8,2048]{3,0,1,2:T(4,128)} %all-to-all-done, f32[8,4]{1,0:T(8,128)S(1)} %get-tuple-element.43), kind=kLoop, calls=%fused_computation.69 | loop fusion | flops 14149632 | bytes 9462144 | tf_op jit(solution)/shard_map/reduce_sum | solution.py:124
  412.2 10.3 %multiply_divide_fusion = f32[32,36,2048]{2,0,1:T(8,128)} fusion(f32[32,36,2048]{2,0,1:T(8,128)S(1)} %bitcast.58, f32[32,33,2048]{2,0,1:T(8,128)} %get-tuple-element.17, f32[32,3,2048]{2,0,1:T(8,128)} %get-tuple-element.15, f32[32,1,2048]{2,0,1:T(8,128)S(1)} %copy-done.3, f32[32,35,2048]{2,0,1:T(8,128)S(1)} %copy-done.2, f32[2048]{0:T(1024)S(1)} %get-tuple-element.27), kind=kLoop, calls=%fused_computation.67 | loop fusion | flops 25952256 | bytes 37756928 | tf_op jit(solution)/shard_map/div | solution.py:81
  422.5 15.0 %fusion.65 = (f32[31,36,2048]{2,0,1:T(8,128)}, f32[31,36,2048]{2,0,1:T(8,128)}) fusion(f32[32,36,2048]{2,0,1:T(8,128)} %multiply_divide_fusion), kind=kLoop, calls=%fused_computation.132 | loop fusion | bytes 36569088 | tf_op jit(solution)/shard_map/slice | solution.py:98
  437.5 9.3 %slice_bitcast_fusion = f32[32,35,1,2048]{3,0,2,1:T(8,128)} fusion(f32[31,36,2048]{2,0,1:T(8,128)} %get-tuple-element.19), kind=kLoop, calls=%fused_computation.70 | loop fusion | bytes 18317312 | tf_op jit(solution)/shard_map/jit(_roll_static)/concatenate | solution.py:90
  446.8 1.8 fusion.43
  448.7 2.0 copy-done
  450.7 0.9 fusion.39
  451.6 4.3 fusion.38
  455.9 12.2 %copy.131 = f32[8,4,36,1,2048]{4,3,2,1,0:T(1,128)} copy(f32[8,4,36,1,2048]{4,1,2,0,3:T(4,128)} %bitcast.1) | data formatting | bytes 18874368 | tf_op jit(solution)/shard_map/all_to_all | solution.py:178
  468.0 0.7 fusion.67
  468.7 0.1 fusion.42
  468.9 20.5 %fusion.31 = f32[32,36,1,2048]{3,0,2,1:T(8,128)S(1)} fusion(f32[32,35,1,2048]{3,0,2,1:T(8,128)} %slice_bitcast_fusion, f32[32,1,1,2048]{3,0,2,1:T(8,128)} %fusion.43, f32[32,3,1,2048]{3,0,2,1:T(8,128)} %fusion.39, f32[32,33,1,2048]{3,0,2,1:T(8,128)} %fusion.38, f32[32,36,1,2048]{3,2,1,0:T(1,128)} %bitcast.60, f32[32,33,1,2048]{3,0,1,2:T(8,128)} %get-tuple-element.16, ...), kind=kLoop, calls=%fused_computation.58 | loop fusion | flops 58982400 | bytes 57458816 | tf_op jit(solution)/shard_map/mul | solution.py:190
  489.3 12.6 %copy.140 = f32[32,36,1,2048]{3,2,1,0:T(1,128)S(1)} copy(f32[32,36,1,2048]{3,0,2,1:T(8,128)S(1)} %fusion.31) | data formatting | bytes 18874368 | tf_op jit(solution)/shard_map/mul | solution.py:190
  501.9 214.1 %all_to_all.30 = f32[32,36,1,2048]{3,2,1,0:T(1,128)S(1)} all-to-all(f32[32,36,1,2048]{3,2,1,0:T(1,128)S(1)} %copy.140), channel_id=1, replica_groups=mesh['geo'=4,'spec'=8] {'spec'}, dimensions={0} | all-to-all | bytes 18874368 | tf_op jit(solution)/shard_map/all_to_all | solution.py:191
  716.0 9.1 %copy.141 = f32[4,36,8,1,2048]{4,2,1,0,3:T(8,128)} copy(f32[4,36,8,1,2048]{4,3,1,0,2:T(1,128)S(1)} %bitcast.59) | data formatting | bytes 18874368 | tf_op jit(solution)/shard_map/all_to_all | solution.py:191
  725.2 11.7 %reshape.746 = f32[4,36,32,512]{3,2,1,0:T(8,128)} reshape(f32[4,36,8,1,2048]{4,2,1,0,3:T(8,128)} %copy.141) | data formatting | bytes 18874368 | tf_op jit(solution)/shard_map/reshape | solution.py:198
  (36 shorter events, 0.3 us)
Async XLA Ops:
  0.9 19.2 %copy-start.4 = (f32[32,512]{1,0:T(8,128)S(1)}, f32[32,512]{1,0:T(8,128)}, u32[]{:S(2)}) copy-start(f32[32,512]{1,0:T(8,128)} %param.13) | copy-start | bytes 196612
  10.1 3.9 copy-start.1
  14.9 6.5 collective-permute-start.1
  16.2 5.2 collective-permute-start
  135.3 7.7 %copy-start.5 = (f32[32,512]{1,0:T(8,128)S(1)}, f32[32,512]{1,0:T(8,128)}, u32[]{:S(2)}) copy-start(f32[32,512]{1,0:T(8,128)} %param.11) | copy-start | bytes 196612
  135.3 7.8 %copy-start.6 = (f32[32,512]{1,0:T(8,128)S(1)}, f32[32,512]{1,0:T(8,128)}, u32[]{:S(2)}) copy-start(f32[32,512]{1,0:T(8,128)} %param.10) | copy-start | bytes 196612
  135.3 209.8 %all-to-all-start = ((f32[4,36,8,2048]{3,0,1,2:T(4,128)}), f32[4,36,8,2048]{3,0,1,2:T(4,128)}, u32[]{:S(2)}, u32[]{:S(2)}) async-start(f32[4,36,8,2048]{3,0,1,2:T(4,128)} %copy.130), calls=%async_computation | async-start | bytes 18874368 | tf_op jit(solution)/shard_map/all_to_all | solution.py:178
  394.7 17.5 %slice-start = ((s8[9437184]{0:T(1024)(128)(4,1)}), s8[4194304]{0:T(1024)(128)(4,1)S(1)}, s32[]{:S(2)}) async-start(s8[9437184]{0:T(1024)(128)(4,1)} %bitcast.57), calls=%async_computation.2 | async-start | bytes 8388608
  395.4 16.8 %slice-start.1 = ((s8[9437184]{0:T(1024)(128)(4,1)}), s8[4194304]{0:T(1024)(128)(4,1)S(1)}, s32[]{:S(2)}) async-start(s8[9437184]{0:T(1024)(128)(4,1)} %bitcast.57), calls=%async_computation.3 | async-start | bytes 8388608
  395.4 16.8 %slice-start.2 = ((s8[9437184]{0:T(1024)(128)(4,1)}), s8[1048576]{0:T(1024)(128)(4,1)S(1)}, s32[]{:S(2)}) async-start(s8[9437184]{0:T(1024)(128)(4,1)} %bitcast.57), calls=%async_computation.4 | async-start | bytes 2097152
  403.4 8.8 %copy-start.2 = (f32[32,35,2048]{2,0,1:T(8,128)S(1)}, f32[32,35,2048]{2,0,1:T(8,128)}, u32[]{:S(2)}) copy-start(f32[32,35,2048]{2,0,1:T(8,128)} %get-tuple-element.13) | copy-start | bytes 27525124
  403.4 8.8 %copy-start.3 = (f32[32,1,2048]{2,0,1:T(8,128)S(1)}, f32[32,1,2048]{2,0,1:T(8,128)}, u32[]{:S(2)}) copy-start(f32[32,1,2048]{2,0,1:T(8,128)} %pad_slice_fusion.13) | copy-start | bytes 786436
  446.8 3.9 copy-start
where the time goes:
time: 743 us; the launch traced here: 737 us
  blocking collectives  214 us (29%)
  waiting for transfers between devices  200 us (27%)
  local copies, waits for them, and re-layouts  183 us (25%)
  other arithmetic  127 us (17%)
  starting transfers between devices  12.6 us (2%)
    all_to_all x1, blocking collectives, shards(): lax.all_to_all(updated.reshape(band_total, dir_count, 1, per_device), 'sp...  214 us
    all_to_all x1, waiting for transfers between devices, shards(): lax.all_to_all(outgoing, 'spec', split_axis=2, concat_axis=0, tiled=True)  200 us
    mul x3, other arithmetic, quick_flux(): return courant * face_value  44.8 us
    slice x2, local copies, waits for them, and re-layouts, band_neighbours(): values[1:]  26.5 us
    reshape x2, local copies, waits for them, and re-layouts, shards(): outgoing = floored.reshape(local_bands, dir_count, spec_count, per_device)  26.1 us
    all_to_all x2, local copies, waits for them, and re-layouts, shards(): lax.all_to_all(outgoing, 'spec', split_axis=2, concat_axis=0, tiled=True)  23.8 us
    mul x1, other arithmetic, shards(): local_sources(point_block, wind_block, wind_angle, angles, dtheta)  20.5 us
  transfers between devices with their start and end apart: 3, of which 1 were waited for; matrix products, arithmetic and copies ran while one was open for 0% of the time, Pallas kernels for 0%

commit v1 on v0

v1 whole, which is shorter than its diff:
```python
import functools
import math

import jax
import jax.numpy as jnp
import numpy as np
from jax import lax
from jax.experimental import pallas as pl
from jax.experimental.pallas import tpu as pltpu
from jax.sharding import PartitionSpec as P

GRAVITY = 9.81
BASE_FREQ = 0.035
GROWTH = 1.1
COURANT_TOP = 0.9
TURN_TOP = 1.2
SPACING = 0.1
USTAR_RATIO = 0.035
WIND_COEF = 0.0375
WHITECAP = 0.36
STEEP_REF = 1.6
EPSILON = 1e-06
QUAD_COEF = 100.0

STRIP = 8
LANES = 128
VMEM_BYTES = 56 * 1024 * 1024


def tables(band_total, dir_count):
    dtheta = 2.0 * math.pi / dir_count
    angles = (np.arange(dir_count) + 0.5) * dtheta
    faces = np.arange(dir_count) * dtheta
    parts = [
        np.abs(np.cos(angles)),
        np.abs(np.sin(angles)),
        np.sin(faces),
        np.cos(faces),
        np.cos(angles),
        np.sin(angles),
        GROWTH ** np.arange(band_total),
    ]
    return np.concatenate(parts).astype(np.float32)


def sign_runs(dir_count):
    angles = (np.arange(dir_count) + 0.5) * 2.0 * math.pi / dir_count
    signs = [(bool(np.cos(a) >= 0), bool(np.sin(a) >= 0)) for a in angles]
    runs, first = [], 0
    for j in range(1, dir_count + 1):
        if j == dir_count or signs[j] != signs[first]:
            runs.append((first, j) + signs[first])
            first = j
    return runs


def plan_kernel(kept, spill, land_ref, *out_refs):
    cols = land_ref.shape[1]
    flags = [land_ref[STRIP * s : STRIP * s + 1, :].astype(jnp.float32) for s in (spill,) + tuple(kept)]
    rows = [flags[0]] + [1.0 - flag for flag in flags[1:]]
    rows += [jnp.zeros((1, cols), jnp.float32)] * (8 - len(rows))
    table = jnp.concatenate(rows, axis=0)
    first = lax.broadcasted_iota(jnp.int32, (cols, cols), 0)
    second = lax.broadcasted_iota(jnp.int32, (cols, cols), 1)
    block = STRIP
    before = jnp.where(
        jnp.logical_and(first < second // block * block, first % block == 0), 1.0, 0.0
    ).astype(jnp.bfloat16)
    before_t = jnp.where(
        jnp.logical_and(second < first // block * block, second % block == 0), 1.0, 0.0
    ).astype(jnp.bfloat16)
    same = jnp.where(first == second, 1.0, 0.0).astype(jnp.bfloat16)
    narrow = table.astype(jnp.bfloat16)
    ranks = jnp.dot(narrow, before, preferred_element_type=jnp.float32)
    dims = (((1,), (1,)), ((), ()))
    rank_col = lax.dot_general(before_t, narrow, dims, preferred_element_type=jnp.float32)[:, 0:1]
    flag_col = lax.dot_general(same, narrow, dims, preferred_element_type=jnp.float32)[:, 0:1]
    wanted = jnp.where(flag_col > 0.5, rank_col, -1.0)
    phase = first % block == second % block
    offset = jnp.zeros((1, 1), jnp.float32)
    for index, out_ref in enumerate(out_refs):
        hole = table[index + 1 : index + 2, :]
        place = jnp.where(hole > 0.5, ranks[index + 1 : index + 2, :] + offset, -2.0)
        match = jnp.logical_and(phase, jnp.abs(wanted - place) < 0.5)
        out_ref[...] = jnp.where(match, 1.0, 0.0).astype(jnp.bfloat16)
        offset = offset + jnp.sum(hole, axis=1, keepdims=True) * (1.0 / block)


def plan(land_sea, kept, spill):
    cols = land_sea.shape[1]
    return pl.pallas_call(
        functools.partial(plan_kernel, kept, spill),
        out_shape=[jax.ShapeDtypeStruct((cols, cols), jnp.bfloat16)] * len(kept),
        compiler_params=pltpu.CompilerParams(vmem_limit_bytes=VMEM_BYTES),
        name="plan",
    )(land_sea)


def taps(courant):
    rest = (1.0 - courant * courant) * (1.0 / 6.0)
    down = courant * (0.5 - 0.5 * courant - rest)
    centre = courant * (0.5 + 0.5 * courant + 2.0 * rest)
    far = -courant * rest
    return -down, 1.0 - centre + down, centre - far, far


def row_shift(before, cells, after, shift, row_ids):
    if shift > 0:
        return jnp.where(row_ids < shift, pltpu.roll(before, shift, 0), pltpu.roll(cells, shift, 0))
    count = cells.shape[0]
    return jnp.where(
        row_ids >= count + shift, pltpu.roll(after, count + shift, 0), pltpu.roll(cells, count + shift, 0)
    )


def lane_shift(pieces, shift, lane_ids):
    rolled = [pltpu.roll(piece, shift % LANES, 1) for piece in pieces]
    zero = jnp.zeros_like(pieces[0])
    moved = []
    for index in range(len(pieces)):
        if shift > 0:
            other = rolled[index - 1] if index > 0 else zero
            moved.append(jnp.where(lane_ids < shift, other, rolled[index]))
        else:
            other = rolled[index + 1] if index + 1 < len(pieces) else zero
            moved.append(jnp.where(lane_ids >= LANES + shift, other, rolled[index]))
    return moved


def exact_dot(cells, chooser, split_ref, dims):
    count = cells.shape[0]
    high = cells.astype(jnp.bfloat16)
    rest = cells - high.astype(jnp.float32)
    mid = rest.astype(jnp.bfloat16)
    low = (rest - mid.astype(jnp.float32)).astype(jnp.bfloat16)
    split_ref[0:count, :] = high
    split_ref[count : 2 * count, :] = mid
    split_ref[2 * count : 3 * count, :] = low
    product = lax.dot_general(split_ref[...], chooser, dims, preferred_element_type=jnp.float32)
    return product[0:count] + product[count : 2 * count] + product[2 * count : 3 * count]


def propagate_kernel(strips, spill_slot, dests, edge, group, band_total, dir_count, local_bands, *refs):
    refs = list(refs)
    pos_ref, tab_ref, spec_ref, land_ref, sx_ref, sy_ref = refs[:6]
    refs = refs[6:]
    lower_ref = upper_ref = spill_ref = None
    if edge:
        lower_ref, upper_ref, spill_ref = refs[:3]
        refs = refs[3:]
    choosers = refs[: len(dests)]
    refs = refs[len(dests) :]
    out_refs = refs[: len(strips)]
    refs = refs[len(strips) :]
    send_refs = refs[: len(dests)]
    refs = refs[len(dests) :]
    sum_ref = refs[0]
    refs = refs[1:]
    head_ref = tail_ref = None
    if not edge:
        head_ref, tail_ref = refs[:2]
        refs = refs[2:]
    turn_ref, moved_ref, split_ref = refs

    row_count, cols = land_ref.shape
    step = pl.program_id(0)
    band = pos_ref[0] * local_bands + group + step
    growth = tab_ref[6 * dir_count + band]
    courant = COURANT_TOP / growth
    turn_rate = TURN_TOP / growth
    radian_freq = (2.0 * math.pi * BASE_FREQ) * growth
    weight = SPACING * radian_freq * (2.0 * math.pi / dir_count)
    row_ids = lax.broadcasted_iota(jnp.int32, (STRIP, cols), 0)
    lane_ids = lax.broadcasted_iota(jnp.int32, (STRIP, LANES), 1)

    def wet(s):
        return land_ref[STRIP * s : STRIP * (s + 1), :].astype(jnp.float32)

    @pl.when(step == 0)
    def _():
        sum_ref[...] = jnp.zeros_like(sum_ref)

        @pl.loop(0, dir_count)
        def _(f):
            face_sin = tab_ref[2 * dir_count + f]
            face_cos = tab_ref[3 * dir_count + f]
            for slot, s in enumerate(strips):
                rows = slice(STRIP * s, STRIP * (s + 1))
                turn_ref[slot, f] = face_sin * sx_ref[rows, :] - face_cos * sy_ref[rows, :]

    if not edge:
        wet_head = land_ref[0:2, :].astype(jnp.float32)
        wet_tail = land_ref[row_count - 2 : row_count, :].astype(jnp.float32)

    for first, last, cos_up, sin_up in sign_runs(dir_count):

        @pl.loop(first, last)
        def _(j):
            row_taps = taps(courant * tab_ref[j])
            col_taps = taps(courant * tab_ref[dir_count + j])
            if not edge:
                head_ref[0, j] = spec_ref[0, j, 0:2, :] * wet_head
                tail_ref[0, j] = spec_ref[0, j, row_count - 2 : row_count, :] * wet_tail
            for slot, s in enumerate(strips):
                wet_s = wet(s)
                cells = spec_ref[0, j, STRIP * s : STRIP * (s + 1), :] * wet_s
                if s == 0:
                    before = jnp.concatenate(
                        [jnp.zeros((STRIP - 2, cols), jnp.float32), lower_ref[0, j]], axis=0
                    )
                else:
                    before = spec_ref[0, j, STRIP * (s - 1) : STRIP * s, :] * wet(s - 1)
                if STRIP * (s + 1) == row_count:
                    after = jnp.concatenate(
                        [upper_ref[0, j], jnp.zeros((STRIP - 2, cols), jnp.float32)], axis=0
                    )
                else:
                    after = spec_ref[0, j, STRIP * (s + 1) : STRIP * (s + 2), :] * wet(s + 1)
                way = 1 if cos_up else -1
                cells = (
                    row_taps[1] * cells
                    + row_taps[0] * row_shift(before, cells, after, -way, row_ids)
                    + row_taps[2] * row_shift(before, cells, after, way, row_ids)
                    + row_taps[3] * row_shift(before, cells, after, 2 * way, row_ids)
                ) * wet_s
                way = 1 if sin_up else -1
                pieces = [cells[:, LANES * c : LANES * (c + 1)] for c in range(cols // LANES)]
                down = lane_shift(pieces, -way, lane_ids)
                upwind = lane_shift(pieces, way, lane_ids)
                far = lane_shift(pieces, 2 * way, lane_ids)
                for c in range(cols // LANES):
                    lanes = slice(LANES * c, LANES * (c + 1))
                    moved_ref[slot, j + 2, :, lanes] = (
                        col_taps[1] * pieces[c]
                        + col_taps[0] * down[c]
                        + col_taps[2] * upwind[c]
                        + col_taps[3] * far[c]
                    ) * wet_s[:, lanes]

    for slot, s in enumerate(strips):
        moved_ref[slot, 0:2] = moved_ref[slot, dir_count : dir_count + 2]
        moved_ref[slot, dir_count + 2 : dir_count + 4] = moved_ref[slot, 2:4]

        def face_flux(f, turning):
            far_left, left = moved_ref[slot, f], moved_ref[slot, f + 1]
            right, far_right = moved_ref[slot, f + 2], moved_ref[slot, f + 3]
            rate = turn_rate * turning
            square = rate * rate
            slope = right - left
            bend = jnp.where(rate >= 0, slope - (left - far_left), (far_right - right) - slope)
            return rate * (
                0.5 * ((left + right) - rate * slope) - (1.0 / 6.0 - square * (1.0 / 6.0)) * bend
            )

        def turn(f, carry):
            lower, total = carry
            flux = face_flux(f, turn_ref[slot, lax.rem(f, dir_count)])
            cell = jnp.maximum(moved_ref[slot, f + 1] - (flux - lower), 0.0)
            out_refs[slot][0, f - 1] = cell
            return flux, total + cell

        flux = face_flux(0, turn_ref[slot, 0])
        _, total = lax.fori_loop(1, dir_count + 1, turn, (flux, jnp.zeros((STRIP, cols), jnp.float32)))
        rows = slice(STRIP * slot, STRIP * (slot + 1))
        sum_ref[0, rows, :] += weight * total
        sum_ref[1, rows, :] += (SPACING * 2.0 * math.pi / dir_count) * total

    source = spill_ref if edge else out_refs[spill_slot]
    spill = source[0].reshape(dir_count * STRIP, cols)
    for chooser, dest, send_ref in zip(choosers, dests, send_refs):
        filled = exact_dot(spill, chooser[...], split_ref, (((1,), (0,)), ((), ())))
        send_ref[0] = out_refs[dest][0] + filled.reshape(dir_count, STRIP, cols)


def propagate(strips, spill_slot, dests, edge, group, size, band_total, pos, table, spectrum, land_sea, slope_x, slope_y, extra, choosers):
    local_bands, dir_count, row_count, cols = spectrum.shape
    whole = lambda shape: pl.BlockSpec(shape, lambda b: (0,) * len(shape))
    one = lambda rows: pl.BlockSpec((1, dir_count, rows, cols), lambda b: (b, 0, 0, 0))
    smem = pl.BlockSpec(memory_space=pltpu.SMEM)
    flat = whole((row_count, cols))
    in_specs = [smem, smem]
    in_specs += [pl.BlockSpec((1, dir_count, row_count, cols), lambda b: (b + group, 0, 0, 0))]
    in_specs += [flat, flat, flat]
    if edge:
        halo = pl.BlockSpec((1, dir_count, 2, cols), lambda b: (b, 0, 0, 0))
        in_specs += [halo, halo, one(STRIP)]
    in_specs += [whole((cols, cols))] * len(choosers)
    band_array = lambda rows: jax.ShapeDtypeStruct((size, dir_count, rows, cols), jnp.float32)
    out_shape = [band_array(STRIP)] * (len(strips) + len(dests))
    out_specs = [one(STRIP)] * (len(strips) + len(dests))
    sums = (2, STRIP * len(strips), cols)
    out_shape.append(jax.ShapeDtypeStruct(sums, jnp.float32))
    out_specs.append(whole(sums))
    if not edge:
        out_shape += [band_array(2)] * 2
        out_specs += [one(2)] * 2
    cells = size * dir_count * len(strips) * STRIP * cols
    return pl.pallas_call(
        functools.partial(
            propagate_kernel, strips, spill_slot, dests, edge, group, band_total, dir_count, local_bands
        ),
        grid=(size,),
        in_specs=in_specs,
        out_specs=out_specs,
        out_shape=out_shape,
        scratch_shapes=[
            pltpu.VMEM((len(strips), dir_count, STRIP, cols), jnp.float32),
            pltpu.VMEM((len(strips), dir_count + 4, STRIP, cols), jnp.float32),
            pltpu.VMEM((3 * dir_count * STRIP, cols), jnp.bfloat16),
        ],
        compiler_params=pltpu.CompilerParams(vmem_limit_bytes=VMEM_BYTES),
        cost_estimate=pl.CostEstimate(flops=60 * cells, bytes_accessed=16 * cells, transcendentals=0),
        name="propagate_edge" if edge else "propagate_inner",
    )(pos, table, spectrum, land_sea, slope_x, slope_y, *extra, *choosers)


def source_kernel(strip, band_total, dir_count, local_bands, group_count, below_shape, above_shape, spill_count, first_call, *refs):
    refs = list(refs)
    pos_ref, tab_ref, land_ref, wind_ref, sum_ref = refs[:5]
    refs = refs[5:]
    own = refs[:group_count]
    refs = refs[group_count:]
    below = refs[: below_shape * max(spill_count, 1)]
    refs = refs[below_shape * max(spill_count, 1) :]
    above = refs[: above_shape * max(spill_count, 1)]
    refs = refs[above_shape * max(spill_count, 1) :]
    choosers = refs[:spill_count]
    refs = refs[spill_count:]
    if not first_call:
        refs = refs[1:]
    out_ref = refs[0]
    delta_ref = refs[1]
    lanes = out_ref.shape[-1]
    if spill_count:
        split_ref, halo_ref = refs[2:4]
        per_side = below[0].shape[0]
        lists = []
        slot = 0
        for side, count in ((below, below_shape), (above, above_shape)):
            found = []
            for part in range(count):
                for member in range(per_side):
                    total = None
                    for d in range(spill_count):
                        cells = side[d * count + part][member]
                        piece = exact_dot(
                            cells.reshape(dir_count * STRIP, cells.shape[-1]),
                            choosers[d][...],
                            split_ref,
                            (((1,), (1,)), ((), ())),
                        )
                        total = piece if total is None else total + piece
                    halo_ref[slot] = total.reshape(dir_count, STRIP, lanes)
                    found.append((halo_ref, slot))
                    slot += 1
            lists.append(found)
        below_list, above_list = lists
    else:
        below_list = [(ref, i) for ref in below for i in range(ref.shape[0])]
        above_list = [(ref, i) for ref in above for i in range(ref.shape[0])]
    own_list = [(ref, i) for ref in own for i in range(ref.shape[0])]
    bands = below_list + own_list + above_list

    def density(index, j):
        ref, slot = bands[index + 2]
        return ref[slot, j]

    energy = sum_ref[0] + EPSILON
    first_sum = sum_ref[1]
    mean_sigma = energy / (first_sum + EPSILON)
    ratio = energy / (math.sqrt(GRAVITY) * first_sum + EPSILON)
    mean_k = ratio * ratio
    steepness = energy * mean_k * mean_k / STEEP_REF
    decay = WHITECAP * mean_sigma / mean_k * steepness * steepness
    active = land_ref[...].astype(jnp.float32)
    quad_scale = active * QUAD_COEF / (energy * energy)

    @pl.loop(0, dir_count)
    def _(j):
        up = lax.rem(j + 1, dir_count)
        back = lax.rem(j + dir_count - 3, dir_count)
        for index in range(-1, local_bands + 1):
            center = density(index, j)
            plus = density(index + 1, up)
            minus = density(index - 1, back)
            delta_ref[index + 1, j] = center * (center * (plus + minus) - 2.0 * (plus * minus))

    growths, keeps = [], []
    for index in range(local_bands):
        growth = tab_ref[6 * dir_count + pos_ref[0] * local_bands + index]
        radian_freq = (2.0 * math.pi * BASE_FREQ) * growth
        wavenum = radian_freq * radian_freq * (1.0 / GRAVITY)
        growths.append(radian_freq)
        keeps.append(active / (1.0 + decay * wavenum))

    @pl.loop(0, dir_count)
    def _(j):
        up = lax.rem(j + 3, dir_count)
        back = lax.rem(j + dir_count - 1, dir_count)
        wind = tab_ref[4 * dir_count + j] * wind_ref[0] + tab_ref[5 * dir_count + j] * wind_ref[1]
        for index in range(local_bands):
            radian_freq = growths[index]
            quad = delta_ref[index, back] + delta_ref[index + 2, up] - 2.0 * delta_ref[index + 1, j]
            gain = 1.0 + jnp.maximum(radian_freq * wind - 1.0, 0.0) * (WIND_COEF * radian_freq)
            out_ref[index, j] = density(index, j) * gain * keeps[index] + quad * quad_scale


def source(strip, shape, band_total, pos, table, land_sea, wind, sums, sum_block, own, below, above, choosers, previous):
    local_bands, dir_count, row_count, cols = shape
    spill_count = len(choosers)
    lane_grid = cols // LANES
    smem = pl.BlockSpec(memory_space=pltpu.SMEM)
    part = lambda ref: pl.BlockSpec((ref.shape[0], dir_count, STRIP, LANES), lambda c: (0, 0, 0, c))
    full = lambda ref: pl.BlockSpec(ref.shape, lambda c: (0,) * ref.ndim)
    in_specs = [smem, smem]
    in_specs.append(pl.BlockSpec((STRIP, LANES), lambda c: (strip, c)))
    in_specs.append(pl.BlockSpec((2, STRIP, LANES), lambda c: (0, strip, c)))
    in_specs.append(pl.BlockSpec((2, STRIP, LANES), lambda c: (0, sum_block, c)))
    in_specs += [part(ref) for ref in own]
    in_specs += [full(ref) if spill_count else part(ref) for ref in below + above]
    in_specs += [pl.BlockSpec((LANES, cols), lambda c: (c, 0))] * spill_count
    operands = [pos, table, land_sea, wind, sums, *own, *below, *above, *choosers]
    aliases = {}
    if previous is not None:
        in_specs.append(pl.BlockSpec(memory_space=pl.ANY))
        aliases = {len(operands): 0}
        operands.append(previous)
    scratch = [pltpu.VMEM((local_bands + 2, dir_count, STRIP, LANES), jnp.float32)]
    sides = (len(below) // max(spill_count, 1), len(above) // max(spill_count, 1))
    if spill_count:
        scratch.append(pltpu.VMEM((3 * dir_count * STRIP, cols), jnp.bfloat16))
        scratch.append(pltpu.VMEM((4, dir_count, STRIP, LANES), jnp.float32))
    cells = local_bands * dir_count * STRIP * cols
    return pl.pallas_call(
        functools.partial(
            source_kernel, strip, band_total, dir_count, local_bands, len(own), sides[0], sides[1], spill_count, previous is None
        ),
        grid=(lane_grid,),
        in_specs=in_specs,
        out_specs=pl.BlockSpec((local_bands, dir_count, STRIP, LANES), lambda c: (0, 0, strip, c)),
        out_shape=jax.ShapeDtypeStruct(shape, jnp.float32),
        scratch_shapes=scratch,
        input_output_aliases=aliases,
        compiler_params=pltpu.CompilerParams(vmem_limit_bytes=VMEM_BYTES),
        cost_estimate=pl.CostEstimate(flops=30 * cells, bytes_accessed=16 * cells, transcendentals=0),
        name="source",
    )(*operands)


def shards(spectrum, land_sea, sea_index, sea_count, wind_speed, wind_dir, slope_x, slope_y):
    local_bands, dir_count, row_count, cols = spectrum.shape
    spec_count = lax.axis_size("spec")
    geo_count = lax.axis_size("geo")
    band_total = local_bands * spec_count
    pos = lax.axis_index("spec").astype(jnp.int32).reshape(1)
    table = jnp.asarray(tables(band_total, dir_count))
    inner, outer, spill = (1, 2), (0, 3), 2
    choose = plan(land_sea, (1, 0, 3), spill)
    size = min(2, local_bands)
    groups = list(range(0, local_bands, size))

    args = (band_total, pos, table, spectrum, land_sea, slope_x, slope_y)
    cells = {s: [] for s in range(4)}
    sends = {1: [], 0: [], 3: []}
    inner_sums, outer_sums = [], []
    for group in groups:
        strip_a, strip_b, send, sums, head, tail = propagate(
            inner, 1, (0,), False, group, size, *args, (), choose[:1]
        )
        cells[1].append(strip_a)
        cells[2].append(strip_b)
        sends[1].append(send)
        inner_sums.append((sums, head, tail))
    ups = [(i, i + 1) for i in range(geo_count - 1)]
    downs = [(i + 1, i) for i in range(geo_count - 1)]
    for index, group in enumerate(groups):
        _, head, tail = inner_sums[index]
        lower = lax.ppermute(tail, "geo", ups)
        upper = lax.ppermute(head, "geo", downs)
        strip_a, strip_b, send_a, send_b, sums = propagate(
            outer, None, (0, 1), True, group, size, *args, (lower, upper, cells[2][index]), choose[1:]
        )
        cells[0].append(strip_a)
        cells[3].append(strip_b)
        sends[0].append(send_a)
        sends[3].append(send_b)
        outer_sums.append(sums)
    total_inner = functools.reduce(jnp.add, [entry[0] for entry in inner_sums])
    total_outer = functools.reduce(jnp.add, outer_sums)
    sums = lax.psum(jnp.concatenate([total_inner, total_outer], axis=1), "spec")

    def hop(value, count):
        pairs = [(i, i + count) for i in range(spec_count) if 0 <= i + count < spec_count]
        return lax.ppermute(value, "spec", pairs)

    below, above = {}, {}
    for s in (1, 0, 3):
        if size == 2:
            below[s] = [hop(sends[s][-1], 1)]
            above[s] = [hop(sends[s][0], -1)]
        else:
            below[s] = [hop(sends[s][0], 2), hop(sends[s][0], 1)]
            above[s] = [hop(sends[s][0], -1), hop(sends[s][0], -2)]

    scale = (28.0 * USTAR_RATIO / GRAVITY) * wind_speed
    wind = jnp.stack([scale * jnp.cos(wind_dir), scale * jnp.sin(wind_dir)])
    result = None
    sum_block = {1: 0, 2: 1, 0: 2, 3: 3}
    for s in (1, 0, 3):
        result = source(
            s, spectrum.shape, band_total, pos, table, land_sea, wind, sums, sum_block[s], cells[s], below[s], above[s], [], result
        )
    all_below = [ref for s in (1, 0, 3) for ref in below[s]]
    all_above = [ref for s in (1, 0, 3) for ref in above[s]]
    return source(
        spill, spectrum.shape, band_total, pos, table, land_sea, wind, sums, sum_block[spill], cells[spill], all_below, all_above, list(choose), result
    )


def solution(mesh):
    placed = (
        P("spec", None, "geo", None),
        P("geo", None),
        P("geo", None),
        P("geo"),
        P("geo", None),
        P("geo", None),
        P("geo", None),
        P("geo", None),
    )
    return jax.shard_map(
        shards, mesh=mesh, in_specs=placed, out_specs=P("spec", None, "geo", None), check_vma=False
    )
```

time: 743 us -> 260 us (0.35)
  blocking collectives: 214 us -> 0 us
  local copies, waits for them, and re-layouts: 183 us -> 3.59 us
  other arithmetic: 127 us -> 3.29 us
  Pallas kernels: 0 us -> 118 us
  waiting for transfers between devices: 200 us -> 91.9 us
  starting transfers between devices: 12.6 us -> 29.4 us
  between operations: 0.52 us -> 13.7 us
    all_to_all x1 -> x0, blocking collectives: 214 us -> none  [shards(): lax.all_to_all(updated.reshape(band_total, dir_count, 1, per_device), 'sp...]
    all_to_all x1 -> x0, waiting for transfers between devices: 200 us -> none  [shards(): lax.all_to_all(outgoing, 'spec', split_axis=2, concat_axis=0, tiled=True)]
    pallas_call x0 -> x9, Pallas kernels: none -> 118 us  [the longest x4 68.8 us: propagate(): pl.pallas_call(functools.partial(propagate_kernel, strips, spill_slot, de...]
    mul x14 -> x0, other arithmetic: 97.9 us -> none  [the longest x3 44.8 us: quick_flux(): return courant * face_value]
    psum x0 -> x1, waiting for transfers between devices: none -> 91.8 us  [shards(): sums = lax.psum(jnp.concatenate([total_inner, total_outer], axis=1), 'spec')]
    reshape x4 -> x0, local copies, waits for them, and re-layouts: 49.7 us -> none  [the longest x2 26.1 us: shards(): outgoing = floored.reshape(local_bands, dir_count, spec_count, per_device)]
    concatenate x8 -> x0, local copies, waits for them, and re-layouts: 39.4 us -> none  [the longest x2 14.4 us: quad_delta(): minus = jnp.roll(below, 3, axis=dir_axis)]
    all_to_all x3 -> x0, local copies, waits for them, and re-layouts: 33 us -> none  [the longest x2 23.8 us: shards(): lax.all_to_all(outgoing, 'spec', split_axis=2, concat_axis=0, tiled=True)]
  transfers between devices with their start and end apart: 3 -> 11, of which waited for: 1 -> 1; matrix products, arithmetic and copies ran while one was open for 0% -> 1% of each run, Pallas kernels for 0% -> 26%
where the time goes in v1:
time: 260 us
  Pallas kernels  118 us (45%)
  waiting for transfers between devices  91.9 us (35%)
  starting transfers between devices  29.4 us (11%)
  between operations  13.7 us (5%)
  local copies, waits for them, and re-layouts  3.59 us (1%)
  other arithmetic  3.29 us (1%)
    psum x1, waiting for transfers between devices, shards(): sums = lax.psum(jnp.concatenate([total_inner, total_outer], axis=1), 'spec')  91.8 us
    pallas_call x4, Pallas kernels, propagate(): pl.pallas_call(functools.partial(propagate_kernel, strips, spill_slot, de...  68.8 us
    pallas_call x4, Pallas kernels, source(): pl.pallas_call(functools.partial(source_kernel, strip, band_total, dir_co...  46 us
    ppermute x6, starting transfers between devices, hop(): return lax.ppermute(value, 'spec', pairs)  20.7 us
    ppermute x2, starting transfers between devices, shards(): lower = lax.ppermute(tail, 'geo', ups)  6.06 us
  transfers between devices with their start and end apart: 11, of which 1 were waited for; matrix products, arithmetic and copies ran while one was open for 1% of the time, Pallas kernels for 26%

profile of v1, /device:TPU:0, one launch (start us, length us, event | category | flops | bytes accessed | tf_op | source)
XLA Modules:
  0.0 259.6 jit_solution(3127197992225419500)
XLA Ops:
  6.5 0.0 all-reduce.2.cloned.1.call-start
  6.5 3.0 %plan.1 = (bf16[512,512]{1,0:T(8,128)(2,1)}, bf16[512,512]{1,0:T(8,128)(2,1)}, bf16[512,512]{1,0:T(8,128)(2,1)}) custom-call(s32[32,512]{1,0:T(8,128)} %refs_2_.15), custom_call_target="tpu_custom_call" | custom-call | tf_op jit(solution)/shard_map/plan/pallas_call | solution.py:91
  9.6 16.5 %propagate_inner.3 = (f32[2,36,8,512]{3,2,1,0:T(8,128)}, f32[2,36,8,512]{3,2,1,0:T(8,128)}, f32[2,36,8,512]{3,2,1,0:T(8,128)}, f32[2,16,512]{2,1,0:T(8,128)}, f3...) custom-call(s32[1]{0:T(128)} %bitcast.refs_0_, f32[248]{0:T(256)} %constant.8.clone.refs_1_, ...), custom_call_target="tpu_custom_call" | custom-call | flops 35389440 | bytes 9437184 | tf_op jit(solution)/shard_map/propagate_inner/pallas_call | solution.py:298
  26.1 0.0 copy-start.11
  26.1 0.0 copy-start.10
  26.1 5.1 %collective-permute-start.4 = (f32[2,36,8,512]{3,2,1,0:T(8,128)}, f32[2,36,8,512]{3,2,1,0:T(8,128)S(1)}, u32[]{:S(2)}, u32[]{:S(2)}) collective-permute-start(f32[2,36,8,512]{3,2,1,0:T(8,128)} %get-tuple-element.43), channel_id=1, source_target_pairs={{0,1},{1,2},{2,3},{3,4},{4,5},{5,6},{6,7},{8,9},{9,10},{10,11},{11... | collective-permute-start | bytes 3538952 | tf_op jit(solution)/shard_map/ppermute | solution.py:494
  31.2 16.5 %propagate_inner.2 = (f32[2,36,8,512]{3,2,1,0:T(8,128)}, f32[2,36,8,512]{3,2,1,0:T(8,128)}, f32[2,36,8,512]{3,2,1,0:T(8,128)}, f32[2,16,512]{2,1,0:T(8,128)}, f3...) custom-call(s32[1]{0:T(128)} %bitcast.refs_0_, f32[248]{0:T(256)} %constant.8.clone.refs_1_, ...), custom_call_target="tpu_custom_call" | custom-call | flops 35389440 | bytes 9437184 | tf_op jit(solution)/shard_map/propagate_inner/pallas_call | solution.py:298
  47.6 1.5 collective-permute-start
  49.1 1.3 collective-permute-start.1
  50.4 0.0 copy-done.11
  50.4 4.6 %collective-permute-start.2 = (f32[2,36,2,512]{3,2,1,0:T(2,128)S(1)}, f32[2,36,2,512]{3,2,1,0:T(2,128)S(1)}, u32[]{:S(2)}, u32[]{:S(2)}) collective-permute-start(f32[2,36,2,512]{3,2,1,0:T(2,128)S(1)} %copy-done.11), channel_id=1, source_target_pairs={{0,8},{8,16},{16,24},{1,9},{9,17},{17,25},{2,10},{10,18},{18,26},{... | collective-permute-start | bytes 884744 | tf_op jit(solution)/shard_map/ppermute | solution.py:478
  55.0 0.0 copy-done.10
  55.0 1.3 collective-permute-start.3
  56.3 0.0 collective-permute-done.refs_6_
  56.4 0.0 copy-start.5
  56.4 1.3 collective-permute-start.7
  57.7 0.0 collective-permute-done.1.refs_7_
  57.7 0.7 copy-done.6
  58.4 17.9 %propagate_edge.2 = (f32[2,36,8,512]{3,2,1,0:T(8,128)}, f32[2,36,8,512]{3,2,1,0:T(8,128)}, f32[2,36,8,512]{3,2,1,0:T(8,128)}, f32[2,36,8,512]{3,2,1,0:T(8,128)}, f32[2,16,512]{2,1,0:T(8,128)}) custom-call(s32[1]{0:T(128)} %bitcast.refs_0_, f32[248]{0:T(256)} %constant.8.clone.refs_1_, f32[4,36,32,512]{3,2,1,0:T(8,128)} %refs_2_.11, s32[32,512]{1,0:T(8,128)} %refs_2_.15, ...), custom_call_target="tpu_custom_call" | custom-call | flops 35389440 | bytes 9437184 | tf_op jit(solution)/shard_map/propagate_edge/pallas_call | solution.py:298
  76.3 1.3 collective-permute-start.8
  77.6 0.0 collective-permute-done.2.refs_6_
  77.6 0.0 collective-permute-done.3.refs_7_
  77.6 0.7 copy-done.3
  78.3 0.1 copy-done.4
  78.4 18.0 %propagate_edge.3 = (f32[2,36,8,512]{3,2,1,0:T(8,128)}, f32[2,36,8,512]{3,2,1,0:T(8,128)}, f32[2,36,8,512]{3,2,1,0:T(8,128)}, f32[2,36,8,512]{3,2,1,0:T(8,128)}, f32[2,16,512]{2,1,0:T(8,128)}) custom-call(s32[1]{0:T(128)} %bitcast.refs_0_, f32[248]{0:T(256)} %constant.8.clone.refs_1_, f32[4,36,32,512]{3,2,1,0:T(8,128)} %refs_2_.11, s32[32,512]{1,0:T(8,128)} %refs_2_.15, ...), custom_call_target="tpu_custom_call" | custom-call | flops 35389440 | bytes 9437184 | tf_op jit(solution)/shard_map/propagate_edge/pallas_call | solution.py:298
  96.4 6.2 %collective-permute-start.5 = (f32[2,36,8,512]{3,2,1,0:T(8,128)}, f32[2,36,8,512]{3,2,1,0:T(8,128)}, u32[]{:S(2)}, u32[]{:S(2)}) collective-permute-start(f32[2,36,8,512]{3,2,1,0:T(8,128)} %get-tuple-element.44), channel_id=1, source_target_pairs={{0,1},{1,2},{2,3},{3,4},{4,5},{5,6},{6,7},{8,9},{9,10},{10,11},{11... | collective-permute-start | bytes 3538952 | tf_op jit(solution)/shard_map/ppermute | solution.py:494
  102.6 1.3 collective-permute-start.9
  103.9 0.0 collective-permute-done.4.refs_7_
  103.9 5.6 %collective-permute-start.6 = (f32[2,36,8,512]{3,2,1,0:T(8,128)}, f32[2,36,8,512]{3,2,1,0:T(8,128)}, u32[]{:S(2)}, u32[]{:S(2)}) collective-permute-start(f32[2,36,8,512]{3,2,1,0:T(8,128)} %get-tuple-element.45), channel_id=1, source_target_pairs={{0,1},{1,2},{2,3},{3,4},{4,5},{5,6},{6,7},{8,9},{9,10},{10,11},{11... | collective-permute-start | bytes 3538952 | tf_op jit(solution)/shard_map/ppermute | solution.py:494
  109.5 0.9 add.9
  110.4 0.7 pad_maximum_fusion.1
  111.0 0.0 all-reduce.2.cloned.1.call-update
  111.0 1.1 multiply_bitcast_fusion.1
  112.2 0.7 pad_maximum_fusion.refs_3_
  112.8 91.8 %all-reduce.2.cloned.1.call-done.refs_4_ = f32[2,32,512]{2,1,0:T(8,128)} async-done(((f32[2,32,512]{2,1,0:T(8,128)}), f32[2,32,512]{2,1,0:T(8,128)}) %all-reduce.2.cloned.1.call-update) | async-done | bytes 131088 | tf_op jit(solution)/shard_map/psum | solution.py:490
  204.7 0.0 collective-permute-done.7.refs_8_.refs_10_
  204.7 0.0 copy-done
  204.7 1.0 copy-done.1
  205.7 8.0 %source.4.refs_9_ = f32[4,36,32,512]{3,2,1,0:T(8,128)} custom-call(s32[1]{0:T(128)} %bitcast.refs_0_, f32[248]{0:T(256)} %constant.8.clone.refs_1_, s32[32,512]{1,0:T(8,128)} %refs_2_.15, f32[2,32,512]{2,1,0:T(8,128)} %pad_maximum_fusion.refs_3_, f32[2,32,512]{2,1,0:T(8,128)} %all-reduce.2.cloned.1.call-done.refs_4_, ...), custom_call_target="tpu_custom_call" | custom-call | flops 17694720 | bytes 9437184 | tf_op jit(solution)/shard_map/source/pallas_call | solution.py:434
  213.7 0.0 collective-permute-done.8.refs_8_.refs_11_
  213.7 0.0 copy-start.2
  213.8 0.0 collective-permute-done.5.refs_7_.refs_8_
  213.8 1.0 copy-done.2
  214.8 8.0 %source.5.refs_9_ = f32[4,36,32,512]{3,2,1,0:T(8,128)} custom-call(s32[1]{0:T(128)} %bitcast.refs_0_, f32[248]{0:T(256)} %constant.8.clone.refs_1_, s32[32,512]{1,0:T(8,128)} %refs_2_.15, f32[2,32,512]{2,1,0:T(8,128)} %pad_maximum_fusion.refs_3_, f32[2,32,512]{2,1,0:T(8,128)} %all-reduce.2.cloned.1.call-done.refs_4_, ...), custom_call_target="tpu_custom_call", output_to_operand_aliasing={{}: (9, {})} | custom-call | flops 17694720 | bytes 9437184 | tf_op jit(solution)/shard_map/source/pallas_call | solution.py:434
  222.8 0.0 collective-permute-done.9.refs_8_.refs_12_
  222.8 0.0 collective-permute-done.6.refs_7_.refs_9_
  222.8 8.1 %source.6.refs_16_ = f32[4,36,32,512]{3,2,1,0:T(8,128)} custom-call(s32[1]{0:T(128)} %bitcast.refs_0_, f32[248]{0:T(256)} %constant.8.clone.refs_1_, s32[32,512]{1,0:T(8,128)} %refs_2_.15, f32[2,32,512]{2,1,0:T(8,128)} %pad_maximum_fusion.refs_3_, f32[2,32,512]{2,1,0:T(8,128)} %all-reduce.2.cloned.1.call-done.refs_4_, ...), custom_call_target="tpu_custom_call", output_to_operand_aliasing={{}: (9, {})} | custom-call | flops 17694720 | bytes 9437184 | tf_op jit(solution)/shard_map/source/pallas_call | solution.py:434
  230.9 21.8 %source.7 = f32[4,36,32,512]{3,2,1,0:T(8,128)} custom-call(s32[1]{0:T(128)} %bitcast.refs_0_, f32[248]{0:T(256)} %constant.8.clone.refs_1_, s32[32,512]{1,0:T(8,128)} %refs_2_.15, f32[2,32,512]{2,1,0:T(8,128)} %pad_maximum_fusion.refs_3_, f32[2,32,512]{2,1,0:T(8,128)} %all-reduce.2.cloned.1.call-done.refs_4_, ...), custom_call_target="tpu_custom_call", output_to_operand_aliasing={{}: (16, {})} | custom-call | flops 17694720 | bytes 9437184 | tf_op jit(solution)/shard_map/source/pallas_call | solution.py:434
  (13 shorter events, 0.0 us)
Async XLA Ops:
  6.5 198.1 %all-reduce.2.cloned.1.call-start = ((), (), s32[]{:S(2)}) async-start(), calls=%async_computation | async-start | bytes 262144 | tf_op jit(solution)/shard_map/psum | solution.py:490
  26.1 24.4 %copy-start.11 = (f32[2,36,2,512]{3,2,1,0:T(2,128)S(1)}, f32[2,36,2,512]{3,2,1,0:T(2,128)}, u32[]{:S(2)}) copy-start(f32[2,36,2,512]{3,2,1,0:T(2,128)} %get-tuple-element.39) | copy-start | bytes 884740
  26.1 29.0 %copy-start.10 = (f32[2,36,2,512]{3,2,1,0:T(2,128)S(1)}, f32[2,36,2,512]{3,2,1,0:T(2,128)}, u32[]{:S(2)}) copy-start(f32[2,36,2,512]{3,2,1,0:T(2,128)} %get-tuple-element.40) | copy-start | bytes 884740
  26.1 77.8 %collective-permute-start.4 = (f32[2,36,8,512]{3,2,1,0:T(8,128)}, f32[2,36,8,512]{3,2,1,0:T(8,128)S(1)}, u32[]{:S(2)}, u32[]{:S(2)}) collective-permute-start(f32[2,36,8,512]{3,2,1,0:T(8,128)} %get-tuple-element.43), channel_id=1, source_target_pairs={{0,1},{1,2},{2,3},{3,4},{4,5},{5,6},{6,7},{8,9},{9,10},{10,11},{11... | collective-permute-start | bytes 3538952 | tf_op jit(solution)/shard_map/ppermute | solution.py:494
  47.6 8.7 %collective-permute-start = (f32[2,36,2,512]{3,2,1,0:T(2,128)}, f32[2,36,2,512]{3,2,1,0:T(2,128)S(1)}, u32[]{:S(2)}, u32[]{:S(2)}) collective-permute-start(f32[2,36,2,512]{3,2,1,0:T(2,128)} %get-tuple-element.33), channel_id=1, source_target_pairs={{0,8},{8,16},{16,24},{1,9},{9,17},{17,25},{2,10},{10,18},{18,26},{... | collective-permute-start | bytes 884744 | tf_op jit(solution)/shard_map/ppermute | solution.py:478
  49.1 8.5 %collective-permute-start.1 = (f32[2,36,2,512]{3,2,1,0:T(2,128)}, f32[2,36,2,512]{3,2,1,0:T(2,128)S(1)}, u32[]{:S(2)}, u32[]{:S(2)}) collective-permute-start(f32[2,36,2,512]{3,2,1,0:T(2,128)} %get-tuple-element.34), channel_id=1, source_target_pairs={{8,0},{16,8},{24,16},{9,1},{17,9},{25,17},{10,2},{18,10},{26,18},{... | collective-permute-start | bytes 884744 | tf_op jit(solution)/shard_map/ppermute | solution.py:479
  50.4 27.1 %collective-permute-start.2 = (f32[2,36,2,512]{3,2,1,0:T(2,128)S(1)}, f32[2,36,2,512]{3,2,1,0:T(2,128)S(1)}, u32[]{:S(2)}, u32[]{:S(2)}) collective-permute-start(f32[2,36,2,512]{3,2,1,0:T(2,128)S(1)} %copy-done.11), channel_id=1, source_target_pairs={{0,8},{8,16},{16,24},{1,9},{9,17},{17,25},{2,10},{10,18},{18,26},{... | collective-permute-start | bytes 884744 | tf_op jit(solution)/shard_map/ppermute | solution.py:478
  55.0 22.6 %collective-permute-start.3 = (f32[2,36,2,512]{3,2,1,0:T(2,128)S(1)}, f32[2,36,2,512]{3,2,1,0:T(2,128)S(1)}, u32[]{:S(2)}, u32[]{:S(2)}) collective-permute-start(f32[2,36,2,512]{3,2,1,0:T(2,128)S(1)} %copy-done.10), channel_id=1, source_target_pairs={{8,0},{16,8},{24,16},{9,1},{17,9},{25,17},{10,2},{18,10},{26,18},{... | collective-permute-start | bytes 884744 | tf_op jit(solution)/shard_map/ppermute | solution.py:479
  56.4 1.3 copy-start.5
  56.4 148.3 %collective-permute-start.7 = (f32[2,36,8,512]{3,2,1,0:T(8,128)}, f32[2,36,8,512]{3,2,1,0:T(8,128)S(1)}, u32[]{:S(2)}, u32[]{:S(2)}) collective-permute-start(f32[2,36,8,512]{3,2,1,0:T(8,128)} %get-tuple-element.46), channel_id=1, source_target_pairs={{1,0},{2,1},{3,2},{4,3},{5,4},{6,5},{7,6},{9,8},{10,9},{11,10},{12... | collective-permute-start | bytes 3538952 | tf_op jit(solution)/shard_map/ppermute | solution.py:494
  57.7 0.7 copy-start.6
  76.3 137.5 %collective-permute-start.8 = (f32[2,36,8,512]{3,2,1,0:T(8,128)}, f32[2,36,8,512]{3,2,1,0:T(8,128)S(1)}, u32[]{:S(2)}, u32[]{:S(2)}) collective-permute-start(f32[2,36,8,512]{3,2,1,0:T(8,128)} %get-tuple-element.47), channel_id=1, source_target_pairs={{1,0},{2,1},{3,2},{4,3},{5,4},{6,5},{7,6},{9,8},{10,9},{11,10},{12... | collective-permute-start | bytes 3538952 | tf_op jit(solution)/shard_map/ppermute | solution.py:494
  77.6 0.7 copy-start.3
  77.6 0.8 copy-start.4
  78.4 31.1 %copy-start.7 = (f32[2,16,512]{2,1,0:T(8,128)S(1)}, f32[2,16,512]{2,1,0:T(8,128)}, u32[]{:S(2)}) copy-start(f32[2,16,512]{2,1,0:T(8,128)} %get-tuple-element.32) | copy-start | bytes 196612
  78.4 31.1 %copy-start.8 = (f32[2,16,512]{2,1,0:T(8,128)S(1)}, f32[2,16,512]{2,1,0:T(8,128)}, u32[]{:S(2)}) copy-start(f32[2,16,512]{2,1,0:T(8,128)} %get-tuple-element.31) | copy-start | bytes 196612
  78.4 31.1 %copy-start.9 = (f32[2,16,512]{2,1,0:T(8,128)S(1)}, f32[2,16,512]{2,1,0:T(8,128)}, u32[]{:S(2)}) copy-start(f32[2,16,512]{2,1,0:T(8,128)} %get-tuple-element.38) | copy-start | bytes 196612
  96.4 117.4 %collective-permute-start.5 = (f32[2,36,8,512]{3,2,1,0:T(8,128)}, f32[2,36,8,512]{3,2,1,0:T(8,128)}, u32[]{:S(2)}, u32[]{:S(2)}) collective-permute-start(f32[2,36,8,512]{3,2,1,0:T(8,128)} %get-tuple-element.44), channel_id=1, source_target_pairs={{0,1},{1,2},{2,3},{3,4},{4,5},{5,6},{6,7},{8,9},{9,10},{10,11},{11... | collective-permute-start | bytes 3538952 | tf_op jit(solution)/shard_map/ppermute | solution.py:494
  102.6 120.2 %collective-permute-start.9 = (f32[2,36,8,512]{3,2,1,0:T(8,128)}, f32[2,36,8,512]{3,2,1,0:T(8,128)}, u32[]{:S(2)}, u32[]{:S(2)}) collective-permute-start(f32[2,36,8,512]{3,2,1,0:T(8,128)} %get-tuple-element.48), channel_id=1, source_target_pairs={{1,0},{2,1},{3,2},{4,3},{5,4},{6,5},{7,6},{9,8},{10,9},{11,10},{12... | collective-permute-start | bytes 3538952 | tf_op jit(solution)/shard_map/ppermute | solution.py:494
  103.9 100.8 %copy-start = (f32[2,36,8,512]{3,2,1,0:T(8,128)}, f32[2,36,8,512]{3,2,1,0:T(8,128)S(1)}, u32[]{:S(2)}) copy-start(f32[2,36,8,512]{3,2,1,0:T(8,128)S(1)} %collective-permute-done.4.refs_7_) | copy-start | bytes 3538948
  103.9 118.9 %collective-permute-start.6 = (f32[2,36,8,512]{3,2,1,0:T(8,128)}, f32[2,36,8,512]{3,2,1,0:T(8,128)}, u32[]{:S(2)}, u32[]{:S(2)}) collective-permute-start(f32[2,36,8,512]{3,2,1,0:T(8,128)} %get-tuple-element.45), channel_id=1, source_target_pairs={{0,1},{1,2},{2,3},{3,4},{4,5},{5,6},{6,7},{8,9},{9,10},{10,11},{11... | collective-permute-start | bytes 3538952 | tf_op jit(solution)/shard_map/ppermute | solution.py:494
  204.7 1.0 copy-start.1
  213.7 1.0 copy-start.2
Sparse Core Ops, SparseCore 0:
  111.2 93.4 all-reduce.1

commit v2 on v1

--- a/solution.py
+++ b/solution.py
@@ -25,6 +25,10 @@
 STRIP = 8
 LANES = 128
 VMEM_BYTES = 56 * 1024 * 1024
+ROW_UNROLL = 9
+TURN_UNROLL = 3
+DELTA_UNROLL = 4
+SOURCE_UNROLL = 4
 
 
 def tables(band_total, dir_count):
@@ -54,7 +58,23 @@
     return runs
 
 
-def plan_kernel(kept, spill, land_ref, *out_refs):
+def unrolled(first, last, count):
+    def wrap(body):
+        turns = (last - first) // count
+        if turns:
+
+            @pl.loop(0, turns)
+            def _(turn):
+                for k in range(count):
+                    body(first + turn * count + k)
+
+        for j in range(first + turns * count, last):
+            body(j)
+
+    return wrap
+
+
+def plan_kernel(kept, spill, wanted, back, land_ref, *out_refs):
     cols = land_ref.shape[1]
     flags = [land_ref[STRIP * s : STRIP * s + 1, :].astype(jnp.float32) for s in (spill,) + tuple(kept)]
     rows = [flags[0]] + [1.0 - flag for flag in flags[1:]]
@@ -63,36 +83,34 @@
     first = lax.broadcasted_iota(jnp.int32, (cols, cols), 0)
     second = lax.broadcasted_iota(jnp.int32, (cols, cols), 1)
     block = STRIP
-    before = jnp.where(
-        jnp.logical_and(first < second // block * block, first % block == 0), 1.0, 0.0
-    ).astype(jnp.bfloat16)
-    before_t = jnp.where(
-        jnp.logical_and(second < first // block * block, second % block == 0), 1.0, 0.0
-    ).astype(jnp.bfloat16)
-    same = jnp.where(first == second, 1.0, 0.0).astype(jnp.bfloat16)
-    narrow = table.astype(jnp.bfloat16)
+    starts = lax.broadcasted_iota(jnp.int32, (8, cols), 1) % block == 0
+    narrow = jnp.where(starts, table, 0.0).astype(jnp.bfloat16)
+    before = jnp.where(first < (second & ~(block - 1)), 1.0, 0.0).astype(jnp.bfloat16)
     ranks = jnp.dot(narrow, before, preferred_element_type=jnp.float32)
-    dims = (((1,), (1,)), ((), ()))
-    rank_col = lax.dot_general(before_t, narrow, dims, preferred_element_type=jnp.float32)[:, 0:1]
-    flag_col = lax.dot_general(same, narrow, dims, preferred_element_type=jnp.float32)[:, 0:1]
-    wanted = jnp.where(flag_col > 0.5, rank_col, -1.0)
-    phase = first % block == second % block
+    phase = (first & (block - 1)) == (second & (block - 1))
+    marks = [jnp.where(table[0:1] > 0.5, ranks[0:1], -1.0)]
     offset = jnp.zeros((1, 1), jnp.float32)
-    for index, out_ref in enumerate(out_refs):
+    for index in range(len(kept)):
         hole = table[index + 1 : index + 2, :]
-        place = jnp.where(hole > 0.5, ranks[index + 1 : index + 2, :] + offset, -2.0)
-        match = jnp.logical_and(phase, jnp.abs(wanted - place) < 0.5)
-        out_ref[...] = jnp.where(match, 1.0, 0.0).astype(jnp.bfloat16)
+        marks.append(jnp.where(hole > 0.5, ranks[index + 1 : index + 2, :] + offset, -2.0))
         offset = offset + jnp.sum(hole, axis=1, keepdims=True) * (1.0 / block)
-
-
-def plan(land_sea, kept, spill):
+    marks = jnp.concatenate(marks + [jnp.zeros((1, cols), jnp.float32)] * (8 - len(marks)), axis=0)
+    columns = marks.T
+    for index, out_ref in zip(wanted, out_refs):
+        if back:
+            match = jnp.abs(columns[:, index + 1 : index + 2] - marks[0:1, :]) < 0.5
+        else:
+            match = jnp.abs(columns[:, 0:1] - marks[index + 1 : index + 2, :]) < 0.5
+        out_ref[...] = jnp.where(jnp.logical_and(phase, match), 1.0, 0.0).astype(jnp.bfloat16)
+
+
+def plan(land_sea, kept, spill, wanted, back):
     cols = land_sea.shape[1]
     return pl.pallas_call(
-        functools.partial(plan_kernel, kept, spill),
-        out_shape=[jax.ShapeDtypeStruct((cols, cols), jnp.bfloat16)] * len(kept),
+        functools.partial(plan_kernel, kept, spill, wanted, back),
+        out_shape=[jax.ShapeDtypeStruct((cols, cols), jnp.bfloat16)] * len(wanted),
         compiler_params=pltpu.CompilerParams(vmem_limit_bytes=VMEM_BYTES),
-        name="plan",
+        name="plan_back" if back else "plan",
     )(land_sea)
 
 
@@ -127,7 +145,7 @@
     return moved
 
 
-def exact_dot(cells, chooser, split_ref, dims):
+def exact_dot(cells, chooser, split_ref):
     count = cells.shape[0]
     high = cells.astype(jnp.bfloat16)
     rest = cells - high.astype(jnp.float32)
@@ -136,7 +154,7 @@
     split_ref[0:count, :] = high
     split_ref[count : 2 * count, :] = mid
     split_ref[2 * count : 3 * count, :] = low
-    product = lax.dot_general(split_ref[...], chooser, dims, preferred_element_type=jnp.float32)
+    product = jnp.dot(split_ref[...], chooser, preferred_element_type=jnp.float32)
     return product[0:count] + product[count : 2 * count] + product[2 * count : 3 * count]
 
 
@@ -194,7 +212,7 @@
 
     for first, last, cos_up, sin_up in sign_runs(dir_count):
 
-        @pl.loop(first, last)
+        @unrolled(first, last, ROW_UNROLL)
         def _(j):
             row_taps = taps(courant * tab_ref[j])
             col_taps = taps(courant * tab_ref[dir_count + j])
@@ -237,30 +255,37 @@
                         + col_taps[3] * far[c]
                     ) * wet_s[:, lanes]
 
-    for slot, s in enumerate(strips):
-        moved_ref[slot, 0:2] = moved_ref[slot, dir_count : dir_count + 2]
-        moved_ref[slot, dir_count + 2 : dir_count + 4] = moved_ref[slot, 2:4]
-
-        def face_flux(f, turning):
-            far_left, left = moved_ref[slot, f], moved_ref[slot, f + 1]
-            right, far_right = moved_ref[slot, f + 2], moved_ref[slot, f + 3]
-            rate = turn_rate * turning
-            square = rate * rate
-            slope = right - left
-            bend = jnp.where(rate >= 0, slope - (left - far_left), (far_right - right) - slope)
-            return rate * (
-                0.5 * ((left + right) - rate * slope) - (1.0 / 6.0 - square * (1.0 / 6.0)) * bend
-            )
-
-        def turn(f, carry):
-            lower, total = carry
-            flux = face_flux(f, turn_ref[slot, lax.rem(f, dir_count)])
-            cell = jnp.maximum(moved_ref[slot, f + 1] - (flux - lower), 0.0)
-            out_refs[slot][0, f - 1] = cell
-            return flux, total + cell
-
-        flux = face_flux(0, turn_ref[slot, 0])
-        _, total = lax.fori_loop(1, dir_count + 1, turn, (flux, jnp.zeros((STRIP, cols), jnp.float32)))
+    moved_ref[:, 0:2] = moved_ref[:, dir_count : dir_count + 2]
+    moved_ref[:, dir_count + 2 : dir_count + 4] = moved_ref[:, 2:4]
+
+    def face_flux(slot, f, turning):
+        far_left, left = moved_ref[slot, f], moved_ref[slot, f + 1]
+        right, far_right = moved_ref[slot, f + 2], moved_ref[slot, f + 3]
+        rate = turn_rate * turning
+        square = rate * rate
+        slope = right - left
+        bend = jnp.where(rate >= 0, slope - (left - far_left), (far_right - right) - slope)
+        return rate * (
+            0.5 * ((left + right) - rate * slope) - (1.0 / 6.0 - square * (1.0 / 6.0)) * bend
+        )
+
+    def turn(step, carry):
+        carry = list(carry)
+        for k in range(TURN_UNROLL):
+            f = step * TURN_UNROLL + k + 1
+            face = f if k < TURN_UNROLL - 1 else lax.rem(f, dir_count)
+            for slot in range(len(strips)):
+                lower, total = carry[slot]
+                flux = face_flux(slot, f, turn_ref[slot, face])
+                cell = jnp.maximum(moved_ref[slot, f + 1] - (flux - lower), 0.0)
+                out_refs[slot][0, f - 1] = cell
+                carry[slot] = (flux, total + cell)
+        return tuple(carry)
+
+    zero = jnp.zeros((STRIP, cols), jnp.float32)
+    start = tuple((face_flux(slot, 0, turn_ref[slot, 0]), zero) for slot in range(len(strips)))
+    ends = lax.fori_loop(0, dir_count // TURN_UNROLL, turn, start)
+    for slot, (_, total) in enumerate(ends):
         rows = slice(STRIP * slot, STRIP * (slot + 1))
         sum_ref[0, rows, :] += weight * total
         sum_ref[1, rows, :] += (SPACING * 2.0 * math.pi / dir_count) * total
@@ -268,7 +293,7 @@
     source = spill_ref if edge else out_refs[spill_slot]
     spill = source[0].reshape(dir_count * STRIP, cols)
     for chooser, dest, send_ref in zip(choosers, dests, send_refs):
-        filled = exact_dot(spill, chooser[...], split_ref, (((1,), (0,)), ((), ())))
+        filled = exact_dot(spill, chooser[...], split_ref)
         send_ref[0] = out_refs[dest][0] + filled.reshape(dir_count, STRIP, cols)
 
 
@@ -314,52 +339,39 @@
     )(pos, table, spectrum, land_sea, slope_x, slope_y, *extra, *choosers)
 
 
-def source_kernel(strip, band_total, dir_count, local_bands, group_count, below_shape, above_shape, spill_count, first_call, *refs):
-    refs = list(refs)
+def unpack_kernel(has_total, send_ref, chooser_ref, *refs):
+    out_ref, split_ref = refs[-2:]
+    _, dir_count, rows, cols = send_ref.shape
+    cells = exact_dot(send_ref[0].reshape(dir_count * rows, cols), chooser_ref[...], split_ref)
+    cells = cells.reshape(dir_count, rows, cols)
+    out_ref[0] = cells + refs[0][0] if has_total else cells
+
+
+def unpack(sent, chooser, total):
+    bands, dir_count, rows, cols = sent.shape
+    one = pl.BlockSpec((1, dir_count, rows, cols), lambda b: (b, 0, 0, 0))
+    totals = [] if total is None else [total]
+    return pl.pallas_call(
+        functools.partial(unpack_kernel, total is not None),
+        grid=(bands,),
+        in_specs=[one, pl.BlockSpec(chooser.shape, lambda b: (0, 0))] + [one] * len(totals),
+        out_specs=one,
+        out_shape=jax.ShapeDtypeStruct(sent.shape, jnp.float32),
+        scratch_shapes=[pltpu.VMEM((3 * dir_count * rows, cols), jnp.bfloat16)],
+        compiler_params=pltpu.CompilerParams(vmem_limit_bytes=VMEM_BYTES),
+        cost_estimate=pl.CostEstimate(flops=8 * sent.size, bytes_accessed=12 * sent.size, transcendentals=0),
+        name="unpack",
+    )(sent, chooser, *totals)
+
+
+def source_kernel(dir_count, local_bands, group_count, below_count, above_count, *refs):
     pos_ref, tab_ref, land_ref, wind_ref, sum_ref = refs[:5]
     refs = refs[5:]
     own = refs[:group_count]
-    refs = refs[group_count:]
-    below = refs[: below_shape * max(spill_count, 1)]
-    refs = refs[below_shape * max(spill_count, 1) :]
-    above = refs[: above_shape * max(spill_count, 1)]
-    refs = refs[above_shape * max(spill_count, 1) :]
-    choosers = refs[:spill_count]
-    refs = refs[spill_count:]
-    if not first_call:
-        refs = refs[1:]
-    out_ref = refs[0]
-    delta_ref = refs[1]
-    lanes = out_ref.shape[-1]
-    if spill_count:
-        split_ref, halo_ref = refs[2:4]
-        per_side = below[0].shape[0]
-        lists = []
-        slot = 0
-        for side, count in ((below, below_shape), (above, above_shape)):
-            found = []
-            for part in range(count):
-                for member in range(per_side):
-                    total = None
-                    for d in range(spill_count):
-                        cells = side[d * count + part][member]
-                        piece = exact_dot(
-                            cells.reshape(dir_count * STRIP, cells.shape[-1]),
-                            choosers[d][...],
-                            split_ref,
-                            (((1,), (1,)), ((), ())),
-                        )
-                        total = piece if total is None else total + piece
-                    halo_ref[slot] = total.reshape(dir_count, STRIP, lanes)
-                    found.append((halo_ref, slot))
-                    slot += 1
-            lists.append(found)
-        below_list, above_list = lists
-    else:
-        below_list = [(ref, i) for ref in below for i in range(ref.shape[0])]
-        above_list = [(ref, i) for ref in above for i in range(ref.shape[0])]
-    own_list = [(ref, i) for ref in own for i in range(ref.shape[0])]
-    bands = below_list + own_list + above_list
+    below = refs[group_count : group_count + below_count]
+    above = refs[group_count + below_count : group_count + below_count + above_count]
+    out_ref, delta_ref = refs[-2:]
+    bands = [(ref, i) for ref in (*below, *own, *above) for i in range(ref.shape[0])]
 
     def density(index, j):
         ref, slot = bands[index + 2]
@@ -375,7 +387,7 @@
     active = land_ref[...].astype(jnp.float32)
     quad_scale = active * QUAD_COEF / (energy * energy)
 
-    @pl.loop(0, dir_count)
+    @unrolled(0, dir_count, DELTA_UNROLL)
     def _(j):
         up = lax.rem(j + 1, dir_count)
         back = lax.rem(j + dir_count - 3, dir_count)
@@ -393,7 +405,7 @@
         growths.append(radian_freq)
         keeps.append(active / (1.0 + decay * wavenum))
 
-    @pl.loop(0, dir_count)
+    @unrolled(0, dir_count, SOURCE_UNROLL)
     def _(j):
         up = lax.rem(j + 3, dir_count)
         back = lax.rem(j + dir_count - 1, dir_count)
@@ -405,46 +417,45 @@
             out_ref[index, j] = density(index, j) * gain * keeps[index] + quad * quad_scale
 
 
-def source(strip, shape, band_total, pos, table, land_sea, wind, sums, sum_block, own, below, above, choosers, previous):
+def source(strip, shape, pos, table, land_sea, wind, sums, sum_block, own, below, above, previous):
     local_bands, dir_count, row_count, cols = shape
-    spill_count = len(choosers)
-    lane_grid = cols // LANES
     smem = pl.BlockSpec(memory_space=pltpu.SMEM)
     part = lambda ref: pl.BlockSpec((ref.shape[0], dir_count, STRIP, LANES), lambda c: (0, 0, 0, c))
-    full = lambda ref: pl.BlockSpec(ref.shape, lambda c: (0,) * ref.ndim)
     in_specs = [smem, smem]
     in_specs.append(pl.BlockSpec((STRIP, LANES), lambda c: (strip, c)))
     in_specs.append(pl.BlockSpec((2, STRIP, LANES), lambda c: (0, strip, c)))
     in_specs.append(pl.BlockSpec((2, STRIP, LANES), lambda c: (0, sum_block, c)))
-    in_specs += [part(ref) for ref in own]
-    in_specs += [full(ref) if spill_count else part(ref) for ref in below + above]
-    in_specs += [pl.BlockSpec((LANES, cols), lambda c: (c, 0))] * spill_count
-    operands = [pos, table, land_sea, wind, sums, *own, *below, *above, *choosers]
+    in_specs += [part(ref) for ref in own + below + above]
+    operands = [pos, table, land_sea, wind, sums, *own, *below, *above]
     aliases = {}
     if previous is not None:
         in_specs.append(pl.BlockSpec(memory_space=pl.ANY))
         aliases = {len(operands): 0}
         operands.append(previous)
-    scratch = [pltpu.VMEM((local_bands + 2, dir_count, STRIP, LANES), jnp.float32)]
-    sides = (len(below) // max(spill_count, 1), len(above) // max(spill_count, 1))
-    if spill_count:
-        scratch.append(pltpu.VMEM((3 * dir_count * STRIP, cols), jnp.bfloat16))
-        scratch.append(pltpu.VMEM((4, dir_count, STRIP, LANES), jnp.float32))
     cells = local_bands * dir_count * STRIP * cols
     return pl.pallas_call(
-        functools.partial(
-            source_kernel, strip, band_total, dir_count, local_bands, len(own), sides[0], sides[1], spill_count, previous is None
-        ),
-        grid=(lane_grid,),
+        functools.partial(source_kernel, dir_count, local_bands, len(own), len(below), len(above)),
+        grid=(cols // LANES,),
         in_specs=in_specs,
         out_specs=pl.BlockSpec((local_bands, dir_count, STRIP, LANES), lambda c: (0, 0, strip, c)),
         out_shape=jax.ShapeDtypeStruct(shape, jnp.float32),
-        scratch_shapes=scratch,
+        scratch_shapes=[pltpu.VMEM((local_bands + 2, dir_count, STRIP, LANES), jnp.float32)],
         input_output_aliases=aliases,
         compiler_params=pltpu.CompilerParams(vmem_limit_bytes=VMEM_BYTES),
         cost_estimate=pl.CostEstimate(flops=30 * cells, bytes_accessed=16 * cells, transcendentals=0),
         name="source",
     )(*operands)
+
+
+def spec_total(value):
+    count = lax.axis_size("spec")
+    if count & (count - 1):
+        return lax.psum(value, "spec")
+    reach = 1
+    while reach < count:
+        value = value + lax.ppermute(value, "spec", [(i, i ^ reach) for i in range(count)])
+        reach *= 2
+    return value
 
 
 def shards(spectrum, land_sea, sea_index, sea_count, wind_speed, wind_dir, slope_x, slope_y):
@@ -455,7 +466,8 @@
     pos = lax.axis_index("spec").astype(jnp.int32).reshape(1)
     table = jnp.asarray(tables(band_total, dir_count))
     inner, outer, spill = (1, 2), (0, 3), 2
-    choose = plan(land_sea, (1, 0, 3), spill)
+    kept = (1, 0, 3)
+    choose = plan(land_sea, kept, spill, (0,), False)
     size = min(2, local_bands)
     groups = list(range(0, local_bands, size))
 
@@ -471,6 +483,7 @@
         cells[2].append(strip_b)
         sends[1].append(send)
         inner_sums.append((sums, head, tail))
+    choose = choose + plan(land_sea, kept, spill, (1, 2), False)
     ups = [(i, i + 1) for i in range(geo_count - 1)]
     downs = [(i + 1, i) for i in range(geo_count - 1)]
     for index, group in enumerate(groups):
@@ -485,16 +498,15 @@
         sends[0].append(send_a)
         sends[3].append(send_b)
         outer_sums.append(sums)
-    total_inner = functools.reduce(jnp.add, [entry[0] for entry in inner_sums])
-    total_outer = functools.reduce(jnp.add, outer_sums)
-    sums = lax.psum(jnp.concatenate([total_inner, total_outer], axis=1), "spec")
+    inner_total = spec_total(functools.reduce(jnp.add, [entry[0] for entry in inner_sums]))
+    outer_total = spec_total(functools.reduce(jnp.add, outer_sums))
 
     def hop(value, count):
         pairs = [(i, i + count) for i in range(spec_count) if 0 <= i + count < spec_count]
         return lax.ppermute(value, "spec", pairs)
 
     below, above = {}, {}
-    for s in (1, 0, 3):
+    for s in kept:
         if size == 2:
             below[s] = [hop(sends[s][-1], 1)]
             above[s] = [hop(sends[s][0], -1)]
@@ -504,17 +516,18 @@
 
     scale = (28.0 * USTAR_RATIO / GRAVITY) * wind_speed
     wind = jnp.stack([scale * jnp.cos(wind_dir), scale * jnp.sin(wind_dir)])
+    back = plan(land_sea, kept, spill, (0, 1, 2), True)
+    below[spill], above[spill] = [None] * len(below[1]), [None] * len(above[1])
+    for s, chooser in zip(kept, back):
+        for side in (below, above):
+            side[spill] = [unpack(sent, chooser, total) for sent, total in zip(side[s], side[spill])]
     result = None
-    sum_block = {1: 0, 2: 1, 0: 2, 3: 3}
-    for s in (1, 0, 3):
+    for s in kept + (spill,):
+        sums, block = (inner_total, inner.index(s)) if s in inner else (outer_total, outer.index(s))
         result = source(
-            s, spectrum.shape, band_total, pos, table, land_sea, wind, sums, sum_block[s], cells[s], below[s], above[s], [], result
+            s, spectrum.shape, pos, table, land_sea, wind, sums, block, cells[s], below[s], above[s], result
         )
-    all_below = [ref for s in (1, 0, 3) for ref in below[s]]
-    all_above = [ref for s in (1, 0, 3) for ref in above[s]]
-    return source(
-        spill, spectrum.shape, band_total, pos, table, land_sea, wind, sums, sum_block[spill], cells[spill], all_below, all_above, list(choose), result
-    )
+    return result
 
 
 def solution(mesh):

time: 260 us -> 231 us (0.89); the launches traced: 260 us -> 227 us
  Pallas kernels: 118 us -> 91.8 us
  between operations: 13.7 us -> 0.27 us
  starting transfers between devices: 29.4 us -> 38.1 us
  waiting for transfers between devices: 91.9 us -> 86.3 us
  local copies, waits for them, and re-layouts: 3.59 us -> 6.72 us
    psum x1 -> x0, waiting for transfers between devices: 91.8 us -> none  [shards(): sums = lax.psum(jnp.concatenate([total_inner, total_outer], axis=1), 'spec')]
    ppermute x6, waiting for transfers between devices: 0.02 us -> 82.4 us  [hop(): return lax.ppermute(value, 'spec', pairs)]
    pallas_call x4, Pallas kernels: 68.8 us -> 38.9 us  [propagate(): pl.pallas_call(functools.partial(propagate_kernel, strips, spill_slot, de...]
    ppermute x0 -> x6, starting transfers between devices: none -> 9.64 us  [spec_total(): lax.ppermute(value, 'spec', [(i, i ^ reach) for i in range(count)])]
    pallas_call x5 -> x13, Pallas kernels: 49 us -> 52.9 us  [the longest x4 24.7 us: source(): pl.pallas_call(functools.partial(source_kernel, dir_count, local_bands, l...]
    ppermute x0 -> x6, waiting for transfers between devices: none -> 3.86 us  [spec_total(): lax.ppermute(value, 'spec', [(i, i ^ reach) for i in range(count)])]
    unnamed x24 -> x32, local copies, waits for them, and re-layouts: 3.59 us -> 6.72 us
  transfers between devices with their start and end apart: 11 -> 16, of which waited for: 1 -> 6; matrix products, arithmetic and copies ran while one was open for 1% -> 2% of each run, Pallas kernels for 26% -> 26%
where the time goes in v2:
time: 231 us; the launch traced here: 227 us
  Pallas kernels  91.8 us (40%)
  waiting for transfers between devices  86.3 us (37%)
  starting transfers between devices  38.1 us (16%)
  local copies, waits for them, and re-layouts  6.72 us (3%)
  other arithmetic  3.92 us (2%)
    ppermute x6, waiting for transfers between devices, hop(): return lax.ppermute(value, 'spec', pairs)  82.4 us
    pallas_call x4, Pallas kernels, propagate(): pl.pallas_call(functools.partial(propagate_kernel, strips, spill_slot, de...  38.9 us
    pallas_call x4, Pallas kernels, source(): pl.pallas_call(functools.partial(source_kernel, dir_count, local_bands, l...  24.7 us
    pallas_call x6, Pallas kernels, unpack(): pl.pallas_call(functools.partial(unpack_kernel, total is not None), grid=...  20.6 us
    ppermute x6, starting transfers between devices, hop(): return lax.ppermute(value, 'spec', pairs)  19.8 us
    ppermute x6, starting transfers between devices, spec_total(): lax.ppermute(value, 'spec', [(i, i ^ reach) for i in range(count)])  9.64 us
    pallas_call x3, Pallas kernels, plan(): pl.pallas_call(functools.partial(plan_kernel, kept, spill, wanted, back),...  7.68 us
    unnamed x32, local copies, waits for them, and re-layouts  6.72 us
  transfers between devices with their start and end apart: 16, of which 6 were waited for; matrix products, arithmetic and copies ran while one was open for 2% of the time, Pallas kernels for 26%

profile of v2, /device:TPU:0, one launch (start us, length us, event | category | flops | bytes accessed | tf_op | source)
XLA Modules:
  0.0 227.2 jit_solution(18303533003511531625)
XLA Ops:
  0.0 2.2 plan.2.refs_6_
  2.2 9.0 %propagate_inner.3 = (f32[2,36,8,512]{3,2,1,0:T(8,128)}, f32[2,36,8,512]{3,2,1,0:T(8,128)}, f32[2,36,8,512]{3,2,1,0:T(8,128)}, f32[2,16,512]{2,1,0:T(8,128)}, f3...) custom-call(s32[1]{0:T(128)} %bitcast.refs_0_, f32[248]{0:T(256)} %constant.8.clone.refs_1_, ...), custom_call_target="tpu_custom_call" | custom-call | flops 35389440 | bytes 9437184 | tf_op jit(solution)/shard_map/propagate_inner/pallas_call | solution.py:323
  11.2 5.1 %collective-permute-start.7 = (f32[2,36,8,512]{3,2,1,0:T(8,128)}, f32[2,36,8,512]{3,2,1,0:T(8,128)S(1)}, u32[]{:S(2)}, u32[]{:S(2)}) collective-permute-start(f32[2,36,8,512]{3,2,1,0:T(8,128)} %get-tuple-element.44), channel_id=1, source_target_pairs={{0,1},{1,2},{2,3},{3,4},{4,5},{5,6},{6,7},{8,9},{9,10},{10,11},{11... | collective-permute-start | bytes 3538952 | tf_op jit(solution)/shard_map/ppermute | solution.py:506
  16.3 9.0 %propagate_inner.2 = (f32[2,36,8,512]{3,2,1,0:T(8,128)}, f32[2,36,8,512]{3,2,1,0:T(8,128)}, f32[2,36,8,512]{3,2,1,0:T(8,128)}, f32[2,16,512]{2,1,0:T(8,128)}, f3...) custom-call(s32[1]{0:T(128)} %bitcast.refs_0_, f32[248]{0:T(256)} %constant.8.clone.refs_1_, ...), custom_call_target="tpu_custom_call" | custom-call | flops 35389440 | bytes 9437184 | tf_op jit(solution)/shard_map/propagate_inner/pallas_call | solution.py:323
  25.3 1.5 collective-permute-start.8
  26.8 1.3 collective-permute-start.9
  28.1 4.6 %collective-permute-start.3 = (f32[2,36,2,512]{3,2,1,0:T(2,128)S(1)}, f32[2,36,2,512]{3,2,1,0:T(2,128)S(1)}, u32[]{:S(2)}, u32[]{:S(2)}) collective-permute-start(f32[2,36,2,512]{3,2,1,0:T(2,128)S(1)} %copy-done.15), channel_id=1, source_target_pairs={{0,8},{8,16},{16,24},{1,9},{9,17},{17,25},{2,10},{10,18},{18,26},{... | collective-permute-start | bytes 884744 | tf_op jit(solution)/shard_map/ppermute | solution.py:491
  32.7 1.3 collective-permute-start.4
  34.0 2.6 %plan.3 = (bf16[512,512]{1,0:T(8,128)(2,1)}, bf16[512,512]{1,0:T(8,128)(2,1)}) custom-call(s32[32,512]{1,0:T(8,128)} %refs_2_.15), custom_call_target="tpu_custom_call" | custom-call | tf_op jit(solution)/shard_map/plan/pallas_call | solution.py:109
  36.6 0.8 add.24
  37.4 1.5 collective-permute-start
  39.0 0.7 copy-done.9
  39.7 10.4 %propagate_edge.3 = (f32[2,36,8,512]{3,2,1,0:T(8,128)}, f32[2,36,8,512]{3,2,1,0:T(8,128)}, f32[2,36,8,512]{3,2,1,0:T(8,128)}, f32[2,36,8,512]{3,2,1,0:T(8,128)}, f32[2,16,512]{2,1,0:T(8,128)}) custom-call(s32[1]{0:T(128)} %bitcast.refs_0_, f32[248]{0:T(256)} %constant.8.clone.refs_1_, f32[4,36,32,512]{3,2,1,0:T(8,128)} %refs_2_.11, s32[32,512]{1,0:T(8,128)} %refs_2_.15, ...), custom_call_target="tpu_custom_call" | custom-call | flops 35389440 | bytes 9437184 | tf_op jit(solution)/shard_map/propagate_edge/pallas_call | solution.py:323
  50.1 0.7 copy-done.6
  50.9 10.5 %propagate_edge.2 = (f32[2,36,8,512]{3,2,1,0:T(8,128)}, f32[2,36,8,512]{3,2,1,0:T(8,128)}, f32[2,36,8,512]{3,2,1,0:T(8,128)}, f32[2,36,8,512]{3,2,1,0:T(8,128)}, f32[2,16,512]{2,1,0:T(8,128)}) custom-call(s32[1]{0:T(128)} %bitcast.refs_0_, f32[248]{0:T(256)} %constant.8.clone.refs_1_, f32[4,36,32,512]{3,2,1,0:T(8,128)} %refs_2_.11, s32[32,512]{1,0:T(8,128)} %refs_2_.15, ...), custom_call_target="tpu_custom_call" | custom-call | flops 35389440 | bytes 9437184 | tf_op jit(solution)/shard_map/propagate_edge/pallas_call | solution.py:323
  61.5 0.9 add.28
  63.0 1.6 collective-permute-start.1
  64.5 2.1 collective-permute-done.13
  66.7 1.6 collective-permute-start.14
  68.3 1.6 collective-permute-start.2
  69.9 1.7 collective-permute-done.14
  71.7 2.7 %collective-permute-start.15 = (f32[2,16,512]{2,1,0:T(8,128)S(1)}, f32[2,16,512]{2,1,0:T(8,128)S(1)}, u32[]{:S(2)}, u32[]{:S(2)}) collective-permute-start(f32[2,16,512]{2,1,0:T(8,128)S(1)} %add.30), channel_id=1, source_target_pairs={{0,4},{1,5},{2,6},{3,7},{4,0},{5,1},{6,2},{7,3},{8,12},{9,13},{10,... | collective-permute-start | bytes 196616 | tf_op jit(solution)/shard_map/ppermute | solution.py:456
  74.4 1.3 collective-permute-start.12
  75.6 1.3 collective-permute-start.11
  76.9 5.2 %collective-permute-start.6 = (f32[2,36,8,512]{3,2,1,0:T(8,128)}, f32[2,36,8,512]{3,2,1,0:T(8,128)S(1)}, u32[]{:S(2)}, u32[]{:S(2)}) collective-permute-start(f32[2,36,8,512]{3,2,1,0:T(8,128)} %get-tuple-element.42), channel_id=1, source_target_pairs={{0,1},{1,2},{2,3},{3,4},{4,5},{5,6},{6,7},{8,9},{9,10},{10,11},{11... | collective-permute-start | bytes 3538952 | tf_op jit(solution)/shard_map/ppermute | solution.py:506
  82.2 1.3 collective-permute-start.10
  83.5 5.6 %collective-permute-start.5 = (f32[2,36,8,512]{3,2,1,0:T(8,128)}, f32[2,36,8,512]{3,2,1,0:T(8,128)S(1)}, u32[]{:S(2)}, u32[]{:S(2)}) collective-permute-start(f32[2,36,8,512]{3,2,1,0:T(8,128)} %get-tuple-element.40), channel_id=1, source_target_pairs={{0,1},{1,2},{2,3},{3,4},{4,5},{5,6},{6,7},{8,9},{9,10},{10,11},{11... | collective-permute-start | bytes 3538952 | tf_op jit(solution)/shard_map/ppermute | solution.py:506
  89.2 2.9 %plan_back.1 = (bf16[512,512]{1,0:T(8,128)(2,1)}, bf16[512,512]{1,0:T(8,128)(2,1)}, bf16[512,512]{1,0:T(8,128)(2,1)}) custom-call(s32[32,512]{1,0:T(8,128)} %refs_2_.15), custom_call_target="tpu_custom_call" | custom-call | tf_op jit(solution)/shard_map/plan_back/pallas_call | solution.py:109
  92.4 0.7 pad_maximum_fusion.refs_3_
  94.3 3.3 %unpack.6.refs_0_ = f32[2,36,8,512]{3,2,1,0:T(8,128)} custom-call(f32[2,36,8,512]{3,2,1,0:T(8,128)} %copy-done, bf16[512,512]{1,0:T(8,128)(2,1)} %get-tuple-element.45.chooser_ref), custom_call_target="tpu_custom_call" | custom-call | flops 2359296 | bytes 3538944 | tf_op jit(solution)/shard_map/unpack/pallas_call | solution.py:354
  97.6 7.7 %collective-permute-done.12.send_ref.refs_8_ = f32[2,36,8,512]{3,2,1,0:T(8,128)S(1)} collective-permute-done((f32[2,36,8,512]{3,2,1,0:T(8,128)}, f32[2,36,8,512]{3,2,1,0:T(8,128)S(1)}, u32[]{:S(2)}, u32[]{:S(2)}) %collective-permute-start.12) | collective-permute-done | bytes 1179680 | tf_op jit(solution)/shard_map/ppermute | solution.py:506
  105.3 1.0 copy-done.1
  106.3 3.3 %unpack.9.refs_0_ = f32[2,36,8,512]{3,2,1,0:T(8,128)} custom-call(f32[2,36,8,512]{3,2,1,0:T(8,128)} %copy-done.1, bf16[512,512]{1,0:T(8,128)(2,1)} %get-tuple-element.45.chooser_ref), custom_call_target="tpu_custom_call" | custom-call | flops 2359296 | bytes 3538944 | tf_op jit(solution)/shard_map/unpack/pallas_call | solution.py:354
  109.6 6.2 %source.4.refs_9_ = f32[4,36,32,512]{3,2,1,0:T(8,128)} custom-call(s32[1]{0:T(128)} %bitcast.refs_0_, f32[248]{0:T(256)} %constant.8.clone.refs_1_, s32[32,512]{1,0:T(8,128)} %refs_2_.15, f32[2,32,512]{2,1,0:T(8,128)} %pad_maximum_fusion.refs_3_, f32[2,16,512]{2,1,0:T(8,128)} %add.27.refs_4_, f32[2,36,8,512]{3,2,1,0:T(8,128)} %get-tuple-element.57.refs_5_, ...), custom_call_target="tpu_custom_call" | custom-call | flops 17694720 | bytes 9437184 | tf_op jit(solution)/shard_map/source/pallas_call | solution.py:436
  115.8 14.8 %collective-permute-done.11.send_ref.refs_8_ = f32[2,36,8,512]{3,2,1,0:T(8,128)S(1)} collective-permute-done((f32[2,36,8,512]{3,2,1,0:T(8,128)}, f32[2,36,8,512]{3,2,1,0:T(8,128)S(1)}, u32[]{:S(2)}, u32[]{:S(2)}) %collective-permute-start.11) | collective-permute-done | bytes 1179680 | tf_op jit(solution)/shard_map/ppermute | solution.py:506
  130.6 1.0 copy-done.2
  131.6 3.5 %unpack.10.refs_0_ = f32[2,36,8,512]{3,2,1,0:T(8,128)} custom-call(f32[2,36,8,512]{3,2,1,0:T(8,128)} %copy-done.2, bf16[512,512]{1,0:T(8,128)(2,1)} %get-tuple-element.43.chooser_ref, f32[2,36,8,512]{3,2,1,0:T(8,128)} %unpack.9.refs_0_), custom_call_target="tpu_custom_call" | custom-call | flops 2359296 | bytes 3538944 | tf_op jit(solution)/shard_map/unpack/pallas_call | solution.py:354
  135.1 43.8 %collective-permute-done.6.send_ref.refs_7_ = f32[2,36,8,512]{3,2,1,0:T(8,128)S(1)} collective-permute-done((f32[2,36,8,512]{3,2,1,0:T(8,128)}, f32[2,36,8,512]{3,2,1,0:T(8,128)S(1)}, u32[]{:S(2)}, u32[]{:S(2)}) %collective-permute-start.6) | collective-permute-done | bytes 1179680 | tf_op jit(solution)/shard_map/ppermute | solution.py:506
  178.9 1.0 copy-done.3
  179.9 3.5 %unpack.7.refs_0_ = f32[2,36,8,512]{3,2,1,0:T(8,128)} custom-call(f32[2,36,8,512]{3,2,1,0:T(8,128)} %copy-done.3, bf16[512,512]{1,0:T(8,128)(2,1)} %get-tuple-element.43.chooser_ref, f32[2,36,8,512]{3,2,1,0:T(8,128)} %unpack.6.refs_0_), custom_call_target="tpu_custom_call" | custom-call | flops 2359296 | bytes 3538944 | tf_op jit(solution)/shard_map/unpack/pallas_call | solution.py:354
  183.4 1.0 copy-done.4
  184.4 3.5 %unpack.11.refs_8_ = f32[2,36,8,512]{3,2,1,0:T(8,128)} custom-call(f32[2,36,8,512]{3,2,1,0:T(8,128)} %copy-done.4, bf16[512,512]{1,0:T(8,128)(2,1)} %get-tuple-element.41.chooser_ref, f32[2,36,8,512]{3,2,1,0:T(8,128)} %unpack.10.refs_0_), custom_call_target="tpu_custom_call" | custom-call | flops 2359296 | bytes 3538944 | tf_op jit(solution)/shard_map/unpack/pallas_call | solution.py:354
  187.9 16.2 %collective-permute-done.5.send_ref.refs_7_ = f32[2,36,8,512]{3,2,1,0:T(8,128)S(1)} collective-permute-done((f32[2,36,8,512]{3,2,1,0:T(8,128)}, f32[2,36,8,512]{3,2,1,0:T(8,128)S(1)}, u32[]{:S(2)}, u32[]{:S(2)}) %collective-permute-start.5) | collective-permute-done | bytes 1179680 | tf_op jit(solution)/shard_map/ppermute | solution.py:506
  204.1 1.1 copy-done.5
  205.2 3.5 %unpack.8.refs_7_ = f32[2,36,8,512]{3,2,1,0:T(8,128)} custom-call(f32[2,36,8,512]{3,2,1,0:T(8,128)} %copy-done.5, bf16[512,512]{1,0:T(8,128)(2,1)} %get-tuple-element.41.chooser_ref, f32[2,36,8,512]{3,2,1,0:T(8,128)} %unpack.7.refs_0_), custom_call_target="tpu_custom_call" | custom-call | flops 2359296 | bytes 3538944 | tf_op jit(solution)/shard_map/unpack/pallas_call | solution.py:354
  208.7 6.2 %source.5.refs_9_ = f32[4,36,32,512]{3,2,1,0:T(8,128)} custom-call(s32[1]{0:T(128)} %bitcast.refs_0_, f32[248]{0:T(256)} %constant.8.clone.refs_1_, s32[32,512]{1,0:T(8,128)} %refs_2_.15, f32[2,32,512]{2,1,0:T(8,128)} %pad_maximum_fusion.refs_3_, f32[2,16,512]{2,1,0:T(8,128)} %add.31.refs_4_, ...), custom_call_target="tpu_custom_call", output_to_operand_aliasing={{}: (9, {})} | custom-call | flops 17694720 | bytes 9437184 | tf_op jit(solution)/shard_map/source/pallas_call | solution.py:436
  214.8 6.2 %source.6.refs_9_ = f32[4,36,32,512]{3,2,1,0:T(8,128)} custom-call(s32[1]{0:T(128)} %bitcast.refs_0_, f32[248]{0:T(256)} %constant.8.clone.refs_1_, s32[32,512]{1,0:T(8,128)} %refs_2_.15, f32[2,32,512]{2,1,0:T(8,128)} %pad_maximum_fusion.refs_3_, f32[2,16,512]{2,1,0:T(8,128)} %add.31.refs_4_, ...), custom_call_target="tpu_custom_call", output_to_operand_aliasing={{}: (9, {})} | custom-call | flops 17694720 | bytes 9437184 | tf_op jit(solution)/shard_map/source/pallas_call | solution.py:436
  221.0 6.2 %source.7 = f32[4,36,32,512]{3,2,1,0:T(8,128)} custom-call(s32[1]{0:T(128)} %bitcast.refs_0_, f32[248]{0:T(256)} %constant.8.clone.refs_1_, s32[32,512]{1,0:T(8,128)} %refs_2_.15, f32[2,32,512]{2,1,0:T(8,128)} %pad_maximum_fusion.refs_3_, f32[2,16,512]{2,1,0:T(8,128)} %add.27.refs_4_, ...), custom_call_target="tpu_custom_call", output_to_operand_aliasing={{}: (9, {})} | custom-call | flops 17694720 | bytes 9437184 | tf_op jit(solution)/shard_map/source/pallas_call | solution.py:436
  (43 shorter events, 2.4 us)
Async XLA Ops:
  11.2 16.9 %copy-start.15 = (f32[2,36,2,512]{3,2,1,0:T(2,128)S(1)}, f32[2,36,2,512]{3,2,1,0:T(2,128)}, u32[]{:S(2)}) copy-start(f32[2,36,2,512]{3,2,1,0:T(2,128)} %get-tuple-element.36) | copy-start | bytes 884740
  11.2 21.5 %copy-start.14 = (f32[2,36,2,512]{3,2,1,0:T(2,128)S(1)}, f32[2,36,2,512]{3,2,1,0:T(2,128)}, u32[]{:S(2)}) copy-start(f32[2,36,2,512]{3,2,1,0:T(2,128)} %get-tuple-element.37) | copy-start | bytes 884740
  11.2 25.4 %copy-start.10 = (f32[2,16,512]{2,1,0:T(8,128)S(1)}, f32[2,16,512]{2,1,0:T(8,128)}, u32[]{:S(2)}) copy-start(f32[2,16,512]{2,1,0:T(8,128)} %get-tuple-element.33) | copy-start | bytes 196612
  11.2 72.3 %collective-permute-start.7 = (f32[2,36,8,512]{3,2,1,0:T(8,128)}, f32[2,36,8,512]{3,2,1,0:T(8,128)S(1)}, u32[]{:S(2)}, u32[]{:S(2)}) collective-permute-start(f32[2,36,8,512]{3,2,1,0:T(8,128)} %get-tuple-element.44), channel_id=1, source_target_pairs={{0,1},{1,2},{2,3},{3,4},{4,5},{5,6},{6,7},{8,9},{9,10},{10,11},{11... | collective-permute-start | bytes 3538952 | tf_op jit(solution)/shard_map/ppermute | solution.py:506
  25.3 12.1 %collective-permute-start.8 = (f32[2,36,2,512]{3,2,1,0:T(2,128)}, f32[2,36,2,512]{3,2,1,0:T(2,128)S(1)}, u32[]{:S(2)}, u32[]{:S(2)}) collective-permute-start(f32[2,36,2,512]{3,2,1,0:T(2,128)} %get-tuple-element.46), channel_id=1, source_target_pairs={{0,8},{8,16},{16,24},{1,9},{9,17},{17,25},{2,10},{10,18},{18,26},{... | collective-permute-start | bytes 884744 | tf_op jit(solution)/shard_map/ppermute | solution.py:491
  26.8 12.2 %collective-permute-start.9 = (f32[2,36,2,512]{3,2,1,0:T(2,128)}, f32[2,36,2,512]{3,2,1,0:T(2,128)S(1)}, u32[]{:S(2)}, u32[]{:S(2)}) collective-permute-start(f32[2,36,2,512]{3,2,1,0:T(2,128)} %get-tuple-element.47), channel_id=1, source_target_pairs={{8,0},{16,8},{24,16},{9,1},{17,9},{25,17},{10,2},{18,10},{26,18},{... | collective-permute-start | bytes 884744 | tf_op jit(solution)/shard_map/ppermute | solution.py:492
  28.1 22.0 %collective-permute-start.3 = (f32[2,36,2,512]{3,2,1,0:T(2,128)S(1)}, f32[2,36,2,512]{3,2,1,0:T(2,128)S(1)}, u32[]{:S(2)}, u32[]{:S(2)}) collective-permute-start(f32[2,36,2,512]{3,2,1,0:T(2,128)S(1)} %copy-done.15), channel_id=1, source_target_pairs={{0,8},{8,16},{16,24},{1,9},{9,17},{17,25},{2,10},{10,18},{18,26},{... | collective-permute-start | bytes 884744 | tf_op jit(solution)/shard_map/ppermute | solution.py:491
  32.7 17.4 %collective-permute-start.4 = (f32[2,36,2,512]{3,2,1,0:T(2,128)S(1)}, f32[2,36,2,512]{3,2,1,0:T(2,128)S(1)}, u32[]{:S(2)}, u32[]{:S(2)}) collective-permute-start(f32[2,36,2,512]{3,2,1,0:T(2,128)S(1)} %copy-done.14), channel_id=1, source_target_pairs={{8,0},{16,8},{24,16},{9,1},{17,9},{25,17},{10,2},{18,10},{26,18},{... | collective-permute-start | bytes 884744 | tf_op jit(solution)/shard_map/ppermute | solution.py:492
  37.4 1.5 copy-start.8
  37.4 25.5 %collective-permute-start = (f32[2,16,512]{2,1,0:T(8,128)S(1)}, f32[2,16,512]{2,1,0:T(8,128)S(1)}, u32[]{:S(2)}, u32[]{:S(2)}) collective-permute-start(f32[2,16,512]{2,1,0:T(8,128)S(1)} %add.24), channel_id=1, source_target_pairs={{0,1},{1,0},{2,3},{3,2},{4,5},{5,4},{6,7},{7,6},{8,9},{9,8},{10,11... | collective-permute-start | bytes 196616 | tf_op jit(solution)/shard_map/ppermute | solution.py:456
  39.0 0.7 copy-start.9
  50.1 0.7 copy-start.6
  50.1 0.8 copy-start.7
  50.9 10.5 %copy-start.11 = (f32[2,16,512]{2,1,0:T(8,128)S(1)}, f32[2,16,512]{2,1,0:T(8,128)}, u32[]{:S(2)}) copy-start(f32[2,16,512]{2,1,0:T(8,128)} %get-tuple-element.51) | copy-start | bytes 196612
  50.9 41.2 %copy-start.12 = (f32[32,512]{1,0:T(8,128)S(1)}, f32[32,512]{1,0:T(8,128)}, u32[]{:S(2)}) copy-start(f32[32,512]{1,0:T(8,128)} %param.12) | copy-start | bytes 196612
  50.9 41.2 %copy-start.13 = (f32[32,512]{1,0:T(8,128)S(1)}, f32[32,512]{1,0:T(8,128)}, u32[]{:S(2)}) copy-start(f32[32,512]{1,0:T(8,128)} %param.11) | copy-start | bytes 196612
  62.3 4.3 %collective-permute-start.13 = (f32[2,16,512]{2,1,0:T(8,128)S(1)}, f32[2,16,512]{2,1,0:T(8,128)S(1)}, u32[]{:S(2)}, u32[]{:S(2)}) collective-permute-start(f32[2,16,512]{2,1,0:T(8,128)S(1)} %add.28), channel_id=1, source_target_pairs={{0,1},{1,0},{2,3},{3,2},{4,5},{5,4},{6,7},{7,6},{8,9},{9,8},{10,11... | collective-permute-start | bytes 196616 | tf_op jit(solution)/shard_map/ppermute | solution.py:456
  63.0 5.3 %collective-permute-start.1 = (f32[2,16,512]{2,1,0:T(8,128)S(1)}, f32[2,16,512]{2,1,0:T(8,128)S(1)}, u32[]{:S(2)}, u32[]{:S(2)}) collective-permute-start(f32[2,16,512]{2,1,0:T(8,128)S(1)} %add.25), channel_id=1, source_target_pairs={{0,2},{1,3},{2,0},{3,1},{4,6},{5,7},{6,4},{7,5},{8,10},{9,11},{10,... | collective-permute-start | bytes 196616 | tf_op jit(solution)/shard_map/ppermute | solution.py:456
  66.7 5.0 %collective-permute-start.14 = (f32[2,16,512]{2,1,0:T(8,128)S(1)}, f32[2,16,512]{2,1,0:T(8,128)S(1)}, u32[]{:S(2)}, u32[]{:S(2)}) collective-permute-start(f32[2,16,512]{2,1,0:T(8,128)S(1)} %add.29), channel_id=1, source_target_pairs={{0,2},{1,3},{2,0},{3,1},{4,6},{5,7},{6,4},{7,5},{8,10},{9,11},{10,... | collective-permute-start | bytes 196616 | tf_op jit(solution)/shard_map/ppermute | solution.py:456
  68.3 8.6 %collective-permute-start.2 = (f32[2,16,512]{2,1,0:T(8,128)S(1)}, f32[2,16,512]{2,1,0:T(8,128)S(1)}, u32[]{:S(2)}, u32[]{:S(2)}) collective-permute-start(f32[2,16,512]{2,1,0:T(8,128)S(1)} %add.26), channel_id=1, source_target_pairs={{0,4},{1,5},{2,6},{3,7},{4,0},{5,1},{6,2},{7,3},{8,12},{9,13},{10,... | collective-permute-start | bytes 196616 | tf_op jit(solution)/shard_map/ppermute | solution.py:456
  71.7 10.6 %collective-permute-start.15 = (f32[2,16,512]{2,1,0:T(8,128)S(1)}, f32[2,16,512]{2,1,0:T(8,128)S(1)}, u32[]{:S(2)}, u32[]{:S(2)}) collective-permute-start(f32[2,16,512]{2,1,0:T(8,128)S(1)} %add.30), channel_id=1, source_target_pairs={{0,4},{1,5},{2,6},{3,7},{4,0},{5,1},{6,2},{7,3},{8,12},{9,13},{10,... | collective-permute-start | bytes 196616 | tf_op jit(solution)/shard_map/ppermute | solution.py:456
  74.4 31.0 %collective-permute-start.12 = (f32[2,36,8,512]{3,2,1,0:T(8,128)}, f32[2,36,8,512]{3,2,1,0:T(8,128)S(1)}, u32[]{:S(2)}, u32[]{:S(2)}) collective-permute-start(f32[2,36,8,512]{3,2,1,0:T(8,128)} %get-tuple-element.50), channel_id=1, source_target_pairs={{1,0},{2,1},{3,2},{4,3},{5,4},{6,5},{7,6},{9,8},{10,9},{11,10},{12... | collective-permute-start | bytes 3538952 | tf_op jit(solution)/shard_map/ppermute | solution.py:506
  75.6 54.9 %collective-permute-start.11 = (f32[2,36,8,512]{3,2,1,0:T(8,128)}, f32[2,36,8,512]{3,2,1,0:T(8,128)S(1)}, u32[]{:S(2)}, u32[]{:S(2)}) collective-permute-start(f32[2,36,8,512]{3,2,1,0:T(8,128)} %get-tuple-element.49), channel_id=1, source_target_pairs={{1,0},{2,1},{3,2},{4,3},{5,4},{6,5},{7,6},{9,8},{10,9},{11,10},{12... | collective-permute-start | bytes 3538952 | tf_op jit(solution)/shard_map/ppermute | solution.py:506
  76.9 101.9 %collective-permute-start.6 = (f32[2,36,8,512]{3,2,1,0:T(8,128)}, f32[2,36,8,512]{3,2,1,0:T(8,128)S(1)}, u32[]{:S(2)}, u32[]{:S(2)}) collective-permute-start(f32[2,36,8,512]{3,2,1,0:T(8,128)} %get-tuple-element.42), channel_id=1, source_target_pairs={{0,1},{1,2},{2,3},{3,4},{4,5},{5,6},{6,7},{8,9},{9,10},{10,11},{11... | collective-permute-start | bytes 3538952 | tf_op jit(solution)/shard_map/ppermute | solution.py:506
  82.2 101.2 %collective-permute-start.10 = (f32[2,36,8,512]{3,2,1,0:T(8,128)}, f32[2,36,8,512]{3,2,1,0:T(8,128)S(1)}, u32[]{:S(2)}, u32[]{:S(2)}) collective-permute-start(f32[2,36,8,512]{3,2,1,0:T(8,128)} %get-tuple-element.48), channel_id=1, source_target_pairs={{1,0},{2,1},{3,2},{4,3},{5,4},{6,5},{7,6},{9,8},{10,9},{11,10},{12... | collective-permute-start | bytes 3538952 | tf_op jit(solution)/shard_map/ppermute | solution.py:506
  83.5 10.8 %copy-start = (f32[2,36,8,512]{3,2,1,0:T(8,128)}, f32[2,36,8,512]{3,2,1,0:T(8,128)S(1)}, u32[]{:S(2)}) copy-start(f32[2,36,8,512]{3,2,1,0:T(8,128)S(1)} %collective-permute-done.7.send_ref.refs_7_) | copy-start | bytes 3538948
  83.5 120.5 %collective-permute-start.5 = (f32[2,36,8,512]{3,2,1,0:T(8,128)}, f32[2,36,8,512]{3,2,1,0:T(8,128)S(1)}, u32[]{:S(2)}, u32[]{:S(2)}) collective-permute-start(f32[2,36,8,512]{3,2,1,0:T(8,128)} %get-tuple-element.40), channel_id=1, source_target_pairs={{0,1},{1,2},{2,3},{3,4},{4,5},{5,6},{6,7},{8,9},{9,10},{10,11},{11... | collective-permute-start | bytes 3538952 | tf_op jit(solution)/shard_map/ppermute | solution.py:506
  105.3 1.0 copy-start.1
  130.6 1.0 copy-start.2
  178.9 1.0 copy-start.3
  183.4 1.0 copy-start.4
  204.1 1.1 copy-start.5

commit v3 on v2

--- a/solution.py
+++ b/solution.py
@@ -29,6 +29,8 @@
 TURN_UNROLL = 3
 DELTA_UNROLL = 4
 SOURCE_UNROLL = 4
+SOURCE_LANES = 256
+COST = pl.CostEstimate(flops=1024, bytes_accessed=1024, transcendentals=0)
 
 
 def tables(band_total, dir_count):
@@ -147,6 +149,13 @@
 
 def exact_dot(cells, chooser, split_ref):
     count = cells.shape[0]
+    split_store(cells, split_ref)
+    product = jnp.dot(split_ref[...], chooser, preferred_element_type=jnp.float32)
+    return product[0:count] + product[count : 2 * count] + product[2 * count : 3 * count]
+
+
+def split_store(cells, split_ref):
+    count = cells.shape[0]
     high = cells.astype(jnp.bfloat16)
     rest = cells - high.astype(jnp.float32)
     mid = rest.astype(jnp.bfloat16)
@@ -154,14 +163,20 @@
     split_ref[0:count, :] = high
     split_ref[count : 2 * count, :] = mid
     split_ref[2 * count : 3 * count, :] = low
-    product = jnp.dot(split_ref[...], chooser, preferred_element_type=jnp.float32)
-    return product[0:count] + product[count : 2 * count] + product[2 * count : 3 * count]
-
-
-def propagate_kernel(strips, spill_slot, dests, edge, group, band_total, dir_count, local_bands, *refs):
+
+
+def local_band(index, flip, local_bands):
+    return index + flip * (local_bands - 1 - 2 * index)
+
+
+def propagate_kernel(strips, spill_slot, dests, split, edge, chained, group, dir_count, local_bands, *refs):
     refs = list(refs)
-    pos_ref, tab_ref, spec_ref, land_ref, sx_ref, sy_ref = refs[:6]
+    meta_ref, tab_ref, spec_ref, land_ref, sx_ref, sy_ref = refs[:6]
     refs = refs[6:]
+    prior_ref = None
+    if chained:
+        prior_ref = refs[0]
+        refs = refs[1:]
     lower_ref = upper_ref = spill_ref = None
     if edge:
         lower_ref, upper_ref, spill_ref = refs[:3]
@@ -170,8 +185,9 @@
     refs = refs[len(dests) :]
     out_refs = refs[: len(strips)]
     refs = refs[len(strips) :]
-    send_refs = refs[: len(dests)]
-    refs = refs[len(dests) :]
+    send_count = sum(2 if two else 1 for two in split)
+    send_refs = refs[:send_count]
+    refs = refs[send_count:]
     sum_ref = refs[0]
     refs = refs[1:]
     head_ref = tail_ref = None
@@ -182,7 +198,7 @@
 
     row_count, cols = land_ref.shape
     step = pl.program_id(0)
-    band = pos_ref[0] * local_bands + group + step
+    band = meta_ref[0] * local_bands + local_band(group + step, meta_ref[1], local_bands)
     growth = tab_ref[6 * dir_count + band]
     courant = COURANT_TOP / growth
     turn_rate = TURN_TOP / growth
@@ -196,7 +212,7 @@
 
     @pl.when(step == 0)
     def _():
-        sum_ref[...] = jnp.zeros_like(sum_ref)
+        sum_ref[...] = prior_ref[...] if chained else jnp.zeros_like(sum_ref)
 
         @pl.loop(0, dir_count)
         def _(f):
@@ -286,92 +302,154 @@
     start = tuple((face_flux(slot, 0, turn_ref[slot, 0]), zero) for slot in range(len(strips)))
     ends = lax.fori_loop(0, dir_count // TURN_UNROLL, turn, start)
     for slot, (_, total) in enumerate(ends):
-        rows = slice(STRIP * slot, STRIP * (slot + 1))
+        rows = slice(STRIP * strips[slot], STRIP * (strips[slot] + 1))
         sum_ref[0, rows, :] += weight * total
         sum_ref[1, rows, :] += (SPACING * 2.0 * math.pi / dir_count) * total
 
     source = spill_ref if edge else out_refs[spill_slot]
     spill = source[0].reshape(dir_count * STRIP, cols)
-    for chooser, dest, send_ref in zip(choosers, dests, send_refs):
-        filled = exact_dot(spill, chooser[...], split_ref)
-        send_ref[0] = out_refs[dest][0] + filled.reshape(dir_count, STRIP, cols)
-
-
-def propagate(strips, spill_slot, dests, edge, group, size, band_total, pos, table, spectrum, land_sea, slope_x, slope_y, extra, choosers):
+    for chooser, dest, two in zip(choosers, dests, split):
+        filled = exact_dot(spill, chooser[...], split_ref).reshape(dir_count, STRIP, cols)
+        if two:
+            for index in range(2):
+
+                @pl.when(step == index)
+                def _():
+                    send_refs[index][0] = out_refs[dest][0] + filled
+
+            send_refs = send_refs[2:]
+        else:
+            send_refs[0][0] = out_refs[dest][0] + filled
+            send_refs = send_refs[1:]
+
+
+def propagate(strips, spill_slot, dests, split, edge, group, size, meta, table, spectrum, land_sea, slope_x, slope_y, prior, extra, choosers):
     local_bands, dir_count, row_count, cols = spectrum.shape
-    whole = lambda shape: pl.BlockSpec(shape, lambda b: (0,) * len(shape))
-    one = lambda rows: pl.BlockSpec((1, dir_count, rows, cols), lambda b: (b, 0, 0, 0))
-    smem = pl.BlockSpec(memory_space=pltpu.SMEM)
+    whole = lambda shape: pl.BlockSpec(shape, lambda b, meta: (0,) * len(shape))
+    one = lambda rows: pl.BlockSpec((1, dir_count, rows, cols), lambda b, meta: (b, 0, 0, 0))
     flat = whole((row_count, cols))
-    in_specs = [smem, smem]
-    in_specs += [pl.BlockSpec((1, dir_count, row_count, cols), lambda b: (b + group, 0, 0, 0))]
+    in_specs = [pl.BlockSpec(memory_space=pltpu.SMEM)]
+    in_specs += [
+        pl.BlockSpec(
+            (1, dir_count, row_count, cols),
+            lambda b, meta: (local_band(b + group, meta[1], local_bands), 0, 0, 0),
+        )
+    ]
     in_specs += [flat, flat, flat]
+    sums = (2, row_count, cols)
+    in_specs += [whole(sums)] * len(prior)
     if edge:
-        halo = pl.BlockSpec((1, dir_count, 2, cols), lambda b: (b, 0, 0, 0))
-        in_specs += [halo, halo, one(STRIP)]
+        in_specs += [one(2), one(2), one(STRIP)]
     in_specs += [whole((cols, cols))] * len(choosers)
     band_array = lambda rows: jax.ShapeDtypeStruct((size, dir_count, rows, cols), jnp.float32)
-    out_shape = [band_array(STRIP)] * (len(strips) + len(dests))
-    out_specs = [one(STRIP)] * (len(strips) + len(dests))
-    sums = (2, STRIP * len(strips), cols)
+    out_shape = [band_array(STRIP)] * len(strips)
+    out_specs = [one(STRIP)] * len(strips)
+    for two in split:
+        if two:
+            out_shape += [jax.ShapeDtypeStruct((1, dir_count, STRIP, cols), jnp.float32)] * 2
+            out_specs += [whole((1, dir_count, STRIP, cols))] * 2
+        else:
+            out_shape.append(band_array(STRIP))
+            out_specs.append(one(STRIP))
     out_shape.append(jax.ShapeDtypeStruct(sums, jnp.float32))
     out_specs.append(whole(sums))
     if not edge:
         out_shape += [band_array(2)] * 2
         out_specs += [one(2)] * 2
-    cells = size * dir_count * len(strips) * STRIP * cols
     return pl.pallas_call(
-        functools.partial(
-            propagate_kernel, strips, spill_slot, dests, edge, group, band_total, dir_count, local_bands
+        functools.partial(propagate_kernel, strips, spill_slot, dests, split, edge, len(prior) > 0, group, dir_count, local_bands),
+        grid_spec=pltpu.PrefetchScalarGridSpec(
+            num_scalar_prefetch=1,
+            grid=(size,),
+            in_specs=in_specs,
+            out_specs=out_specs,
+            scratch_shapes=[
+                pltpu.VMEM((len(strips), dir_count, STRIP, cols), jnp.float32),
+                pltpu.VMEM((len(strips), dir_count + 4, STRIP, cols), jnp.float32),
+                pltpu.VMEM((3 * dir_count * STRIP, cols), jnp.bfloat16),
+            ],
         ),
-        grid=(size,),
+        out_shape=out_shape,
+        compiler_params=pltpu.CompilerParams(vmem_limit_bytes=VMEM_BYTES),
+        cost_estimate=COST,
+        name="propagate_edge" if edge else "propagate_inner",
+    )(meta, table, spectrum, land_sea, slope_x, slope_y, *prior, *extra, *choosers)
+
+
+def unpack_kernel(places, has_total, *refs):
+    out_ref, split_ref = refs[-2:]
+    total_ref, chooser_ref = refs[-4], refs[-4 - has_total]
+    _, dir_count, rows, cols = out_ref.shape
+    count = dir_count * rows
+    for slot, place in enumerate(places):
+
+        @pl.when(pl.program_id(0) == slot)
+        def _():
+            split_store(refs[place][0].reshape(count, cols), split_ref)
+
+    product = jnp.dot(split_ref[...], chooser_ref[...], preferred_element_type=jnp.float32)
+    cells = product[0:count] + product[count : 2 * count] + product[2 * count : 3 * count]
+    cells = cells.reshape(dir_count, rows, cols)
+    out_ref[0] = cells + total_ref[0] if has_total else cells
+
+
+def slot_map(uses, slots):
+    held = []
+    for use, slot in zip(uses, slots):
+        held.append(slot if use else (held[-1] if held else None))
+    first = next(slot for slot in held if slot is not None)
+    held = [first if slot is None else slot for slot in held]
+
+    def index(step):
+        place = held[0]
+        for k in range(1, len(held)):
+            place = place + jnp.where(step >= k, held[k] - held[k - 1], 0)
+        return place
+
+    return index
+
+
+def unpack(halo, chooser, total, after):
+    arrays = distinct(halo)
+    places = [next(i for i, a in enumerate(arrays) if a is array) for array, _ in halo]
+    _, dir_count, rows, cols = arrays[0].shape
+    block = (1, dir_count, rows, cols)
+    in_specs = []
+    for i in range(len(arrays)):
+        index = slot_map([place == i for place in places], [slot for _, slot in halo])
+        in_specs.append(pl.BlockSpec(block, lambda b, index=index: (index(b), 0, 0, 0)))
+    one = pl.BlockSpec(block, lambda b: (b, 0, 0, 0))
+    in_specs.append(pl.BlockSpec(chooser.shape, lambda b: (0, 0)))
+    extra = [] if total is None else [total]
+    in_specs += [one] * len(extra)
+    in_specs.append(pl.BlockSpec(memory_space=pl.ANY))
+    return pl.pallas_call(
+        functools.partial(unpack_kernel, places, len(extra)),
+        grid=(len(halo),),
         in_specs=in_specs,
-        out_specs=out_specs,
-        out_shape=out_shape,
-        scratch_shapes=[
-            pltpu.VMEM((len(strips), dir_count, STRIP, cols), jnp.float32),
-            pltpu.VMEM((len(strips), dir_count + 4, STRIP, cols), jnp.float32),
-            pltpu.VMEM((3 * dir_count * STRIP, cols), jnp.bfloat16),
-        ],
-        compiler_params=pltpu.CompilerParams(vmem_limit_bytes=VMEM_BYTES),
-        cost_estimate=pl.CostEstimate(flops=60 * cells, bytes_accessed=16 * cells, transcendentals=0),
-        name="propagate_edge" if edge else "propagate_inner",
-    )(pos, table, spectrum, land_sea, slope_x, slope_y, *extra, *choosers)
-
-
-def unpack_kernel(has_total, send_ref, chooser_ref, *refs):
-    out_ref, split_ref = refs[-2:]
-    _, dir_count, rows, cols = send_ref.shape
-    cells = exact_dot(send_ref[0].reshape(dir_count * rows, cols), chooser_ref[...], split_ref)
-    cells = cells.reshape(dir_count, rows, cols)
-    out_ref[0] = cells + refs[0][0] if has_total else cells
-
-
-def unpack(sent, chooser, total):
-    bands, dir_count, rows, cols = sent.shape
-    one = pl.BlockSpec((1, dir_count, rows, cols), lambda b: (b, 0, 0, 0))
-    totals = [] if total is None else [total]
-    return pl.pallas_call(
-        functools.partial(unpack_kernel, total is not None),
-        grid=(bands,),
-        in_specs=[one, pl.BlockSpec(chooser.shape, lambda b: (0, 0))] + [one] * len(totals),
         out_specs=one,
-        out_shape=jax.ShapeDtypeStruct(sent.shape, jnp.float32),
+        out_shape=jax.ShapeDtypeStruct((len(halo),) + block[1:], jnp.float32),
         scratch_shapes=[pltpu.VMEM((3 * dir_count * rows, cols), jnp.bfloat16)],
         compiler_params=pltpu.CompilerParams(vmem_limit_bytes=VMEM_BYTES),
-        cost_estimate=pl.CostEstimate(flops=8 * sent.size, bytes_accessed=12 * sent.size, transcendentals=0),
+        cost_estimate=COST,
         name="unpack",
-    )(sent, chooser, *totals)
-
-
-def source_kernel(dir_count, local_bands, group_count, below_count, above_count, *refs):
-    pos_ref, tab_ref, land_ref, wind_ref, sum_ref = refs[:5]
+    )(*arrays, chooser, *extra, after)
+
+
+def distinct(halo):
+    arrays = []
+    for array, _ in halo:
+        if not any(array is other for other in arrays):
+            arrays.append(array)
+    return arrays
+
+
+def source_kernel(dir_count, local_bands, places, *refs):
+    meta_ref, tab_ref, land_ref, wind_ref, sum_ref = refs[:5]
     refs = refs[5:]
-    own = refs[:group_count]
-    below = refs[group_count : group_count + below_count]
-    above = refs[group_count + below_count : group_count + below_count + above_count]
     out_ref, delta_ref = refs[-2:]
-    bands = [(ref, i) for ref in (*below, *own, *above) for i in range(ref.shape[0])]
+    bands = [(refs[place], slot) for place, slot in places]
+    flip = meta_ref[1]
 
     def density(index, j):
         ref, slot = bands[index + 2]
@@ -389,17 +467,18 @@
 
     @unrolled(0, dir_count, DELTA_UNROLL)
     def _(j):
-        up = lax.rem(j + 1, dir_count)
-        back = lax.rem(j + dir_count - 3, dir_count)
+        up = lax.rem(j + dir_count + 1 - 4 * flip, dir_count)
+        back = lax.rem(j + dir_count - 3 + 4 * flip, dir_count)
         for index in range(-1, local_bands + 1):
             center = density(index, j)
             plus = density(index + 1, up)
             minus = density(index - 1, back)
             delta_ref[index + 1, j] = center * (center * (plus + minus) - 2.0 * (plus * minus))
 
-    growths, keeps = [], []
+    growths, keeps, homes = [], [], []
     for index in range(local_bands):
-        growth = tab_ref[6 * dir_count + pos_ref[0] * local_bands + index]
+        homes.append(local_band(index, flip, local_bands))
+        growth = tab_ref[6 * dir_count + meta_ref[0] * local_bands + homes[index]]
         radian_freq = (2.0 * math.pi * BASE_FREQ) * growth
         wavenum = radian_freq * radian_freq * (1.0 / GRAVITY)
         growths.append(radian_freq)
@@ -407,42 +486,45 @@
 
     @unrolled(0, dir_count, SOURCE_UNROLL)
     def _(j):
-        up = lax.rem(j + 3, dir_count)
-        back = lax.rem(j + dir_count - 1, dir_count)
+        up = lax.rem(j + dir_count + 3 - 4 * flip, dir_count)
+        back = lax.rem(j + dir_count - 1 + 4 * flip, dir_count)
         wind = tab_ref[4 * dir_count + j] * wind_ref[0] + tab_ref[5 * dir_count + j] * wind_ref[1]
         for index in range(local_bands):
             radian_freq = growths[index]
             quad = delta_ref[index, back] + delta_ref[index + 2, up] - 2.0 * delta_ref[index + 1, j]
-            gain = 1.0 + jnp.maximum(radian_freq * wind - 1.0, 0.0) * (WIND_COEF * radian_freq)
-            out_ref[index, j] = density(index, j) * gain * keeps[index] + quad * quad_scale
-
-
-def source(strip, shape, pos, table, land_sea, wind, sums, sum_block, own, below, above, previous):
+            rate = WIND_COEF * radian_freq
+            gain = jnp.maximum((rate * radian_freq) * wind + (1.0 - rate), 1.0)
+            out_ref[homes[index], j] = density(index, j) * gain * keeps[index] + quad * quad_scale
+
+
+def source(strip, shape, meta, table, land_sea, wind, sums, sum_block, bands, previous):
     local_bands, dir_count, row_count, cols = shape
+    lanes = SOURCE_LANES if cols % SOURCE_LANES == 0 else cols
+    arrays = distinct(bands)
+    places = [(next(i for i, a in enumerate(arrays) if a is array), slot) for array, slot in bands]
     smem = pl.BlockSpec(memory_space=pltpu.SMEM)
-    part = lambda ref: pl.BlockSpec((ref.shape[0], dir_count, STRIP, LANES), lambda c: (0, 0, 0, c))
+    part = lambda ref: pl.BlockSpec((ref.shape[0], dir_count, STRIP, lanes), lambda c: (0, 0, 0, c))
     in_specs = [smem, smem]
-    in_specs.append(pl.BlockSpec((STRIP, LANES), lambda c: (strip, c)))
-    in_specs.append(pl.BlockSpec((2, STRIP, LANES), lambda c: (0, strip, c)))
-    in_specs.append(pl.BlockSpec((2, STRIP, LANES), lambda c: (0, sum_block, c)))
-    in_specs += [part(ref) for ref in own + below + above]
-    operands = [pos, table, land_sea, wind, sums, *own, *below, *above]
+    in_specs.append(pl.BlockSpec((STRIP, lanes), lambda c: (strip, c)))
+    in_specs.append(pl.BlockSpec((2, STRIP, lanes), lambda c: (0, strip, c)))
+    in_specs.append(pl.BlockSpec((2, STRIP, lanes), lambda c: (0, sum_block, c)))
+    in_specs += [part(ref) for ref in arrays]
+    operands = [meta, table, land_sea, wind, sums, *arrays]
     aliases = {}
     if previous is not None:
         in_specs.append(pl.BlockSpec(memory_space=pl.ANY))
         aliases = {len(operands): 0}
         operands.append(previous)
-    cells = local_bands * dir_count * STRIP * cols
     return pl.pallas_call(
-        functools.partial(source_kernel, dir_count, local_bands, len(own), len(below), len(above)),
-        grid=(cols // LANES,),
+        functools.partial(source_kernel, dir_count, local_bands, places),
+        grid=(cols // lanes,),
         in_specs=in_specs,
-        out_specs=pl.BlockSpec((local_bands, dir_count, STRIP, LANES), lambda c: (0, 0, strip, c)),
+        out_specs=pl.BlockSpec((local_bands, dir_count, STRIP, lanes), lambda c: (0, 0, strip, c)),
         out_shape=jax.ShapeDtypeStruct(shape, jnp.float32),
-        scratch_shapes=[pltpu.VMEM((local_bands + 2, dir_count, STRIP, LANES), jnp.float32)],
+        scratch_shapes=[pltpu.VMEM((local_bands + 2, dir_count, STRIP, lanes), jnp.float32)],
         input_output_aliases=aliases,
         compiler_params=pltpu.CompilerParams(vmem_limit_bytes=VMEM_BYTES),
-        cost_estimate=pl.CostEstimate(flops=30 * cells, bytes_accessed=16 * cells, transcendentals=0),
+        cost_estimate=COST,
         name="source",
     )(*operands)
 
@@ -451,6 +533,10 @@
     count = lax.axis_size("spec")
     if count & (count - 1):
         return lax.psum(value, "spec")
+    if count == 8:
+        value = value + lax.ppermute(value, "spec", [(i, i ^ 1) for i in range(count)])
+        others = [lax.ppermute(value, "spec", [(i, i ^ k) for i in range(count)]) for k in (2, 4, 6)]
+        return (value + others[0]) + (others[1] + others[2])
     reach = 1
     while reach < count:
         value = value + lax.ppermute(value, "spec", [(i, i ^ reach) for i in range(count)])
@@ -458,76 +544,141 @@
     return value
 
 
+def relay_pairs(count, first_across):
+    first, second = [], []
+    for low in range(1, count - 1, 2):
+        for source, goal in ((low + 1, low), (low, low + 1)):
+            rank = low if source > goal else count - 2 - low
+            if first_across(rank):
+                first.append((source, source ^ 1))
+                second.append((source ^ 1, goal))
+            else:
+                first.append((source, goal))
+                second.append((goal, goal))
+    return first, second
+
+
+def along_pairs(count):
+    first, second = [], []
+    for low in range(1, count - 1, 2):
+        for source, goal in ((low + 1, low), (low, low + 1)):
+            first.append((source, goal ^ 1))
+            second.append((goal ^ 1, goal))
+    return first, second
+
+
+def hold(value, *others):
+    whole = pl.BlockSpec(memory_space=pl.ANY)
+    return pl.pallas_call(
+        lambda *refs: None,
+        in_specs=[whole] * (1 + len(others)),
+        out_specs=whole,
+        out_shape=jax.ShapeDtypeStruct(value.shape, value.dtype),
+        input_output_aliases={0: 0},
+        cost_estimate=COST,
+        name="hold",
+    )(value, *others)
+
+
 def shards(spectrum, land_sea, sea_index, sea_count, wind_speed, wind_dir, slope_x, slope_y):
     local_bands, dir_count, row_count, cols = spectrum.shape
     spec_count = lax.axis_size("spec")
     geo_count = lax.axis_size("geo")
-    band_total = local_bands * spec_count
-    pos = lax.axis_index("spec").astype(jnp.int32).reshape(1)
-    table = jnp.asarray(tables(band_total, dir_count))
+    pos = lax.axis_index("spec").astype(jnp.int32)
+    table = jnp.asarray(tables(local_bands * spec_count, dir_count))
     inner, outer, spill = (1, 2), (0, 3), 2
     kept = (1, 0, 3)
-    choose = plan(land_sea, kept, spill, (0,), False)
     size = min(2, local_bands)
     groups = list(range(0, local_bands, size))
-
-    args = (band_total, pos, table, spectrum, land_sea, slope_x, slope_y)
-    cells = {s: [] for s in range(4)}
-    sends = {1: [], 0: [], 3: []}
-    inner_sums, outer_sums = [], []
+    paired = local_bands == 4 and spec_count % 2 == 0
+    meta = jnp.stack([pos, pos % 2 if paired else 0 * pos])
+    choose = plan(land_sea, kept, spill, (0,), False)
+
+    args = (meta, table, spectrum, land_sea, slope_x, slope_y)
+    bands = {s: [] for s in range(4)}
+    sends = {s: [] for s in kept}
+    rims, prior = [], []
     for group in groups:
         strip_a, strip_b, send, sums, head, tail = propagate(
-            inner, 1, (0,), False, group, size, *args, (), choose[:1]
+            inner, 1, (0,), (False,), False, group, size, *args, prior, (), choose[:1]
         )
-        cells[1].append(strip_a)
-        cells[2].append(strip_b)
-        sends[1].append(send)
-        inner_sums.append((sums, head, tail))
-    choose = choose + plan(land_sea, kept, spill, (1, 2), False)
+        bands[1].append(strip_a)
+        bands[2].append(strip_b)
+        sends[1].append([send])
+        rims.append((head, tail))
+        prior = [sums]
+    choose = list(choose) + list(plan(land_sea, kept, spill, (1, 2), False))
     ups = [(i, i + 1) for i in range(geo_count - 1)]
     downs = [(i + 1, i) for i in range(geo_count - 1)]
     for index, group in enumerate(groups):
-        _, head, tail = inner_sums[index]
+        head, tail = rims[index]
         lower = lax.ppermute(tail, "geo", ups)
         upper = lax.ppermute(head, "geo", downs)
-        strip_a, strip_b, send_a, send_b, sums = propagate(
-            outer, None, (0, 1), True, group, size, *args, (lower, upper, cells[2][index]), choose[1:]
+        split = paired and index == 0
+        strip_a, strip_b, *send, sums = propagate(
+            outer, None, (0, 1), (split, False), True, group, size, *args, prior, (lower, upper, bands[2][index]), choose[1:]
         )
-        cells[0].append(strip_a)
-        cells[3].append(strip_b)
-        sends[0].append(send_a)
-        sends[3].append(send_b)
-        outer_sums.append(sums)
-    inner_total = spec_total(functools.reduce(jnp.add, [entry[0] for entry in inner_sums]))
-    outer_total = spec_total(functools.reduce(jnp.add, outer_sums))
-
-    def hop(value, count):
-        pairs = [(i, i + count) for i in range(spec_count) if 0 <= i + count < spec_count]
-        return lax.ppermute(value, "spec", pairs)
-
-    below, above = {}, {}
-    for s in kept:
-        if size == 2:
-            below[s] = [hop(sends[s][-1], 1)]
-            above[s] = [hop(sends[s][0], -1)]
-        else:
-            below[s] = [hop(sends[s][0], 2), hop(sends[s][0], 1)]
-            above[s] = [hop(sends[s][0], -1), hop(sends[s][0], -2)]
-
+        bands[0].append(strip_a)
+        bands[3].append(strip_b)
+        sends[0].append(send[:-1])
+        sends[3].append(send[-1:])
+        prior = [sums]
+    sums = prior[0]
     scale = (28.0 * USTAR_RATIO / GRAVITY) * wind_speed
     wind = jnp.stack([scale * jnp.cos(wind_dir), scale * jnp.sin(wind_dir)])
-    back = plan(land_sea, kept, spill, (0, 1, 2), True)
-    below[spill], above[spill] = [None] * len(below[1]), [None] * len(above[1])
-    for s, chooser in zip(kept, back):
-        for side in (below, above):
-            side[spill] = [unpack(sent, chooser, total) for sent, total in zip(side[s], side[spill])]
-    result = None
-    for s in kept + (spill,):
-        sums, block = (inner_total, inner.index(s)) if s in inner else (outer_total, outer.index(s))
-        result = source(
-            s, spectrum.shape, pos, table, land_sea, wind, sums, block, cells[s], below[s], above[s], result
-        )
-    return result
+    back = dict(zip(kept, plan(land_sea, kept, spill, (0, 1, 2), True)))
+
+    def finish(s, halo, result, total):
+        if s != spill:
+            total = unpack(halo, back[s], total, sums if result is None else result)
+        own = [(array, i) for array in bands[s] for i in range(size)]
+        members = halo[:2] + own + halo[2:]
+        result = source(s, spectrum.shape, meta, table, land_sea, wind, sums, s, members, result)
+        return result, total
+
+    result = total = None
+    if paired:
+        partner = [(i, i ^ 1) for i in range(spec_count)]
+        across = relay_pairs(spec_count, lambda rank: True)
+        most = relay_pairs(spec_count, lambda rank: 2 * rank >= spec_count - 2)
+        some = relay_pairs(spec_count, lambda rank: rank >= spec_count - 3)
+        along = along_pairs(spec_count)
+
+        def send(value, pairs):
+            return lax.ppermute(value, "spec", pairs)
+
+        def members(far, near):
+            return [(far[-1], far[-1].shape[0] - 1), (far[0], 0), (near, 1), (near, 0)]
+
+        far_1 = send(sends[1][0][0], across[0])
+        near_1 = send(sends[1][1][0], partner)
+        sums = spec_total(hold(sums, near_1))
+        near_0 = send(hold(sends[0][1][0], far_1), partner)
+        far_3 = send(sends[3][0][0], along[0])
+        far_0 = [send(value, pairs[0]) for value, pairs in zip(sends[0][0], (some, most))]
+        far_1 = send(far_1, across[1])
+        far_3 = send(far_3, along[1])
+        far_0 = [send(value, pairs[1]) for value, pairs in zip(far_0, (some, most))]
+        near_3 = send(hold(sends[3][1][0], near_0), partner)
+        result, total = finish(1, members([far_1], near_1), result, total)
+        result, total = finish(0, members(far_0, near_0), result, total)
+        result, total = finish(3, members([far_3], near_3), result, total)
+    else:
+
+        def hop(value, count):
+            pairs = [(i, i + count) for i in range(spec_count) if 0 <= i + count < spec_count]
+            return lax.ppermute(value, "spec", pairs)
+
+        sums = spec_total(sums)
+        for s in kept:
+            first, last = sends[s][0][0], sends[s][-1][0]
+            if size == 2:
+                lower, upper = hop(last, 1), hop(first, -1)
+                halo = [(lower, 0), (lower, 1), (upper, 0), (upper, 1)]
+            else:
+                halo = [(hop(last, 2), 0), (hop(last, 1), 0), (hop(first, -1), 0), (hop(first, -2), 0)]
+            result, total = finish(s, halo, result, total)
+    return finish(spill, [(total, i) for i in range(4)], result, total)[0]
 
 
 def solution(mesh):

time: 231 us -> 199 us (0.86); the launches traced: 227 us -> 198 us
  waiting for transfers between devices: 86.3 us -> 59.8 us
  Pallas kernels: 91.8 us -> 88.8 us
    ppermute x12 -> x15, waiting for transfers between devices: 86.3 us -> 59.8 us  [the longest x11 47.6 us: send(): return lax.ppermute(value, 'spec', pairs)]
    pallas_call x10, Pallas kernels: 45.2 us -> 38.6 us  [the longest x4 19.8 us: source(): pl.pallas_call(functools.partial(source_kernel, dir_count, local_bands, p...]
    pallas_call x4, Pallas kernels: 38.9 us -> 42.5 us  [propagate(): pl.pallas_call(functools.partial(propagate_kernel, strips, spill_slot, de...]
    unnamed x32 -> x22, local copies, waits for them, and re-layouts: 6.72 us -> 5.8 us
    ppermute x12 -> x15, starting transfers between devices: 29.5 us -> 29.3 us  [the longest x11 23.9 us: send(): return lax.ppermute(value, 'spec', pairs)]
  transfers between devices with their start and end apart: 16 -> 19, of which waited for: 6 -> 6; matrix products, arithmetic and copies ran while one was open for 2% -> 2% of each run, Pallas kernels for 26% -> 31%
where the time goes in v3:
time: 199 us; the launch traced here: 198 us
  Pallas kernels  88.8 us (45%)
  waiting for transfers between devices  59.8 us (30%)
  starting transfers between devices  39.4 us (20%)
  local copies, waits for them, and re-layouts  5.8 us (3%)
  other arithmetic  4.03 us (2%)
    ppermute x11, waiting for transfers between devices, send(): return lax.ppermute(value, 'spec', pairs)  47.6 us
    pallas_call x4, Pallas kernels, propagate(): pl.pallas_call(functools.partial(propagate_kernel, strips, spill_slot, de...  42.5 us
    ppermute x11, starting transfers between devices, send(): return lax.ppermute(value, 'spec', pairs)  23.9 us
    pallas_call x4, Pallas kernels, source(): pl.pallas_call(functools.partial(source_kernel, dir_count, local_bands, p...  19.8 us
    pallas_call x3, Pallas kernels, unpack(): pl.pallas_call(functools.partial(unpack_kernel, places, len(extra)), grid...  18.8 us
    ppermute x3, waiting for transfers between devices, spec_total(): lax.ppermute(value, 'spec', [(i, i ^ k) for i in range(count)])  12.1 us
    pallas_call x3, Pallas kernels, plan(): pl.pallas_call(functools.partial(plan_kernel, kept, spill, wanted, back),...  7.67 us
    ppermute x2, starting transfers between devices, shards(): lower = lax.ppermute(tail, 'geo', ups)  7.51 us
  transfers between devices with their start and end apart: 19, of which 6 were waited for; matrix products, arithmetic and copies ran while one was open for 2% of the time, Pallas kernels for 31%

profile of v3, /device:TPU:0, one launch (start us, length us, event | category | flops | bytes accessed | tf_op | source)
XLA Modules:
  0.0 198.1 jit_solution(4663634140280136493)
XLA Ops:
  0.0 2.2 %plan.2.refs_6_.refs_7_ = bf16[512,512]{1,0:T(8,128)(2,1)} custom-call(s32[32,512]{1,0:T(8,128)} %refs_2_.15), custom_call_target="tpu_custom_call" | custom-call | tf_op jit(solution)/shard_map/plan/pallas_call | solution.py:111
  2.2 0.6 pad_add_fusion.refs_0_
  2.8 9.7 %propagate_inner.2 = (f32[2,36,8,512]{3,2,1,0:T(8,128)}, f32[2,36,8,512]{3,2,1,0:T(8,128)}, f32[2,36,8,512]{3,2,1,0:T(8,128)}, f32[2,32,512]{2,1,0:T(8,128)}, f3...) custom-call(s32[2]{0:T(128)} %pad_add_fusion.refs_0_, f32[248]{0:T(256)} %constant.21.clone.refs_1_, ...), custom_call_target="tpu_custom_call" | custom-call | flops 1024 | bytes 1024 | tf_op jit(solution)/shard_map/propagate_inner/pallas_call | solution.py:359
  12.5 1.3 collective-permute-start.11
  13.8 2.4 %collective-permute-start = (f32[2,36,2,512]{3,2,1,0:T(2,128)}, f32[2,36,2,512]{3,2,1,0:T(2,128)S(1)}, u32[]{:S(2)}, u32[]{:S(2)}) collective-permute-start(f32[2,36,2,512]{3,2,1,0:T(2,128)} %get-tuple-element.35), channel_id=1, source_target_pairs={{0,8},{8,16},{16,24},{1,9},{9,17},{17,25},{2,10},{10,18},{18,26},{... | collective-permute-start | bytes 884744 | tf_op jit(solution)/shard_map/ppermute | solution.py:615
  16.1 1.3 collective-permute-start.1
  17.4 9.8 %propagate_inner.3 = (f32[2,36,8,512]{3,2,1,0:T(8,128)}, f32[2,36,8,512]{3,2,1,0:T(8,128)}, f32[2,36,8,512]{3,2,1,0:T(8,128)}, f32[2,32,512]{2,1,0:T(8,128)}, f3...) custom-call(s32[2]{0:T(128)} %pad_add_fusion.refs_0_, f32[248]{0:T(256)} %constant.21.clone.refs_1_, ...), custom_call_target="tpu_custom_call" | custom-call | flops 1024 | bytes 1024 | tf_op jit(solution)/shard_map/propagate_inner/pallas_call | solution.py:359
  27.2 5.1 %collective-permute-start.2 = (f32[2,36,2,512]{3,2,1,0:T(2,128)}, f32[2,36,2,512]{3,2,1,0:T(2,128)S(1)}, u32[]{:S(2)}, u32[]{:S(2)}) collective-permute-start(f32[2,36,2,512]{3,2,1,0:T(2,128)} %get-tuple-element.41), channel_id=1, source_target_pairs={{0,8},{8,16},{16,24},{1,9},{9,17},{17,25},{2,10},{10,18},{18,26},{... | collective-permute-start | bytes 884744 | tf_op jit(solution)/shard_map/ppermute | solution.py:615
  32.4 1.3 collective-permute-start.3
  33.7 3.7 %collective-permute-start.4 = (f32[2,36,8,512]{3,2,1,0:T(8,128)}, f32[2,36,8,512]{3,2,1,0:T(8,128)S(1)}, u32[]{:S(2)}, u32[]{:S(2)}) collective-permute-start(f32[2,36,8,512]{3,2,1,0:T(8,128)} %get-tuple-element.45), channel_id=1, source_target_pairs={{0,1},{1,0},{2,3},{3,2},{4,5},{5,4},{6,7},{7,6},{8,9},{9,8},{10,11... | collective-permute-start | bytes 3538952 | tf_op jit(solution)/shard_map/ppermute | solution.py:648
  37.4 2.6 %plan.3 = (bf16[512,512]{1,0:T(8,128)(2,1)}, bf16[512,512]{1,0:T(8,128)(2,1)}) custom-call(s32[32,512]{1,0:T(8,128)} %refs_2_.15), custom_call_target="tpu_custom_call" | custom-call | tf_op jit(solution)/shard_map/plan/pallas_call | solution.py:111
  40.0 0.7 copy-done.10
  40.7 11.9 %propagate_edge.2 = (f32[2,36,8,512]{3,2,1,0:T(8,128)}, f32[2,36,8,512]{3,2,1,0:T(8,128)}, f32[1,36,8,512]{3,2,1,0:T(8,128)}, f32[1,36,8,512]{3,2,1,0:T(8,128)},...) custom-call(s32[2]{0:T(128)} %pad_add_fusion.refs_0_, f32[248]{0:T(256)} %constant.21.clone.refs_1_, ...), custom_call_target="tpu_custom_call" | custom-call | flops 1024 | bytes 1024 | tf_op jit(solution)/shard_map/propagate_edge/pallas_call | solution.py:359
  52.6 1.3 collective-permute-start.9
  53.9 0.7 copy-done.7
  54.7 11.1 %propagate_edge.3 = (f32[2,36,8,512]{3,2,1,0:T(8,128)}, f32[2,36,8,512]{3,2,1,0:T(8,128)}, f32[2,36,8,512]{3,2,1,0:T(8,128)}, f32[2,36,8,512]{3,2,1,0:T(8,128)}, f32[2,32,512]{2,1,0:T(8,128)}) custom-call(s32[2]{0:T(128)} %pad_add_fusion.refs_0_, f32[248]{0:T(256)} %constant.21.clone.refs_1_, f32[4,36,32,512]{3,2,1,0:T(8,128)} %refs_2_.11, ...), custom_call_target="tpu_custom_call" | custom-call | flops 1024 | bytes 1024 | tf_op jit(solution)/shard_map/propagate_edge/pallas_call | solution.py:359
  65.9 3.8 %collective-permute-start.12 = (f32[2,36,8,512]{3,2,1,0:T(8,128)}, f32[2,36,8,512]{3,2,1,0:T(8,128)S(1)}, u32[]{:S(2)}, u32[]{:S(2)}) collective-permute-start(f32[2,36,8,512]{3,2,1,0:T(8,128)} %hold.4), channel_id=1, source_target_pairs={{0,1},{1,0},{2,3},{3,2},{4,5},{5,4},{6,7},{7,6},{8,9},{9,8},{10,11... | collective-permute-start | bytes 3538952 | tf_op jit(solution)/shard_map/ppermute | solution.py:648
  69.6 1.3 collective-permute-start.14
  70.9 1.3 collective-permute-start.16
  72.2 1.0 copy-done
  73.3 3.3 %collective-permute-start.5 = (f32[2,32,512]{2,1,0:T(8,128)}, f32[2,32,512]{2,1,0:T(8,128)}, u32[]{:S(2)}, u32[]{:S(2)}) collective-permute-start(f32[2,32,512]{2,1,0:T(8,128)} %hold.3), channel_id=1, source_target_pairs={{0,1},{1,0},{2,3},{3,2},{4,5},{5,4},{6,7},{7,6},{8,9},{9,8},{10,11... | collective-permute-start | bytes 393224 | tf_op jit(solution)/shard_map/ppermute | solution.py:537
  76.5 6.0 %collective-permute-done.9 = f32[2,36,8,512]{3,2,1,0:T(8,128)} collective-permute-done((f32[2,36,8,512]{3,2,1,0:T(8,128)}, f32[2,36,8,512]{3,2,1,0:T(8,128)}, u32[]{:S(2)}, u32[]{:S(2)}) %collective-permute-start.9) | collective-permute-done | bytes 1179680 | tf_op jit(solution)/shard_map/ppermute | solution.py:648
  82.5 2.5 %collective-permute-start.18 = (f32[2,36,8,512]{3,2,1,0:T(8,128)}, f32[2,36,8,512]{3,2,1,0:T(8,128)S(1)}, u32[]{:S(2)}, u32[]{:S(2)}) collective-permute-start(f32[2,36,8,512]{3,2,1,0:T(8,128)} %collective-permute-done.11.refs_1_), channel_id=1, source_target_pairs={{3,1},{0,2},{5,3},{2,4},{7,5},{4,6},{11,9},{8,10},{13,11},{10,12},... | collective-permute-start | bytes 3538952 | tf_op jit(solution)/shard_map/ppermute | solution.py:648
  85.1 35.7 %collective-permute-done.12.refs_1_.refs_2_.refs_9_ = f32[2,36,8,512]{3,2,1,0:T(8,128)S(1)} collective-permute-done((f32[2,36,8,512]{3,2,1,0:T(8,128)}, f32[2,36,8,512]{3,2,1,0:T(8,128)S(1)}, u32[]{:S(2)}, u32[]{:S(2)}) %collective-permute-start.12) | collective-permute-done | bytes 1179680 | tf_op jit(solution)/shard_map/ppermute | solution.py:648
  120.8 4.3 %collective-permute-start.10 = (f32[2,36,8,512]{3,2,1,0:T(8,128)}, f32[2,36,8,512]{3,2,1,0:T(8,128)S(1)}, u32[]{:S(2)}, u32[]{:S(2)}) collective-permute-start(f32[2,36,8,512]{3,2,1,0:T(8,128)} %collective-permute-done.9), channel_id=1, source_target_pairs={{0,1},{3,2},{2,3},{5,4},{4,5},{7,6},{8,9},{11,10},{10,11},{13,12},... | collective-permute-start | bytes 3538952 | tf_op jit(solution)/shard_map/ppermute | solution.py:648
  125.2 0.9 collective-permute-start.13
  126.1 1.0 add.17
  127.1 2.2 %collective-permute-start.8 = (f32[2,32,512]{2,1,0:T(8,128)S(1)}, f32[2,32,512]{2,1,0:T(8,128)S(1)}, u32[]{:S(2)}, u32[]{:S(2)}) collective-permute-start(f32[2,32,512]{2,1,0:T(8,128)S(1)} %add.17), channel_id=1, source_target_pairs={{0,6},{1,7},{2,4},{3,5},{4,2},{5,3},{6,0},{7,1},{8,14},{9,15},{10,... | collective-permute-start | bytes 393224 | tf_op jit(solution)/shard_map/ppermute | solution.py:538
  129.3 6.2 %collective-permute-done.8 = f32[2,32,512]{2,1,0:T(8,128)S(1)} collective-permute-done((f32[2,32,512]{2,1,0:T(8,128)S(1)}, f32[2,32,512]{2,1,0:T(8,128)S(1)}, u32[]{:S(2)}, u32[]{:S(2)}) %collective-permute-start.8) | collective-permute-done | bytes 131104 | tf_op jit(solution)/shard_map/ppermute | solution.py:538
  135.4 5.3 %collective-permute-done.7 = f32[2,32,512]{2,1,0:T(8,128)S(1)} collective-permute-done((f32[2,32,512]{2,1,0:T(8,128)S(1)}, f32[2,32,512]{2,1,0:T(8,128)S(1)}, u32[]{:S(2)}, u32[]{:S(2)}) %collective-permute-start.7) | collective-permute-done | bytes 131104 | tf_op jit(solution)/shard_map/ppermute | solution.py:538
  140.8 1.6 collective-permute-start.15
  142.4 0.6 collective-permute-done.6
  143.0 1.9 collective-permute-start.17
  144.9 2.9 %plan_back.1 = (bf16[512,512]{1,0:T(8,128)(2,1)}, bf16[512,512]{1,0:T(8,128)(2,1)}, bf16[512,512]{1,0:T(8,128)(2,1)}) custom-call(s32[32,512]{1,0:T(8,128)} %refs_2_.15), custom_call_target="tpu_custom_call" | custom-call | tf_op jit(solution)/shard_map/plan_back/pallas_call | solution.py:111
  147.8 1.1 multiply_bitcast_fusion.1
  148.9 0.7 pad_maximum_fusion.refs_3_
  149.6 0.7 add_add_fusion.refs_3_.refs_4_
  150.3 1.0 copy-done.2
  151.3 5.9 %unpack.3.refs_4_ = f32[4,36,8,512]{3,2,1,0:T(8,128)} custom-call(f32[2,36,8,512]{3,2,1,0:T(8,128)} %copy-done.2, f32[2,36,8,512]{3,2,1,0:T(8,128)} %copy-done, bf16[512,512]{1,0:T(8,128)(2,1)} %get-tuple-element.54.refs_2_, f32[2,32,512]{2,1,0:T(8,128)} %add_add_fusion.refs_3_.refs_4_), custom_call_target="tpu_custom_call" | custom-call | flops 1024 | bytes 1024 | tf_op jit(solution)/shard_map/unpack/pallas_call | solution.py:426
  157.2 5.0 %source.4.refs_5_.refs_10_ = f32[4,36,32,512]{3,2,1,0:T(8,128)} custom-call(s32[2]{0:T(128)} %pad_add_fusion.refs_0_, f32[248]{0:T(256)} %constant.21.clone.refs_1_, s32[32,512]{1,0:T(8,128)} %refs_2_.15, f32[2,32,512]{2,1,0:T(8,128)} %pad_maximum_fusion.refs_3_, f32[2,32,512]{2,1,0:T(8,128)} %add_add_fusion.refs_3_.refs_4_, f32[2,36,8,512]{3,2,1,0:T(8,128)} %copy-done.2, ...), custom_call_target="tpu_custom_call" | custom-call | flops 1024 | bytes 1024 | tf_op jit(solution)/shard_map/source/pallas_call | solution.py:518
  162.2 5.9 %collective-permute-done.17.refs_1_.refs_6_ = f32[1,36,8,512]{3,2,1,0:T(8,128)S(1)} collective-permute-done((f32[1,36,8,512]{3,2,1,0:T(8,128)}, f32[1,36,8,512]{3,2,1,0:T(8,128)S(1)}, u32[]{:S(2)}, u32[]{:S(2)}) %collective-permute-start.17) | collective-permute-done | bytes 589856 | tf_op jit(solution)/shard_map/ppermute | solution.py:648
  168.1 0.8 copy-done.6
  168.9 6.5 %unpack.4.refs_3_ = f32[4,36,8,512]{3,2,1,0:T(8,128)} custom-call(f32[1,36,8,512]{3,2,1,0:T(8,128)} %copy-done.5, f32[1,36,8,512]{3,2,1,0:T(8,128)} %copy-done.6, f32[2,36,8,512]{3,2,1,0:T(8,128)} %copy-done.1, bf16[512,512]{1,0:T(8,128)(2,1)} %get-tuple-element.53.refs_3_, f32[4,36,8,512]{3,2,1,0:T(8,128)} %unpack.3.refs_4_, ...), custom_call_target="tpu_custom_call" | custom-call | flops 1024 | bytes 1024 | tf_op jit(solution)/shard_map/unpack/pallas_call | solution.py:426
  175.4 5.0 %source.5.refs_4_.refs_9_ = f32[4,36,32,512]{3,2,1,0:T(8,128)} custom-call(s32[2]{0:T(128)} %pad_add_fusion.refs_0_, f32[248]{0:T(256)} %constant.21.clone.refs_1_, s32[32,512]{1,0:T(8,128)} %refs_2_.15, f32[2,32,512]{2,1,0:T(8,128)} %pad_maximum_fusion.refs_3_, f32[2,32,512]{2,1,0:T(8,128)} %add_add_fusion.refs_3_.refs_4_, ...), custom_call_target="tpu_custom_call", output_to_operand_aliasing={{}: (10, {})} | custom-call | flops 1024 | bytes 1024 | tf_op jit(solution)/shard_map/source/pallas_call | solution.py:518
  180.4 1.1 copy-done.3
  181.9 6.4 %unpack.5.refs_5_ = f32[4,36,8,512]{3,2,1,0:T(8,128)} custom-call(f32[2,36,8,512]{3,2,1,0:T(8,128)} %copy-done.3, f32[2,36,8,512]{3,2,1,0:T(8,128)} %copy-done.4, bf16[512,512]{1,0:T(8,128)(2,1)} %get-tuple-element.50.refs_2_, f32[4,36,8,512]{3,2,1,0:T(8,128)} %unpack.4.refs_3_, f32[4,36,32,512]{3,2,1,0:T(8,128)} %source.5.refs_4_.refs_9_), custom_call_target="tpu_custom_call" | custom-call | flops 1024 | bytes 1024 | tf_op jit(solution)/shard_map/unpack/pallas_call | solution.py:426
  188.2 5.0 %source.6.refs_8_ = f32[4,36,32,512]{3,2,1,0:T(8,128)} custom-call(s32[2]{0:T(128)} %pad_add_fusion.refs_0_, f32[248]{0:T(256)} %constant.21.clone.refs_1_, s32[32,512]{1,0:T(8,128)} %refs_2_.15, f32[2,32,512]{2,1,0:T(8,128)} %pad_maximum_fusion.refs_3_, f32[2,32,512]{2,1,0:T(8,128)} %add_add_fusion.refs_3_.refs_4_, ...), custom_call_target="tpu_custom_call", output_to_operand_aliasing={{}: (9, {})} | custom-call | flops 1024 | bytes 1024 | tf_op jit(solution)/shard_map/source/pallas_call | solution.py:518
  193.2 5.0 %source.7 = f32[4,36,32,512]{3,2,1,0:T(8,128)} custom-call(s32[2]{0:T(128)} %pad_add_fusion.refs_0_, f32[248]{0:T(256)} %constant.21.clone.refs_1_, s32[32,512]{1,0:T(8,128)} %refs_2_.15, f32[2,32,512]{2,1,0:T(8,128)} %pad_maximum_fusion.refs_3_, f32[2,32,512]{2,1,0:T(8,128)} %add_add_fusion.refs_3_.refs_4_, ...), custom_call_target="tpu_custom_call", output_to_operand_aliasing={{}: (8, {})} | custom-call | flops 1024 | bytes 1024 | tf_op jit(solution)/shard_map/source/pallas_call | solution.py:518
  (34 shorter events, 0.5 us)
Async XLA Ops:
  12.5 53.4 %collective-permute-start.11 = (f32[2,36,8,512]{3,2,1,0:T(8,128)}, f32[2,36,8,512]{3,2,1,0:T(8,128)}, u32[]{:S(2)}, u32[]{:S(2)}) collective-permute-start(f32[2,36,8,512]{3,2,1,0:T(8,128)} %get-tuple-element.49), channel_id=1, source_target_pairs={{2,3},{1,0},{4,5},{3,2},{6,7},{5,4},{10,11},{9,8},{12,13},{11,10},... | collective-permute-start | bytes 3538952 | tf_op jit(solution)/shard_map/ppermute | solution.py:648
  13.8 19.9 %collective-permute-start = (f32[2,36,2,512]{3,2,1,0:T(2,128)}, f32[2,36,2,512]{3,2,1,0:T(2,128)S(1)}, u32[]{:S(2)}, u32[]{:S(2)}) collective-permute-start(f32[2,36,2,512]{3,2,1,0:T(2,128)} %get-tuple-element.35), channel_id=1, source_target_pairs={{0,8},{8,16},{16,24},{1,9},{9,17},{17,25},{2,10},{10,18},{18,26},{... | collective-permute-start | bytes 884744 | tf_op jit(solution)/shard_map/ppermute | solution.py:615
  16.1 23.8 %collective-permute-start.1 = (f32[2,36,2,512]{3,2,1,0:T(2,128)}, f32[2,36,2,512]{3,2,1,0:T(2,128)S(1)}, u32[]{:S(2)}, u32[]{:S(2)}) collective-permute-start(f32[2,36,2,512]{3,2,1,0:T(2,128)} %get-tuple-element.36), channel_id=1, source_target_pairs={{8,0},{16,8},{24,16},{9,1},{17,9},{25,17},{10,2},{18,10},{26,18},{... | collective-permute-start | bytes 884744 | tf_op jit(solution)/shard_map/ppermute | solution.py:616
  27.2 26.7 %collective-permute-start.2 = (f32[2,36,2,512]{3,2,1,0:T(2,128)}, f32[2,36,2,512]{3,2,1,0:T(2,128)S(1)}, u32[]{:S(2)}, u32[]{:S(2)}) collective-permute-start(f32[2,36,2,512]{3,2,1,0:T(2,128)} %get-tuple-element.41), channel_id=1, source_target_pairs={{0,8},{8,16},{16,24},{1,9},{9,17},{17,25},{2,10},{10,18},{18,26},{... | collective-permute-start | bytes 884744 | tf_op jit(solution)/shard_map/ppermute | solution.py:615
  32.4 21.6 %collective-permute-start.3 = (f32[2,36,2,512]{3,2,1,0:T(2,128)}, f32[2,36,2,512]{3,2,1,0:T(2,128)S(1)}, u32[]{:S(2)}, u32[]{:S(2)}) collective-permute-start(f32[2,36,2,512]{3,2,1,0:T(2,128)} %get-tuple-element.42), channel_id=1, source_target_pairs={{8,0},{16,8},{24,16},{9,1},{17,9},{25,17},{10,2},{18,10},{26,18},{... | collective-permute-start | bytes 884744 | tf_op jit(solution)/shard_map/ppermute | solution.py:616
  33.7 6.3 %copy-start.9 = (f32[2,36,2,512]{3,2,1,0:T(2,128)}, f32[2,36,2,512]{3,2,1,0:T(2,128)S(1)}, u32[]{:S(2)}) copy-start(f32[2,36,2,512]{3,2,1,0:T(2,128)S(1)} %collective-permute-done.refs_7_) | copy-start | bytes 884740
  33.7 38.5 %collective-permute-start.4 = (f32[2,36,8,512]{3,2,1,0:T(8,128)}, f32[2,36,8,512]{3,2,1,0:T(8,128)S(1)}, u32[]{:S(2)}, u32[]{:S(2)}) collective-permute-start(f32[2,36,8,512]{3,2,1,0:T(8,128)} %get-tuple-element.45), channel_id=1, source_target_pairs={{0,1},{1,0},{2,3},{3,2},{4,5},{5,4},{6,7},{7,6},{8,9},{9,8},{10,11... | collective-permute-start | bytes 3538952 | tf_op jit(solution)/shard_map/ppermute | solution.py:648
  40.0 0.7 copy-start.10
  52.6 29.9 %collective-permute-start.9 = (f32[2,36,8,512]{3,2,1,0:T(8,128)}, f32[2,36,8,512]{3,2,1,0:T(8,128)}, u32[]{:S(2)}, u32[]{:S(2)}) collective-permute-start(f32[2,36,8,512]{3,2,1,0:T(8,128)} %get-tuple-element.46), channel_id=1, source_target_pairs={{2,0},{1,3},{4,2},{3,5},{6,4},{5,7},{10,8},{9,11},{12,10},{11,13},... | collective-permute-start | bytes 3538952 | tf_op jit(solution)/shard_map/ppermute | solution.py:648
  53.9 0.7 copy-start.7
  53.9 0.8 copy-start.8
  65.9 54.9 %collective-permute-start.12 = (f32[2,36,8,512]{3,2,1,0:T(8,128)}, f32[2,36,8,512]{3,2,1,0:T(8,128)S(1)}, u32[]{:S(2)}, u32[]{:S(2)}) collective-permute-start(f32[2,36,8,512]{3,2,1,0:T(8,128)} %hold.4), channel_id=1, source_target_pairs={{0,1},{1,0},{2,3},{3,2},{4,5},{5,4},{6,7},{7,6},{8,9},{9,8},{10,11... | collective-permute-start | bytes 3538952 | tf_op jit(solution)/shard_map/ppermute | solution.py:648
  69.6 57.4 %collective-permute-start.14 = (f32[1,36,8,512]{3,2,1,0:T(8,128)}, f32[1,36,8,512]{3,2,1,0:T(8,128)}, u32[]{:S(2)}, u32[]{:S(2)}) collective-permute-start(f32[1,36,8,512]{3,2,1,0:T(8,128)} %get-tuple-element.51), channel_id=1, source_target_pairs={{2,1},{1,0},{4,5},{3,2},{6,7},{5,6},{10,9},{9,8},{12,13},{11,10},{... | collective-permute-start | bytes 1769480 | tf_op jit(solution)/shard_map/ppermute | solution.py:648
  70.9 58.3 %collective-permute-start.16 = (f32[1,36,8,512]{3,2,1,0:T(8,128)}, f32[1,36,8,512]{3,2,1,0:T(8,128)}, u32[]{:S(2)}, u32[]{:S(2)}) collective-permute-start(f32[1,36,8,512]{3,2,1,0:T(8,128)} %get-tuple-element.52), channel_id=1, source_target_pairs={{2,1},{1,0},{4,3},{3,4},{6,7},{5,6},{10,9},{9,8},{12,11},{11,12},{... | collective-permute-start | bytes 1769480 | tf_op jit(solution)/shard_map/ppermute | solution.py:648
  72.2 1.0 copy-start
  73.3 51.9 %collective-permute-start.5 = (f32[2,32,512]{2,1,0:T(8,128)}, f32[2,32,512]{2,1,0:T(8,128)}, u32[]{:S(2)}, u32[]{:S(2)}) collective-permute-start(f32[2,32,512]{2,1,0:T(8,128)} %hold.3), channel_id=1, source_target_pairs={{0,1},{1,0},{2,3},{3,2},{4,5},{5,4},{6,7},{7,6},{8,9},{9,8},{10,11... | collective-permute-start | bytes 393224 | tf_op jit(solution)/shard_map/ppermute | solution.py:537
  82.5 67.7 %collective-permute-start.18 = (f32[2,36,8,512]{3,2,1,0:T(8,128)}, f32[2,36,8,512]{3,2,1,0:T(8,128)S(1)}, u32[]{:S(2)}, u32[]{:S(2)}) collective-permute-start(f32[2,36,8,512]{3,2,1,0:T(8,128)} %collective-permute-done.11.refs_1_), channel_id=1, source_target_pairs={{3,1},{0,2},{5,3},{2,4},{7,5},{4,6},{11,9},{8,10},{13,11},{10,12},... | collective-permute-start | bytes 3538952 | tf_op jit(solution)/shard_map/ppermute | solution.py:648
  120.8 4.4 %copy-start.1 = (f32[2,36,8,512]{3,2,1,0:T(8,128)}, f32[2,36,8,512]{3,2,1,0:T(8,128)S(1)}, u32[]{:S(2)}) copy-start(f32[2,36,8,512]{3,2,1,0:T(8,128)S(1)} %collective-permute-done.12.refs_1_.refs_2_.refs_9_) | copy-start | bytes 3538948
  120.8 59.6 %collective-permute-start.10 = (f32[2,36,8,512]{3,2,1,0:T(8,128)}, f32[2,36,8,512]{3,2,1,0:T(8,128)S(1)}, u32[]{:S(2)}, u32[]{:S(2)}) collective-permute-start(f32[2,36,8,512]{3,2,1,0:T(8,128)} %collective-permute-done.9), channel_id=1, source_target_pairs={{0,1},{3,2},{2,3},{5,4},{4,5},{7,6},{8,9},{11,10},{10,11},{13,12},... | collective-permute-start | bytes 3538952 | tf_op jit(solution)/shard_map/ppermute | solution.py:648
  125.2 55.2 %collective-permute-start.13 = (f32[2,36,8,512]{3,2,1,0:T(8,128)}, f32[2,36,8,512]{3,2,1,0:T(8,128)S(1)}, u32[]{:S(2)}, u32[]{:S(2)}) collective-permute-start(f32[2,36,8,512]{3,2,1,0:T(8,128)} %hold.5), channel_id=1, source_target_pairs={{0,1},{1,0},{2,3},{3,2},{4,5},{5,4},{6,7},{7,6},{8,9},{9,8},{10,11... | collective-permute-start | bytes 3538952 | tf_op jit(solution)/shard_map/ppermute | solution.py:648
  127.1 8.3 %collective-permute-start.8 = (f32[2,32,512]{2,1,0:T(8,128)S(1)}, f32[2,32,512]{2,1,0:T(8,128)S(1)}, u32[]{:S(2)}, u32[]{:S(2)}) collective-permute-start(f32[2,32,512]{2,1,0:T(8,128)S(1)} %add.17), channel_id=1, source_target_pairs={{0,6},{1,7},{2,4},{3,5},{4,2},{5,3},{6,0},{7,1},{8,14},{9,15},{10,... | collective-permute-start | bytes 393224 | tf_op jit(solution)/shard_map/ppermute | solution.py:538
  129.3 11.5 %collective-permute-start.7 = (f32[2,32,512]{2,1,0:T(8,128)S(1)}, f32[2,32,512]{2,1,0:T(8,128)S(1)}, u32[]{:S(2)}, u32[]{:S(2)}) collective-permute-start(f32[2,32,512]{2,1,0:T(8,128)S(1)} %add.17), channel_id=1, source_target_pairs={{0,4},{1,5},{2,6},{3,7},{4,0},{5,1},{6,2},{7,3},{8,12},{9,13},{10,... | collective-permute-start | bytes 393224 | tf_op jit(solution)/shard_map/ppermute | solution.py:538
  135.4 7.6 %collective-permute-start.6 = (f32[2,32,512]{2,1,0:T(8,128)S(1)}, f32[2,32,512]{2,1,0:T(8,128)S(1)}, u32[]{:S(2)}, u32[]{:S(2)}) collective-permute-start(f32[2,32,512]{2,1,0:T(8,128)S(1)} %add.17), channel_id=1, source_target_pairs={{0,2},{1,3},{2,0},{3,1},{4,6},{5,7},{6,4},{7,5},{8,10},{9,11},{10,... | collective-permute-start | bytes 393224 | tf_op jit(solution)/shard_map/ppermute | solution.py:538
  140.8 21.4 %collective-permute-start.15 = (f32[1,36,8,512]{3,2,1,0:T(8,128)}, f32[1,36,8,512]{3,2,1,0:T(8,128)S(1)}, u32[]{:S(2)}, u32[]{:S(2)}) collective-permute-start(f32[1,36,8,512]{3,2,1,0:T(8,128)} %collective-permute-done.14), channel_id=1, source_target_pairs={{1,1},{0,2},{5,3},{2,4},{7,5},{6,6},{9,9},{8,10},{13,11},{10,12},{... | collective-permute-start | bytes 1769480 | tf_op jit(solution)/shard_map/ppermute | solution.py:648
  143.0 25.1 %collective-permute-start.17 = (f32[1,36,8,512]{3,2,1,0:T(8,128)}, f32[1,36,8,512]{3,2,1,0:T(8,128)S(1)}, u32[]{:S(2)}, u32[]{:S(2)}) collective-permute-start(f32[1,36,8,512]{3,2,1,0:T(8,128)} %collective-permute-done.16), channel_id=1, source_target_pairs={{1,1},{0,2},{3,3},{4,4},{7,5},{6,6},{9,9},{8,10},{11,11},{12,12},{... | collective-permute-start | bytes 1769480 | tf_op jit(solution)/shard_map/ppermute | solution.py:648
  150.3 1.0 copy-start.2
  162.2 5.9 %copy-start.5 = (f32[1,36,8,512]{3,2,1,0:T(8,128)}, f32[1,36,8,512]{3,2,1,0:T(8,128)S(1)}, u32[]{:S(2)}) copy-start(f32[1,36,8,512]{3,2,1,0:T(8,128)S(1)} %collective-permute-done.15.refs_0_.refs_5_) | copy-start | bytes 1769476
  168.1 0.8 copy-start.6
  180.4 1.1 copy-start.3
  180.4 1.5 copy-start.4

commit v4 on v3

--- a/solution.py
+++ b/solution.py
@@ -30,6 +30,7 @@
 DELTA_UNROLL = 4
 SOURCE_UNROLL = 4
 SOURCE_LANES = 256
+SPARE = 4
 COST = pl.CostEstimate(flops=1024, bytes_accessed=1024, transcendentals=0)
 
 
@@ -124,15 +125,6 @@
     return -down, 1.0 - centre + down, centre - far, far
 
 
-def row_shift(before, cells, after, shift, row_ids):
-    if shift > 0:
-        return jnp.where(row_ids < shift, pltpu.roll(before, shift, 0), pltpu.roll(cells, shift, 0))
-    count = cells.shape[0]
-    return jnp.where(
-        row_ids >= count + shift, pltpu.roll(after, count + shift, 0), pltpu.roll(cells, count + shift, 0)
-    )
-
-
 def lane_shift(pieces, shift, lane_ids):
     rolled = [pltpu.roll(piece, shift % LANES, 1) for piece in pieces]
     zero = jnp.zeros_like(pieces[0])
@@ -147,56 +139,37 @@
     return moved
 
 
-def exact_dot(cells, chooser, split_ref):
-    count = cells.shape[0]
-    split_store(cells, split_ref)
-    product = jnp.dot(split_ref[...], chooser, preferred_element_type=jnp.float32)
-    return product[0:count] + product[count : 2 * count] + product[2 * count : 3 * count]
-
-
 def split_store(cells, split_ref):
     count = cells.shape[0]
     high = cells.astype(jnp.bfloat16)
     rest = cells - high.astype(jnp.float32)
     mid = rest.astype(jnp.bfloat16)
-    low = (rest - mid.astype(jnp.float32)).astype(jnp.bfloat16)
     split_ref[0:count, :] = high
     split_ref[count : 2 * count, :] = mid
-    split_ref[2 * count : 3 * count, :] = low
 
 
 def local_band(index, flip, local_bands):
     return index + flip * (local_bands - 1 - 2 * index)
 
 
-def propagate_kernel(strips, spill_slot, dests, split, edge, chained, group, dir_count, local_bands, *refs):
-    refs = list(refs)
-    meta_ref, tab_ref, spec_ref, land_ref, sx_ref, sy_ref = refs[:6]
-    refs = refs[6:]
-    prior_ref = None
-    if chained:
-        prior_ref = refs[0]
-        refs = refs[1:]
-    lower_ref = upper_ref = spill_ref = None
-    if edge:
-        lower_ref, upper_ref, spill_ref = refs[:3]
-        refs = refs[3:]
-    choosers = refs[: len(dests)]
-    refs = refs[len(dests) :]
-    out_refs = refs[: len(strips)]
-    refs = refs[len(strips) :]
-    send_count = sum(2 if two else 1 for two in split)
-    send_refs = refs[:send_count]
-    refs = refs[send_count:]
-    sum_ref = refs[0]
-    refs = refs[1:]
-    head_ref = tail_ref = None
-    if not edge:
-        head_ref, tail_ref = refs[:2]
-        refs = refs[2:]
-    turn_ref, moved_ref, split_ref = refs
+def take(refs, count):
+    return refs[:count], refs[count:]
+
+
+def propagate_kernel(strips, dests, sends, spills, edge, chained, rims, group, size, dir_count, local_bands, *refs):
+    (meta_ref, tab_ref, spec_ref, land_ref, sx_ref, sy_ref), refs = take(list(refs), 6)
+    prior_refs, refs = take(refs, chained)
+    rim_refs, refs = take(refs, 2 if edge or rims else 0)
+    spill_refs, refs = take(refs, len(spills))
+    choosers, refs = take(refs, len(dests))
+    out_refs, refs = take(refs, len(strips))
+    send_refs, refs = take(refs, len(sends))
+    (sum_ref,), refs = take(refs, 1)
+    edge_refs, refs = take(refs, 0 if edge else 2)
+    turn_ref, moved_ref, split_ref, wet_ref = refs
 
     row_count, cols = land_ref.shape
+    strip_count = row_count // STRIP
     step = pl.program_id(0)
     band = meta_ref[0] * local_bands + local_band(group + step, meta_ref[1], local_bands)
     growth = tab_ref[6 * dir_count + band]
@@ -207,12 +180,13 @@
     row_ids = lax.broadcasted_iota(jnp.int32, (STRIP, cols), 0)
     lane_ids = lax.broadcasted_iota(jnp.int32, (STRIP, LANES), 1)
 
-    def wet(s):
-        return land_ref[STRIP * s : STRIP * (s + 1), :].astype(jnp.float32)
-
     @pl.when(step == 0)
     def _():
-        sum_ref[...] = prior_ref[...] if chained else jnp.zeros_like(sum_ref)
+        sum_ref[...] = prior_refs[0][...] if chained else jnp.zeros_like(sum_ref)
+        wet_ref[...] = land_ref[...].astype(jnp.float32)
+        if rims:
+            for edge_ref, rim_ref in zip(edge_refs, rim_refs):
+                edge_ref[...] = rim_ref[...]
 
         @pl.loop(0, dir_count)
         def _(f):
@@ -222,43 +196,53 @@
                 rows = slice(STRIP * s, STRIP * (s + 1))
                 turn_ref[slot, f] = face_sin * sx_ref[rows, :] - face_cos * sy_ref[rows, :]
 
-    if not edge:
-        wet_head = land_ref[0:2, :].astype(jnp.float32)
-        wet_tail = land_ref[row_count - 2 : row_count, :].astype(jnp.float32)
-
     for first, last, cos_up, sin_up in sign_runs(dir_count):
 
         @unrolled(first, last, ROW_UNROLL)
         def _(j):
             row_taps = taps(courant * tab_ref[j])
             col_taps = taps(courant * tab_ref[dir_count + j])
+            known = {}
+
+            def wet(s):
+                return wet_ref[STRIP * s : STRIP * (s + 1), :]
+
+            def cells(s):
+                if s not in known:
+                    if s < 0:
+                        blank = jnp.zeros((STRIP - 2, cols), jnp.float32)
+                        known[s] = jnp.concatenate([blank, rim_refs[0][0, j]], axis=0)
+                    elif s == strip_count:
+                        blank = jnp.zeros((STRIP - 2, cols), jnp.float32)
+                        known[s] = jnp.concatenate([rim_refs[1][0, j], blank], axis=0)
+                    else:
+                        known[s] = spec_ref[0, j, STRIP * s : STRIP * (s + 1), :] * wet(s)
+                return known[s]
+
+            def rolled(s, shift):
+                if (s, shift) not in known:
+                    known[s, shift] = pltpu.roll(cells(s), shift % STRIP, 0)
+                return known[s, shift]
+
+            def row_shift(s, shift):
+                other = rolled(s - 1 if shift > 0 else s + 1, shift)
+                outside = row_ids < shift if shift > 0 else row_ids >= STRIP + shift
+                return jnp.where(outside, other, rolled(s, shift))
+
             if not edge:
-                head_ref[0, j] = spec_ref[0, j, 0:2, :] * wet_head
-                tail_ref[0, j] = spec_ref[0, j, row_count - 2 : row_count, :] * wet_tail
+                edge_refs[0][group + step, j] = cells(0)[0:2]
+                edge_refs[1][group + step, j] = cells(strip_count - 1)[STRIP - 2 :]
             for slot, s in enumerate(strips):
                 wet_s = wet(s)
-                cells = spec_ref[0, j, STRIP * s : STRIP * (s + 1), :] * wet_s
-                if s == 0:
-                    before = jnp.concatenate(
-                        [jnp.zeros((STRIP - 2, cols), jnp.float32), lower_ref[0, j]], axis=0
-                    )
-                else:
-                    before = spec_ref[0, j, STRIP * (s - 1) : STRIP * s, :] * wet(s - 1)
-                if STRIP * (s + 1) == row_count:
-                    after = jnp.concatenate(
-                        [upper_ref[0, j], jnp.zeros((STRIP - 2, cols), jnp.float32)], axis=0
-                    )
-                else:
-                    after = spec_ref[0, j, STRIP * (s + 1) : STRIP * (s + 2), :] * wet(s + 1)
                 way = 1 if cos_up else -1
-                cells = (
-                    row_taps[1] * cells
-                    + row_taps[0] * row_shift(before, cells, after, -way, row_ids)
-                    + row_taps[2] * row_shift(before, cells, after, way, row_ids)
-                    + row_taps[3] * row_shift(before, cells, after, 2 * way, row_ids)
+                moved = (
+                    row_taps[1] * cells(s)
+                    + row_taps[0] * row_shift(s, -way)
+                    + row_taps[2] * row_shift(s, way)
+                    + row_taps[3] * row_shift(s, 2 * way)
                 ) * wet_s
                 way = 1 if sin_up else -1
-                pieces = [cells[:, LANES * c : LANES * (c + 1)] for c in range(cols // LANES)]
+                pieces = [moved[:, LANES * c : LANES * (c + 1)] for c in range(cols // LANES)]
                 down = lane_shift(pieces, -way, lane_ids)
                 upwind = lane_shift(pieces, way, lane_ids)
                 far = lane_shift(pieces, 2 * way, lane_ids)
@@ -306,27 +290,34 @@
         sum_ref[0, rows, :] += weight * total
         sum_ref[1, rows, :] += (SPACING * 2.0 * math.pi / dir_count) * total
 
-    source = spill_ref if edge else out_refs[spill_slot]
-    spill = source[0].reshape(dir_count * STRIP, cols)
-    for chooser, dest, two in zip(choosers, dests, split):
-        filled = exact_dot(spill, chooser[...], split_ref).reshape(dir_count, STRIP, cols)
-        if two:
-            for index in range(2):
-
-                @pl.when(step == index)
-                def _():
-                    send_refs[index][0] = out_refs[dest][0] + filled
-
-            send_refs = send_refs[2:]
-        else:
-            send_refs[0][0] = out_refs[dest][0] + filled
-            send_refs = send_refs[1:]
-
-
-def propagate(strips, spill_slot, dests, split, edge, group, size, meta, table, spectrum, land_sea, slope_x, slope_y, prior, extra, choosers):
+    count = dir_count * STRIP
+    if spills:
+        for (low, high), spill_ref in zip(spills, spill_refs):
+
+            @pl.when(jnp.logical_and(step >= low, step < high))
+            def _():
+                split_store(spill_ref[0].reshape(count, cols), split_ref)
+
+    else:
+        split_store(out_refs[-1][0].reshape(count, cols), split_ref)
+    filled = []
+    for chooser, dest in zip(choosers, dests):
+        product = jnp.dot(split_ref[...], chooser[...], preferred_element_type=jnp.float32)
+        product = product[0:count] + product[count : 2 * count]
+        filled.append(out_refs[dest][0] + product.reshape(dir_count, STRIP, cols))
+    for (places, low, length, _), send_ref in zip(sends, send_refs):
+
+        @pl.when(jnp.logical_and(step >= low, step < low + length))
+        def _():
+            for index, place in enumerate(places):
+                start = (index * length + step - low) * dir_count
+                send_ref[pl.ds(start, dir_count)] = filled[place]
+
+
+def propagate(strips, dests, sends, edge, group, size, meta, table, spectrum, land_sea, slope_x, slope_y, prior, rims, spills, choosers):
     local_bands, dir_count, row_count, cols = spectrum.shape
     whole = lambda shape: pl.BlockSpec(shape, lambda b, meta: (0,) * len(shape))
-    one = lambda rows: pl.BlockSpec((1, dir_count, rows, cols), lambda b, meta: (b, 0, 0, 0))
+    clip = lambda b, low, length: jnp.clip(b - low, 0, length - 1)
     flat = whole((row_count, cols))
     in_specs = [pl.BlockSpec(memory_space=pltpu.SMEM)]
     in_specs += [
@@ -339,25 +330,43 @@
     sums = (2, row_count, cols)
     in_specs += [whole(sums)] * len(prior)
     if edge:
-        in_specs += [one(2), one(2), one(STRIP)]
+        in_specs += [pl.BlockSpec((1, dir_count, 2, cols), lambda b, meta: (b, 0, 0, 0))] * 2
+    else:
+        in_specs += [whole(rim.shape) for rim in rims]
+    for _, low, high in spills:
+        in_specs.append(
+            pl.BlockSpec(
+                (1, dir_count, STRIP, cols), lambda b, meta, low=low, high=high: (clip(b, low, high - low), 0, 0, 0)
+            )
+        )
     in_specs += [whole((cols, cols))] * len(choosers)
-    band_array = lambda rows: jax.ShapeDtypeStruct((size, dir_count, rows, cols), jnp.float32)
-    out_shape = [band_array(STRIP)] * len(strips)
-    out_specs = [one(STRIP)] * len(strips)
-    for two in split:
-        if two:
-            out_shape += [jax.ShapeDtypeStruct((1, dir_count, STRIP, cols), jnp.float32)] * 2
-            out_specs += [whole((1, dir_count, STRIP, cols))] * 2
-        else:
-            out_shape.append(band_array(STRIP))
-            out_specs.append(one(STRIP))
-    out_shape.append(jax.ShapeDtypeStruct(sums, jnp.float32))
+    shape = lambda *dims: jax.ShapeDtypeStruct(dims, jnp.float32)
+    out_shape = [shape(size, dir_count, STRIP, cols)] * len(strips)
+    out_specs = [pl.BlockSpec((1, dir_count, STRIP, cols), lambda b, meta: (b, 0, 0, 0))] * len(strips)
+    for places, low, length, room in sends:
+        block = (len(places) * length * dir_count + room, STRIP, cols)
+        out_shape.append(shape(*block))
+        out_specs.append(whole(block))
+    out_shape.append(shape(*sums))
     out_specs.append(whole(sums))
     if not edge:
-        out_shape += [band_array(2)] * 2
-        out_specs += [one(2)] * 2
+        out_shape += [shape(local_bands, dir_count, 2, cols)] * 2
+        out_specs += [whole((local_bands, dir_count, 2, cols))] * 2
     return pl.pallas_call(
-        functools.partial(propagate_kernel, strips, spill_slot, dests, split, edge, len(prior) > 0, group, dir_count, local_bands),
+        functools.partial(
+            propagate_kernel,
+            strips,
+            dests,
+            sends,
+            [(low, high) for _, low, high in spills],
+            edge,
+            len(prior),
+            not edge and len(rims) > 0,
+            group,
+            size,
+            dir_count,
+            local_bands,
+        ),
         grid_spec=pltpu.PrefetchScalarGridSpec(
             num_scalar_prefetch=1,
             grid=(size,),
@@ -366,14 +375,15 @@
             scratch_shapes=[
                 pltpu.VMEM((len(strips), dir_count, STRIP, cols), jnp.float32),
                 pltpu.VMEM((len(strips), dir_count + 4, STRIP, cols), jnp.float32),
-                pltpu.VMEM((3 * dir_count * STRIP, cols), jnp.bfloat16),
+                pltpu.VMEM((2 * dir_count * STRIP, cols), jnp.bfloat16),
+                pltpu.VMEM((row_count, cols), jnp.float32),
             ],
         ),
         out_shape=out_shape,
         compiler_params=pltpu.CompilerParams(vmem_limit_bytes=VMEM_BYTES),
         cost_estimate=COST,
         name="propagate_edge" if edge else "propagate_inner",
-    )(meta, table, spectrum, land_sea, slope_x, slope_y, *prior, *extra, *choosers)
+    )(meta, table, spectrum, land_sea, slope_x, slope_y, *prior, *rims, *[spill[0] for spill in spills], *choosers)
 
 
 def unpack_kernel(places, has_total, *refs):
@@ -385,10 +395,10 @@
 
         @pl.when(pl.program_id(0) == slot)
         def _():
-            split_store(refs[place][0].reshape(count, cols), split_ref)
+            split_store(refs[place][...].reshape(count, cols), split_ref)
 
     product = jnp.dot(split_ref[...], chooser_ref[...], preferred_element_type=jnp.float32)
-    cells = product[0:count] + product[count : 2 * count] + product[2 * count : 3 * count]
+    cells = product[0:count] + product[count : 2 * count]
     cells = cells.reshape(dir_count, rows, cols)
     out_ref[0] = cells + total_ref[0] if has_total else cells
 
@@ -409,15 +419,19 @@
     return index
 
 
-def unpack(halo, chooser, total, after):
+def flat_bands(array):
+    return array.reshape((-1,) + array.shape[-2:])
+
+
+def unpack(halo, dir_count, chooser, total, after):
     arrays = distinct(halo)
     places = [next(i for i, a in enumerate(arrays) if a is array) for array, _ in halo]
-    _, dir_count, rows, cols = arrays[0].shape
+    rows, cols = arrays[0].shape[-2:]
     block = (1, dir_count, rows, cols)
     in_specs = []
     for i in range(len(arrays)):
         index = slot_map([place == i for place in places], [slot for _, slot in halo])
-        in_specs.append(pl.BlockSpec(block, lambda b, index=index: (index(b), 0, 0, 0)))
+        in_specs.append(pl.BlockSpec(block[1:], lambda b, index=index: (index(b), 0, 0)))
     one = pl.BlockSpec(block, lambda b: (b, 0, 0, 0))
     in_specs.append(pl.BlockSpec(chooser.shape, lambda b: (0, 0)))
     extra = [] if total is None else [total]
@@ -429,11 +443,11 @@
         in_specs=in_specs,
         out_specs=one,
         out_shape=jax.ShapeDtypeStruct((len(halo),) + block[1:], jnp.float32),
-        scratch_shapes=[pltpu.VMEM((3 * dir_count * rows, cols), jnp.bfloat16)],
+        scratch_shapes=[pltpu.VMEM((2 * dir_count * rows, cols), jnp.bfloat16)],
         compiler_params=pltpu.CompilerParams(vmem_limit_bytes=VMEM_BYTES),
         cost_estimate=COST,
         name="unpack",
-    )(*arrays, chooser, *extra, after)
+    )(*[flat_bands(array) for array in arrays], chooser, *extra, after)
 
 
 def distinct(halo):
@@ -445,16 +459,17 @@
 
 
 def source_kernel(dir_count, local_bands, places, *refs):
-    meta_ref, tab_ref, land_ref, wind_ref, sum_ref = refs[:5]
-    refs = refs[5:]
-    out_ref, delta_ref = refs[-2:]
-    bands = [(refs[place], slot) for place, slot in places]
-    flip = meta_ref[1]
+    bands = [(refs[5 + place], slot) for place, slot in places]
 
     def density(index, j):
         ref, slot = bands[index + 2]
-        return ref[slot, j]
-
+        return ref[slot * dir_count + j]
+
+    source_body(dir_count, local_bands, density, *refs[:5], *refs[-2:])
+
+
+def source_body(dir_count, local_bands, density, meta_ref, tab_ref, land_ref, wind_ref, sum_ref, out_ref, delta_ref):
+    flip = meta_ref[1]
     energy = sum_ref[0] + EPSILON
     first_sum = sum_ref[1]
     mean_sigma = energy / (first_sum + EPSILON)
@@ -497,19 +512,155 @@
             out_ref[homes[index], j] = density(index, j) * gain * keeps[index] + quad * quad_scale
 
 
+def spans_of(bands):
+    arrays = distinct(bands)
+    spans = []
+    for array in arrays:
+        slots = [slot for other, slot in bands if other is array]
+        low, count = min(slots), max(slots) - min(slots) + 1
+        spans.append((low // count, count) if low % count == 0 else (0, max(slots) + 1))
+    places = []
+    for array, slot in bands:
+        index = next(i for i, a in enumerate(arrays) if a is array)
+        places.append((index, slot - spans[index][0] * spans[index][1]))
+    return arrays, spans, places
+
+
+def last_kernel(dir_count, local_bands, halves, unpack_places, band_places, counts, *refs):
+    scalar, refs = take(list(refs), 5)
+    halo_refs = []
+    for count in counts[0]:
+        found, refs = take(refs, count)
+        halo_refs.append(found)
+    (prior_ref, *choosers), refs = take(refs, 1 + len(unpack_places))
+    band_refs = []
+    for count in counts[1]:
+        found, refs = take(refs, count)
+        band_refs.append(found)
+    _, out_ref, delta_ref, split_ref, total_ref = refs
+    step = pl.program_id(0)
+    halo_count = len(unpack_places[0])
+    _, rows, cols = halo_refs[0][0].shape
+    lanes = out_ref.shape[-1]
+    count = dir_count * rows
+
+    @pl.when(step < halo_count)
+    def _():
+        total = prior_ref[...]
+        for found, places, chooser in zip(halo_refs, unpack_places, choosers):
+            for slot, place in enumerate(places):
+
+                @pl.when(step == slot)
+                def _():
+                    split_store(found[place][...].reshape(count, cols), split_ref)
+
+            product = jnp.dot(split_ref[...], chooser[...], preferred_element_type=jnp.float32)
+            total = total + (product[0:count] + product[count : 2 * count]).reshape(dir_count, rows, cols)
+        for half in range(halves):
+            total_ref[half, pl.ds(step * dir_count, dir_count)] = total[:, :, half * lanes : (half + 1) * lanes]
+
+    half = lax.rem(jnp.maximum(step - halo_count, 0), halves)
+    for turn, (found, places) in enumerate(zip(band_refs, band_places)):
+        first = halo_count + turn * halves
+
+        @pl.when(jnp.logical_and(step >= first, step < first + halves))
+        def _():
+            def density(index, j):
+                place, slot = places[index + 2]
+                if place is None:
+                    return total_ref[half, slot * dir_count + j]
+                return found[place][slot * dir_count + j]
+
+            source_body(dir_count, local_bands, density, *scalar, out_ref, delta_ref)
+
+
+def last_sources(strips, shape, meta, table, land_sea, wind, sums, halos, members, choosers, total, previous):
+    local_bands, dir_count, row_count, cols = shape
+    lanes = SOURCE_LANES if cols % SOURCE_LANES == 0 else cols
+    halves = cols // lanes
+    halo_count = len(halos[0])
+    smem = pl.BlockSpec(memory_space=pltpu.SMEM)
+
+    def turn(t):
+        return jnp.maximum(t - halo_count, 0) // halves
+
+    def strip(t):
+        place = strips[0]
+        for k in range(1, len(strips)):
+            place = place + jnp.where(turn(t) >= k, strips[k] - strips[k - 1], 0)
+        return place
+
+    def half(t):
+        return lax.rem(jnp.maximum(t - halo_count, 0), halves)
+
+    def part(t, k):
+        return jnp.clip(t - halo_count - k * halves, 0, halves - 1)
+
+    in_specs = [smem, smem]
+    in_specs.append(pl.BlockSpec((STRIP, lanes), lambda t: (strip(t), half(t))))
+    in_specs += [pl.BlockSpec((2, STRIP, lanes), lambda t: (0, strip(t), half(t)))] * 2
+    operands = [meta, table, land_sea, wind, sums]
+    block = (dir_count, STRIP, cols)
+    unpack_places, counts = [], ([], [])
+    for halo in halos:
+        arrays = distinct(halo)
+        places = [next(i for i, a in enumerate(arrays) if a is array) for array, _ in halo]
+        for i, array in enumerate(arrays):
+            index = slot_map([place == i for place in places], [slot for _, slot in halo])
+            in_specs.append(pl.BlockSpec(block, lambda t, index=index: (index(t), 0, 0)))
+            operands.append(flat_bands(array))
+        unpack_places.append(places)
+        counts[0].append(len(arrays))
+    in_specs.append(pl.BlockSpec(block, lambda t: (jnp.minimum(t, halo_count - 1), 0, 0)))
+    operands.append(flat_bands(total))
+    in_specs += [pl.BlockSpec((cols, cols), lambda t: (0, 0))] * len(choosers)
+    operands += choosers
+    band_places = []
+    for k in range(len(strips)):
+        arrays, spans, found = spans_of([entry for entry in members[k] if entry[0] is not None])
+        found = iter(found)
+        places = [(None, slot) if array is None else next(found) for array, slot in members[k]]
+        for array, (first, count) in zip(arrays, spans):
+            in_specs.append(
+                pl.BlockSpec(
+                    (count * dir_count, STRIP, lanes), lambda t, first=first, k=k: (first, 0, part(t, k))
+                )
+            )
+            operands.append(flat_bands(array))
+        band_places.append(places)
+        counts[1].append(len(arrays))
+    in_specs.append(pl.BlockSpec(memory_space=pl.ANY))
+    operands.append(previous)
+    return pl.pallas_call(
+        functools.partial(last_kernel, dir_count, local_bands, halves, unpack_places, band_places, counts),
+        grid=(halo_count + len(strips) * halves,),
+        in_specs=in_specs,
+        out_specs=pl.BlockSpec((local_bands, dir_count, STRIP, lanes), lambda t: (0, 0, strip(t), half(t))),
+        out_shape=jax.ShapeDtypeStruct(shape, jnp.float32),
+        scratch_shapes=[
+            pltpu.VMEM((local_bands + 2, dir_count, STRIP, lanes), jnp.float32),
+            pltpu.VMEM((2 * dir_count * STRIP, cols), jnp.bfloat16),
+            pltpu.VMEM((halves, halo_count * dir_count, STRIP, lanes), jnp.float32),
+        ],
+        input_output_aliases={len(operands) - 1: 0},
+        compiler_params=pltpu.CompilerParams(vmem_limit_bytes=VMEM_BYTES),
+        cost_estimate=COST,
+        name="last_sources",
+    )(*operands)
+
+
 def source(strip, shape, meta, table, land_sea, wind, sums, sum_block, bands, previous):
     local_bands, dir_count, row_count, cols = shape
     lanes = SOURCE_LANES if cols % SOURCE_LANES == 0 else cols
-    arrays = distinct(bands)
-    places = [(next(i for i, a in enumerate(arrays) if a is array), slot) for array, slot in bands]
+    arrays, spans, places = spans_of(bands)
     smem = pl.BlockSpec(memory_space=pltpu.SMEM)
-    part = lambda ref: pl.BlockSpec((ref.shape[0], dir_count, STRIP, lanes), lambda c: (0, 0, 0, c))
+    part = lambda first, count: pl.BlockSpec((count * dir_count, STRIP, lanes), lambda c: (first, 0, c))
     in_specs = [smem, smem]
     in_specs.append(pl.BlockSpec((STRIP, lanes), lambda c: (strip, c)))
     in_specs.append(pl.BlockSpec((2, STRIP, lanes), lambda c: (0, strip, c)))
     in_specs.append(pl.BlockSpec((2, STRIP, lanes), lambda c: (0, sum_block, c)))
-    in_specs += [part(ref) for ref in arrays]
-    operands = [meta, table, land_sea, wind, sums, *arrays]
+    in_specs += [part(*span) for span in spans]
+    operands = [meta, table, land_sea, wind, sums, *[flat_bands(array) for array in arrays]]
     aliases = {}
     if previous is not None:
         in_specs.append(pl.BlockSpec(memory_space=pl.ANY))
@@ -533,10 +684,6 @@
     count = lax.axis_size("spec")
     if count & (count - 1):
         return lax.psum(value, "spec")
-    if count == 8:
-        value = value + lax.ppermute(value, "spec", [(i, i ^ 1) for i in range(count)])
-        others = [lax.ppermute(value, "spec", [(i, i ^ k) for i in range(count)]) for k in (2, 4, 6)]
-        return (value + others[0]) + (others[1] + others[2])
     reach = 1
     while reach < count:
         value = value + lax.ppermute(value, "spec", [(i, i ^ reach) for i in range(count)])
@@ -550,11 +697,11 @@
         for source, goal in ((low + 1, low), (low, low + 1)):
             rank = low if source > goal else count - 2 - low
             if first_across(rank):
-                first.append((source, source ^ 1))
-                second.append((source ^ 1, goal))
+                middle = source ^ 1
             else:
-                first.append((source, goal))
-                second.append((goal, goal))
+                middle = goal if rank == 1 else goal ^ 1
+            first.append((source, middle))
+            second.append((middle, goal))
     return first, second
 
 
@@ -590,49 +737,43 @@
     kept = (1, 0, 3)
     size = min(2, local_bands)
     groups = list(range(0, local_bands, size))
-    paired = local_bands == 4 and spec_count % 2 == 0
+    paired = local_bands == 4 and spec_count == 8
     meta = jnp.stack([pos, pos % 2 if paired else 0 * pos])
-    choose = plan(land_sea, kept, spill, (0,), False)
+    choose = list(plan(land_sea, kept, spill, (0,), False))
 
     args = (meta, table, spectrum, land_sea, slope_x, slope_y)
-    bands = {s: [] for s in range(4)}
-    sends = {s: [] for s in kept}
-    rims, prior = [], []
-    for group in groups:
+    bands, sends, prior, rims, spills = {1: [], 2: []}, {}, [], [], []
+    for group in groups[::-1]:
         strip_a, strip_b, send, sums, head, tail = propagate(
-            inner, 1, (0,), (False,), False, group, size, *args, prior, (), choose[:1]
+            inner, (0,), [((0,), 0, size, 0)], False, group, size, *args, prior, rims, [], choose[:1]
         )
-        bands[1].append(strip_a)
-        bands[2].append(strip_b)
-        sends[1].append([send])
-        rims.append((head, tail))
-        prior = [sums]
-    choose = list(choose) + list(plan(land_sea, kept, spill, (1, 2), False))
+        bands[1] = [(strip_a, i) for i in range(size)] + bands[1]
+        bands[2] = [(strip_b, i) for i in range(size)] + bands[2]
+        spills = [(strip_b, group, group + size)] + spills
+        sends[1, group] = send
+        prior, rims = [sums], [head, tail]
     ups = [(i, i + 1) for i in range(geo_count - 1)]
     downs = [(i + 1, i) for i in range(geo_count - 1)]
-    for index, group in enumerate(groups):
-        head, tail = rims[index]
-        lower = lax.ppermute(tail, "geo", ups)
-        upper = lax.ppermute(head, "geo", downs)
-        split = paired and index == 0
-        strip_a, strip_b, *send, sums = propagate(
-            outer, None, (0, 1), (split, False), True, group, size, *args, prior, (lower, upper, bands[2][index]), choose[1:]
-        )
-        bands[0].append(strip_a)
-        bands[3].append(strip_b)
-        sends[0].append(send[:-1])
-        sends[3].append(send[-1:])
-        prior = [sums]
-    sums = prior[0]
+    rims = [lax.ppermute(tail, "geo", ups), lax.ppermute(head, "geo", downs)]
+    choose += plan(land_sea, kept, spill, (1, 2), False)
+    first, final = groups[0], groups[-1]
+    if paired:
+        outgoing = [((0,), 0, 1, SPARE), ((0,), 1, 1, SPARE), ((1,), 0, 2, 0), ((0, 1), 2, 2, 0)]
+    else:
+        outgoing = [((place,), group, size, 0) for group in sorted({first, final}) for place in (0, 1)]
+    strip_a, strip_b, *outer_sends, sums = propagate(
+        outer, (0, 1), outgoing, True, 0, local_bands, *args, prior, rims, spills, choose[1:]
+    )
+    bands[0] = [(strip_a, i) for i in range(local_bands)]
+    bands[3] = [(strip_b, i) for i in range(local_bands)]
     scale = (28.0 * USTAR_RATIO / GRAVITY) * wind_speed
     wind = jnp.stack([scale * jnp.cos(wind_dir), scale * jnp.sin(wind_dir)])
     back = dict(zip(kept, plan(land_sea, kept, spill, (0, 1, 2), True)))
 
-    def finish(s, halo, result, total):
-        if s != spill:
-            total = unpack(halo, back[s], total, sums if result is None else result)
-        own = [(array, i) for array in bands[s] for i in range(size)]
-        members = halo[:2] + own + halo[2:]
+    def finish(s, halo, result, total, unpacked=False):
+        if s != spill and not unpacked:
+            total = unpack(halo, dir_count, back[s], total, land_sea if result is None else result)
+        members = halo[:2] + bands[s] + halo[2:]
         result = source(s, spectrum.shape, meta, table, land_sea, wind, sums, s, members, result)
         return result, total
 
@@ -647,22 +788,34 @@
         def send(value, pairs):
             return lax.ppermute(value, "spec", pairs)
 
-        def members(far, near):
-            return [(far[-1], far[-1].shape[0] - 1), (far[0], 0), (near, 1), (near, 0)]
-
-        far_1 = send(sends[1][0][0], across[0])
-        near_1 = send(sends[1][1][0], partner)
-        sums = spec_total(hold(sums, near_1))
-        near_0 = send(hold(sends[0][1][0], far_1), partner)
-        far_3 = send(sends[3][0][0], along[0])
-        far_0 = [send(value, pairs[0]) for value, pairs in zip(sends[0][0], (some, most))]
+        def members(far, near, slot):
+            return [(far[-1], 2 - len(far)), (far[0], 0), (near, slot + 1), (near, slot)]
+
+        near_1 = send(sends[1, final], partner)
+        far_1 = send(sends[1, first], across[0])
+        sums = sums + send(hold(sums, near_1), partner)
+        near = send(hold(outer_sends[3], near_1), partner)
+        others = [send(sums, [(i, i ^ k) for i in range(spec_count)]) for k in (2, 4, 6)]
+        sums = (sums + others[0]) + (others[1] + others[2])
+        far_3 = send(hold(outer_sends[2], sums), along[0])
+        far_0 = [send(value, pairs[0]) for value, pairs in zip(outer_sends[:2], (some, most))]
         far_1 = send(far_1, across[1])
-        far_3 = send(far_3, along[1])
-        far_0 = [send(value, pairs[1]) for value, pairs in zip(far_0, (some, most))]
-        near_3 = send(hold(sends[3][1][0], near_0), partner)
-        result, total = finish(1, members([far_1], near_1), result, total)
-        result, total = finish(0, members(far_0, near_0), result, total)
-        result, total = finish(3, members([far_3], near_3), result, total)
+        far_3 = send(hold(far_3, far_1), along[1])
+        halo = members([far_1], near_1, 0)
+        total_far = unpack(halo[:2], dir_count, back[1], None, land_sea)
+        total_near = unpack(halo[2:], dir_count, back[1], None, land_sea)
+        result, _ = finish(1, halo, None, None, True)
+        far_0 = [send(hold(value, result, total_far, total_near), pairs[1]) for value, pairs in zip(far_0, (some, most))]
+        halo = {0: members(far_0, near, 0), 3: members([far_3], near, 2)}
+        for s in (0, 3):
+            total_near = unpack(halo[s][2:], dir_count, back[s], total_near, result)
+        result, _ = finish(0, halo[0], result, None, True)
+        parts = [halo[3][:2] + bands[3] + halo[3][2:]]
+        parts.append([(None, 0), (None, 1)] + bands[spill] + [(total_near, 0), (total_near, 1)])
+        unpacks, choosers = [halo[0][:2], halo[3][:2]], [back[0], back[3]]
+        return last_sources(
+            (3, spill), spectrum.shape, meta, table, land_sea, wind, sums, unpacks, parts, choosers, total_far, result
+        )
     else:
 
         def hop(value, count):
@@ -670,13 +823,16 @@
             return lax.ppermute(value, "spec", pairs)
 
         sums = spec_total(sums)
+        places = [(group, place) for group in sorted({first, final}) for place in (0, 1)]
+        for (group, place), array in zip(places, outer_sends):
+            sends[kept[place + 1], group] = array
         for s in kept:
-            first, last = sends[s][0][0], sends[s][-1][0]
+            low, high = sends[s, first], sends[s, final]
             if size == 2:
-                lower, upper = hop(last, 1), hop(first, -1)
+                lower, upper = hop(high, 1), hop(low, -1)
                 halo = [(lower, 0), (lower, 1), (upper, 0), (upper, 1)]
             else:
-                halo = [(hop(last, 2), 0), (hop(last, 1), 0), (hop(first, -1), 0), (hop(first, -2), 0)]
+                halo = [(hop(high, 2), 0), (hop(high, 1), 0), (hop(low, -1), 0), (hop(low, -2), 0)]
             result, total = finish(s, halo, result, total)
     return finish(spill, [(total, i) for i in range(4)], result, total)[0]
 

time: 199 us -> 196 us (0.985); the launches traced: 198 us -> 193 us
  starting transfers between devices: 39.4 us -> 30.1 us
  waiting for transfers between devices: 59.8 us -> 66.8 us
  Pallas kernels: 88.8 us -> 84.2 us
    ppermute x11 -> x14, waiting for transfers between devices: 47.6 us -> 65 us  [send(): return lax.ppermute(value, 'spec', pairs)]
    ppermute x8 -> x2, starting transfers between devices: 15.5 us -> 2.79 us  [shards(): rims = [lax.ppermute(tail, 'geo', ups), lax.ppermute(head, 'geo', downs)]]
    pallas_call x4, Pallas kernels: 42.5 us -> 53.3 us  [the longest x3 40.6 us: propagate(): pl.pallas_call(functools.partial(propagate_kernel, strips, dests, sends,...]
    ppermute x8 -> x2, waiting for transfers between devices: 12.1 us -> 1.77 us  [shards(): rims = [lax.ppermute(tail, 'geo', ups), lax.ppermute(head, 'geo', downs)]]
    pallas_call x4 -> x2, Pallas kernels: 19.8 us -> 9.93 us  [source(): pl.pallas_call(functools.partial(source_kernel, dir_count, local_bands, p...]
    pallas_call x3 -> x4, Pallas kernels: 18.8 us -> 13.3 us  [unpack(): pl.pallas_call(functools.partial(unpack_kernel, places, len(extra)), grid...]
    ppermute x11 -> x14, starting transfers between devices: 23.9 us -> 27.3 us  [send(): return lax.ppermute(value, 'spec', pairs)]
    unnamed x22 -> x17, local copies, waits for them, and re-layouts: 5.8 us -> 6.81 us
  transfers between devices with their start and end apart: 19 -> 16, of which waited for: 6 -> 9; matrix products, arithmetic and copies ran while one was open for 2% -> 3% of each run, Pallas kernels for 31% -> 31%
where the time goes in v4:
time: 196 us; the launch traced here: 193 us
  Pallas kernels  84.2 us (43%)
  waiting for transfers between devices  66.8 us (34%)
  starting transfers between devices  30.1 us (15%)
  local copies, waits for them, and re-layouts  6.81 us (3%)
  other arithmetic  4.86 us (2%)
    ppermute x14, waiting for transfers between devices, send(): return lax.ppermute(value, 'spec', pairs)  65 us
    pallas_call x3, Pallas kernels, propagate(): pl.pallas_call(functools.partial(propagate_kernel, strips, dests, sends,...  40.6 us
    ppermute x14, starting transfers between devices, send(): return lax.ppermute(value, 'spec', pairs)  27.3 us
    pallas_call x4, Pallas kernels, unpack(): pl.pallas_call(functools.partial(unpack_kernel, places, len(extra)), grid...  13.3 us
    pallas_call x1, Pallas kernels, last_sources(): pl.pallas_call(functools.partial(last_kernel, dir_count, local_bands, hal...  12.7 us
    pallas_call x2, Pallas kernels, source(): pl.pallas_call(functools.partial(source_kernel, dir_count, local_bands, p...  9.93 us
    pallas_call x3, Pallas kernels, plan(): pl.pallas_call(functools.partial(plan_kernel, kept, spill, wanted, back),...  7.67 us
    unnamed x17, local copies, waits for them, and re-layouts  6.81 us
  transfers between devices with their start and end apart: 16, of which 9 were waited for; matrix products, arithmetic and copies ran while one was open for 3% of the time, Pallas kernels for 31%

profile of v4, /device:TPU:0, one launch (start us, length us, event | category | flops | bytes accessed | tf_op | source)
XLA Modules:
  0.0 193.0 jit_solution(16260853657116799488)
XLA Ops:
  0.0 2.2 %plan.2.refs_6_.refs_9_ = bf16[512,512]{1,0:T(8,128)(2,1)} custom-call(s32[32,512]{1,0:T(8,128)} %refs_2_.15), custom_call_target="tpu_custom_call" | custom-call | tf_op jit(solution)/shard_map/plan/pallas_call | solution.py:112
  2.2 0.6 pad_add_fusion.refs_0_
  2.8 10.2 %propagate_inner.2 = (f32[2,36,8,512]{3,2,1,0:T(8,128)}, f32[2,36,8,512]{3,2,1,0:T(8,128)}, f32[72,8,512]{2,1,0:T(8,128)}, f32[2,32,512]{2,1,0:T(8,128)}, f32[4,...) custom-call(s32[2]{0:T(128)} %pad_add_fusion.refs_0_, f32[248]{0:T(256)} %constant.21.clone.refs_1_, ...), custom_call_target="tpu_custom_call" | custom-call | flops 1024 | bytes 1024 | tf_op jit(solution)/shard_map/propagate_inner/pallas_call | solution.py:355
  13.0 3.0 %collective-permute-start.2 = (f32[72,8,512]{2,1,0:T(8,128)}, f32[72,8,512]{2,1,0:T(8,128)S(1)}, u32[]{:S(2)}, u32[]{:S(2)}) collective-permute-start(f32[72,8,512]{2,1,0:T(8,128)} %get-tuple-element.40), channel_id=1, source_target_pairs={{0,1},{1,0},{2,3},{3,2},{4,5},{5,4},{6,7},{7,6},{8,9},{9,8},{10,11... | collective-permute-start | bytes 3538952 | tf_op jit(solution)/shard_map/ppermute | solution.py:789
  16.1 10.6 %propagate_inner.3 = (f32[2,36,8,512]{3,2,1,0:T(8,128)}, f32[2,36,8,512]{3,2,1,0:T(8,128)}, f32[72,8,512]{2,1,0:T(8,128)}, f32[2,32,512]{2,1,0:T(8,128)}, f32[4,...) custom-call(s32[2]{0:T(128)} %pad_add_fusion.refs_0_, f32[248]{0:T(256)} %constant.21.clone.refs_1_, ...), custom_call_target="tpu_custom_call" | custom-call | flops 1024 | bytes 1024 | tf_op jit(solution)/shard_map/propagate_inner/pallas_call | solution.py:355
  26.7 1.3 collective-permute-start.8
  28.0 1.5 collective-permute-start
  29.5 1.3 collective-permute-start.1
  30.8 2.6 %plan.3 = (bf16[512,512]{1,0:T(8,128)(2,1)}, bf16[512,512]{1,0:T(8,128)(2,1)}) custom-call(s32[32,512]{1,0:T(8,128)} %refs_2_.15), custom_call_target="tpu_custom_call" | custom-call | tf_op jit(solution)/shard_map/plan/pallas_call | solution.py:112
  33.4 1.8 collective-permute-done.1.refs_8_
  35.1 0.9 copy-done.6
  36.0 19.7 %propagate_edge.1 = (f32[4,36,8,512]{3,2,1,0:T(8,128)}, f32[4,36,8,512]{3,2,1,0:T(8,128)}, f32[40,8,512]{2,1,0:T(8,128)}, f32[40,8,512]{2,1,0:T(8,128)}, f32[72,...) custom-call(s32[2]{0:T(128)} %pad_add_fusion.refs_0_, f32[248]{0:T(256)} %constant.21.clone.refs_1_, ...), custom_call_target="tpu_custom_call" | custom-call | flops 1024 | bytes 1024 | tf_op jit(solution)/shard_map/propagate_edge/pallas_call | solution.py:355
  55.7 1.6 copy.16.refs_0_
  57.3 1.0 copy-done.1
  58.4 3.7 %collective-permute-start.3 = (f32[2,32,512]{2,1,0:T(8,128)}, f32[2,32,512]{2,1,0:T(8,128)S(1)}, u32[]{:S(2)}, u32[]{:S(2)}) collective-permute-start(f32[2,32,512]{2,1,0:T(8,128)} %hold.6), channel_id=1, source_target_pairs={{0,1},{1,0},{2,3},{3,2},{4,5},{5,4},{6,7},{7,6},{8,9},{9,8},{10,11... | collective-permute-start | bytes 393224 | tf_op jit(solution)/shard_map/ppermute | solution.py:789
  62.1 6.8 %collective-permute-done.3 = f32[2,32,512]{2,1,0:T(8,128)S(1)} collective-permute-done((f32[2,32,512]{2,1,0:T(8,128)}, f32[2,32,512]{2,1,0:T(8,128)S(1)}, u32[]{:S(2)}, u32[]{:S(2)}) %collective-permute-start.3) | collective-permute-done | bytes 131104 | tf_op jit(solution)/shard_map/ppermute | solution.py:789
  68.9 0.7 add.17
  69.6 3.0 %collective-permute-start.6 = (f32[2,32,512]{2,1,0:T(8,128)}, f32[2,32,512]{2,1,0:T(8,128)}, u32[]{:S(2)}, u32[]{:S(2)}) collective-permute-start(f32[2,32,512]{2,1,0:T(8,128)} %add.17), channel_id=1, source_target_pairs={{0,6},{1,7},{2,4},{3,5},{4,2},{5,3},{6,0},{7,1},{8,14},{9,15},{10,... | collective-permute-start | bytes 393224 | tf_op jit(solution)/shard_map/ppermute | solution.py:789
  72.9 1.1 collective-permute-start.4
  74.0 1.5 collective-permute-start.15
  75.5 3.4 %collective-permute-start.9 = (f32[72,8,512]{2,1,0:T(8,128)}, f32[72,8,512]{2,1,0:T(8,128)S(1)}, u32[]{:S(2)}, u32[]{:S(2)}) collective-permute-start(f32[72,8,512]{2,1,0:T(8,128)} %collective-permute-done.8), channel_id=1, source_target_pairs={{3,1},{0,2},{5,3},{2,4},{7,5},{4,6},{11,9},{8,10},{13,11},{10,12},... | collective-permute-start | bytes 3538952 | tf_op jit(solution)/shard_map/ppermute | solution.py:789
  79.0 6.3 %collective-permute-done.5 = f32[2,32,512]{2,1,0:T(8,128)} collective-permute-done((f32[2,32,512]{2,1,0:T(8,128)}, f32[2,32,512]{2,1,0:T(8,128)}, u32[]{:S(2)}, u32[]{:S(2)}) %collective-permute-start.5) | collective-permute-done | bytes 131104 | tf_op jit(solution)/shard_map/ppermute | solution.py:789
  85.2 1.8 add_add_fusion.refs_4_.refs_1_
  87.0 1.3 collective-permute-start.13
  88.3 1.3 collective-permute-start.7
  89.6 1.3 collective-permute-start.11
  90.9 14.7 %collective-permute-done.9.refs_5_.refs_0_.refs_1_ = f32[72,8,512]{2,1,0:T(8,128)S(1)} collective-permute-done((f32[72,8,512]{2,1,0:T(8,128)}, f32[72,8,512]{2,1,0:T(8,128)S(1)}, u32[]{:S(2)}, u32[]{:S(2)}) %collective-permute-start.9) | collective-permute-done | bytes 1179680 | tf_op jit(solution)/shard_map/ppermute | solution.py:789
  105.6 12.4 %collective-permute-done.13.refs_0_ = f32[72,8,512]{2,1,0:T(8,128)} collective-permute-done((f32[72,8,512]{2,1,0:T(8,128)}, f32[72,8,512]{2,1,0:T(8,128)}, u32[]{:S(2)}, u32[]{:S(2)}) %collective-permute-start.13) | collective-permute-done | bytes 1179680 | tf_op jit(solution)/shard_map/ppermute | solution.py:789
  118.0 1.4 collective-permute-start.14
  119.4 2.9 %plan_back.1 = (bf16[512,512]{1,0:T(8,128)(2,1)}, bf16[512,512]{1,0:T(8,128)(2,1)}, bf16[512,512]{1,0:T(8,128)(2,1)}) custom-call(s32[32,512]{1,0:T(8,128)} %refs_2_.15), custom_call_target="tpu_custom_call" | custom-call | tf_op jit(solution)/shard_map/plan_back/pallas_call | solution.py:112
  122.3 1.1 multiply_bitcast_fusion.1
  123.4 0.7 pad_maximum_fusion.refs_3_
  124.1 3.2 %unpack.5.refs_3_.refs_2_ = f32[2,36,8,512]{3,2,1,0:T(8,128)} custom-call(f32[72,8,512]{2,1,0:T(8,128)} %copy-done.1, bf16[512,512]{1,0:T(8,128)(2,1)} %get-tuple-element.45.refs_1_, s32[32,512]{1,0:T(8,128)} %refs_2_.15), custom_call_target="tpu_custom_call" | custom-call | flops 1024 | bytes 1024 | tf_op jit(solution)/shard_map/unpack/pallas_call | solution.py:440
  127.3 3.3 %unpack.4.refs_2_ = f32[2,36,8,512]{3,2,1,0:T(8,128)} custom-call(f32[72,8,512]{2,1,0:T(8,128)} %copy-done.2, bf16[512,512]{1,0:T(8,128)(2,1)} %get-tuple-element.45.refs_1_, s32[32,512]{1,0:T(8,128)} %refs_2_.15), custom_call_target="tpu_custom_call" | custom-call | flops 1024 | bytes 1024 | tf_op jit(solution)/shard_map/unpack/pallas_call | solution.py:440
  130.6 5.0 %source.2.refs_1_.refs_3_.refs_9_ = f32[4,36,32,512]{3,2,1,0:T(8,128)} custom-call(s32[2]{0:T(128)} %pad_add_fusion.refs_0_, f32[248]{0:T(256)} %constant.21.clone.refs_1_, s32[32,512]{1,0:T(8,128)} %refs_2_.15, f32[2,32,512]{2,1,0:T(8,128)} %pad_maximum_fusion.refs_3_, f32[2,32,512]{2,1,0:T(8,128)} %add_add_fusion.refs_4_.refs_1_, f32[72,8,512]{2,1,0:T(8,128)} %copy-done.2, ...), custom_call_target="tpu_custom_call" | custom-call | flops 1024 | bytes 1024 | tf_op jit(solution)/shard_map/source/pallas_call | solution.py:669
  135.5 5.2 %collective-permute-done.7.refs_0_ = f32[40,8,512]{2,1,0:T(8,128)} collective-permute-done((f32[40,8,512]{2,1,0:T(8,128)}, f32[40,8,512]{2,1,0:T(8,128)}, u32[]{:S(2)}, u32[]{:S(2)}) %collective-permute-start.7) | collective-permute-done | bytes 655392 | tf_op jit(solution)/shard_map/ppermute | solution.py:789
  140.7 3.2 %collective-permute-start.10 = (f32[40,8,512]{2,1,0:T(8,128)}, f32[40,8,512]{2,1,0:T(8,128)}, u32[]{:S(2)}, u32[]{:S(2)}) collective-permute-start(f32[40,8,512]{2,1,0:T(8,128)} %hold.7), channel_id=1, source_target_pairs={{1,1},{0,2},{5,3},{2,4},{7,5},{6,6},{9,9},{8,10},{13,11},{10,12},{... | collective-permute-start | bytes 1966088 | tf_op jit(solution)/shard_map/ppermute | solution.py:789
  143.9 10.8 %collective-permute-done.11.refs_0_ = f32[40,8,512]{2,1,0:T(8,128)} collective-permute-done((f32[40,8,512]{2,1,0:T(8,128)}, f32[40,8,512]{2,1,0:T(8,128)}, u32[]{:S(2)}, u32[]{:S(2)}) %collective-permute-start.11) | collective-permute-done | bytes 655392 | tf_op jit(solution)/shard_map/ppermute | solution.py:789
  154.8 1.5 collective-permute-start.12
  156.3 1.4 copy-done
  157.7 3.4 %unpack.6.refs_2_ = f32[2,36,8,512]{3,2,1,0:T(8,128)} custom-call(f32[144,8,512]{2,1,0:T(8,128)} %copy-done, bf16[512,512]{1,0:T(8,128)(2,1)} %get-tuple-element.48.refs_1_.refs_9_, f32[2,36,8,512]{3,2,1,0:T(8,128)} %unpack.5.refs_3_.refs_2_, f32[4,36,32,512]{3,2,1,0:T(8,128)} %source.2.refs_1_.refs_3_.refs_9_), custom_call_target="tpu_custom_call" | custom-call | flops 1024 | bytes 1024 | tf_op jit(solution)/shard_map/unpack/pallas_call | solution.py:440
  161.1 3.4 %unpack.7 = f32[2,36,8,512]{3,2,1,0:T(8,128)} custom-call(f32[144,8,512]{2,1,0:T(8,128)} %copy-done, bf16[512,512]{1,0:T(8,128)(2,1)} %get-tuple-element.49.refs_1_.refs_10_, f32[2,36,8,512]{3,2,1,0:T(8,128)} %unpack.6.refs_2_, f32[4,36,32,512]{3,2,1,0:T(8,128)} %source.2.refs_1_.refs_3_.refs_9_), custom_call_target="tpu_custom_call" | custom-call | flops 1024 | bytes 1024 | tf_op jit(solution)/shard_map/unpack/pallas_call | solution.py:440
  164.6 7.0 %collective-permute-done.12.refs_6_ = f32[40,8,512]{2,1,0:T(8,128)S(1)} collective-permute-done((f32[40,8,512]{2,1,0:T(8,128)}, f32[40,8,512]{2,1,0:T(8,128)S(1)}, u32[]{:S(2)}, u32[]{:S(2)}) %collective-permute-start.12) | collective-permute-done | bytes 655392 | tf_op jit(solution)/shard_map/ppermute | solution.py:789
  171.5 0.8 copy-done.4
  172.4 5.0 %source.3.refs_17_ = f32[4,36,32,512]{3,2,1,0:T(8,128)} custom-call(s32[2]{0:T(128)} %pad_add_fusion.refs_0_, f32[248]{0:T(256)} %constant.21.clone.refs_1_, s32[32,512]{1,0:T(8,128)} %refs_2_.15, f32[2,32,512]{2,1,0:T(8,128)} %pad_maximum_fusion.refs_3_, f32[2,32,512]{2,1,0:T(8,128)} %add_add_fusion.refs_4_.refs_1_, ...), custom_call_target="tpu_custom_call", output_to_operand_aliasing={{}: (9, {})} | custom-call | flops 1024 | bytes 1024 | tf_op jit(solution)/shard_map/source/pallas_call | solution.py:669
  177.3 1.8 collective-permute-done.14.refs_7_.refs_11_
  179.1 1.0 copy-done.3
  180.2 12.7 %last_sources.1 = f32[4,36,32,512]{3,2,1,0:T(8,128)} custom-call(s32[2]{0:T(128)} %pad_add_fusion.refs_0_, f32[248]{0:T(256)} %constant.21.clone.refs_1_, s32[32,512]{1,0:T(8,128)} %refs_2_.15, f32[2,32,512]{2,1,0:T(8,128)} %pad_maximum_fusion.refs_3_, f32[2,32,512]{2,1,0:T(8,128)} %add_add_fusion.refs_4_.refs_1_, ...), custom_call_target="tpu_custom_call", output_to_operand_aliasing={{}: (17, {})} | custom-call | flops 1024 | bytes 1024 | tf_op jit(solution)/shard_map/last_sources/pallas_call | solution.py:634
  (25 shorter events, 0.3 us)
Async XLA Ops:
  13.0 44.3 %collective-permute-start.2 = (f32[72,8,512]{2,1,0:T(8,128)}, f32[72,8,512]{2,1,0:T(8,128)S(1)}, u32[]{:S(2)}, u32[]{:S(2)}) collective-permute-start(f32[72,8,512]{2,1,0:T(8,128)} %get-tuple-element.40), channel_id=1, source_target_pairs={{0,1},{1,0},{2,3},{3,2},{4,5},{5,4},{6,7},{7,6},{8,9},{9,8},{10,11... | collective-permute-start | bytes 3538952 | tf_op jit(solution)/shard_map/ppermute | solution.py:789
  26.7 48.8 %collective-permute-start.8 = (f32[72,8,512]{2,1,0:T(8,128)}, f32[72,8,512]{2,1,0:T(8,128)}, u32[]{:S(2)}, u32[]{:S(2)}) collective-permute-start(f32[72,8,512]{2,1,0:T(8,128)} %get-tuple-element.42), channel_id=1, source_target_pairs={{2,3},{1,0},{4,5},{3,2},{6,7},{5,4},{10,11},{9,8},{12,13},{11,10},... | collective-permute-start | bytes 3538952 | tf_op jit(solution)/shard_map/ppermute | solution.py:789
  28.0 5.4 %collective-permute-start = (f32[4,36,2,512]{3,2,1,0:T(2,128)}, f32[4,36,2,512]{3,2,1,0:T(2,128)S(1)}, u32[]{:S(2)}, u32[]{:S(2)}) collective-permute-start(f32[4,36,2,512]{3,2,1,0:T(2,128)} %get-tuple-element.33), channel_id=1, source_target_pairs={{0,8},{8,16},{16,24},{1,9},{9,17},{17,25},{2,10},{10,18},{18,26},{... | collective-permute-start | bytes 1769480 | tf_op jit(solution)/shard_map/ppermute | solution.py:757
  29.5 5.6 %collective-permute-start.1 = (f32[4,36,2,512]{3,2,1,0:T(2,128)}, f32[4,36,2,512]{3,2,1,0:T(2,128)S(1)}, u32[]{:S(2)}, u32[]{:S(2)}) collective-permute-start(f32[4,36,2,512]{3,2,1,0:T(2,128)} %get-tuple-element.34), channel_id=1, source_target_pairs={{8,0},{16,8},{24,16},{9,1},{17,9},{25,17},{10,2},{18,10},{26,18},{... | collective-permute-start | bytes 1769480 | tf_op jit(solution)/shard_map/ppermute | solution.py:757
  33.4 1.8 copy-start.5
  35.1 0.9 copy-start.6
  55.7 13.2 %copy-start.7 = (f32[2,32,512]{2,1,0:T(8,128)S(1)}, f32[2,32,512]{2,1,0:T(8,128)}, u32[]{:S(2)}) copy-start(f32[2,32,512]{2,1,0:T(8,128)} %get-tuple-element.39) | copy-start | bytes 393220
  57.3 1.0 copy-start.1
  58.4 10.6 %collective-permute-start.3 = (f32[2,32,512]{2,1,0:T(8,128)}, f32[2,32,512]{2,1,0:T(8,128)S(1)}, u32[]{:S(2)}, u32[]{:S(2)}) collective-permute-start(f32[2,32,512]{2,1,0:T(8,128)} %hold.6), channel_id=1, source_target_pairs={{0,1},{1,0},{2,3},{3,2},{4,5},{5,4},{6,7},{7,6},{8,9},{9,8},{10,11... | collective-permute-start | bytes 393224 | tf_op jit(solution)/shard_map/ppermute | solution.py:789
  69.6 9.4 %collective-permute-start.6 = (f32[2,32,512]{2,1,0:T(8,128)}, f32[2,32,512]{2,1,0:T(8,128)}, u32[]{:S(2)}, u32[]{:S(2)}) collective-permute-start(f32[2,32,512]{2,1,0:T(8,128)} %add.17), channel_id=1, source_target_pairs={{0,6},{1,7},{2,4},{3,5},{4,2},{5,3},{6,0},{7,1},{8,14},{9,15},{10,... | collective-permute-start | bytes 393224 | tf_op jit(solution)/shard_map/ppermute | solution.py:789
  72.6 12.7 %collective-permute-start.5 = (f32[2,32,512]{2,1,0:T(8,128)}, f32[2,32,512]{2,1,0:T(8,128)}, u32[]{:S(2)}, u32[]{:S(2)}) collective-permute-start(f32[2,32,512]{2,1,0:T(8,128)} %add.17), channel_id=1, source_target_pairs={{0,4},{1,5},{2,6},{3,7},{4,0},{5,1},{6,2},{7,3},{8,12},{9,13},{10,... | collective-permute-start | bytes 393224 | tf_op jit(solution)/shard_map/ppermute | solution.py:789
  72.9 12.4 %collective-permute-start.4 = (f32[2,32,512]{2,1,0:T(8,128)}, f32[2,32,512]{2,1,0:T(8,128)}, u32[]{:S(2)}, u32[]{:S(2)}) collective-permute-start(f32[2,32,512]{2,1,0:T(8,128)} %add.17), channel_id=1, source_target_pairs={{0,2},{1,3},{2,0},{3,1},{4,6},{5,7},{6,4},{7,5},{8,10},{9,11},{10,... | collective-permute-start | bytes 393224 | tf_op jit(solution)/shard_map/ppermute | solution.py:789
  74.0 82.3 %collective-permute-start.15 = (f32[144,8,512]{2,1,0:T(8,128)}, f32[144,8,512]{2,1,0:T(8,128)S(1)}, u32[]{:S(2)}, u32[]{:S(2)}) collective-permute-start(f32[144,8,512]{2,1,0:T(8,128)} %hold.11), channel_id=1, source_target_pairs={{0,1},{1,0},{2,3},{3,2},{4,5},{5,4},{6,7},{7,6},{8,9},{9,8},{10,11... | collective-permute-start | bytes 7077896 | tf_op jit(solution)/shard_map/ppermute | solution.py:789
  75.5 30.1 %collective-permute-start.9 = (f32[72,8,512]{2,1,0:T(8,128)}, f32[72,8,512]{2,1,0:T(8,128)S(1)}, u32[]{:S(2)}, u32[]{:S(2)}) collective-permute-start(f32[72,8,512]{2,1,0:T(8,128)} %collective-permute-done.8), channel_id=1, source_target_pairs={{3,1},{0,2},{5,3},{2,4},{7,5},{4,6},{11,9},{8,10},{13,11},{10,12},... | collective-permute-start | bytes 3538952 | tf_op jit(solution)/shard_map/ppermute | solution.py:789
  87.0 31.0 %collective-permute-start.13 = (f32[72,8,512]{2,1,0:T(8,128)}, f32[72,8,512]{2,1,0:T(8,128)}, u32[]{:S(2)}, u32[]{:S(2)}) collective-permute-start(f32[72,8,512]{2,1,0:T(8,128)} %hold.9), channel_id=1, source_target_pairs={{2,0},{1,3},{4,2},{3,5},{6,4},{5,7},{10,8},{9,11},{12,10},{11,13},... | collective-permute-start | bytes 3538952 | tf_op jit(solution)/shard_map/ppermute | solution.py:789
  88.3 52.4 %collective-permute-start.7 = (f32[40,8,512]{2,1,0:T(8,128)}, f32[40,8,512]{2,1,0:T(8,128)}, u32[]{:S(2)}, u32[]{:S(2)}) collective-permute-start(f32[40,8,512]{2,1,0:T(8,128)} %get-tuple-element.41), channel_id=1, source_target_pairs={{2,1},{1,0},{4,5},{3,2},{6,7},{5,6},{10,9},{9,8},{12,13},{11,10},{... | collective-permute-start | bytes 1966088 | tf_op jit(solution)/shard_map/ppermute | solution.py:789
  89.6 65.1 %collective-permute-start.11 = (f32[40,8,512]{2,1,0:T(8,128)}, f32[40,8,512]{2,1,0:T(8,128)}, u32[]{:S(2)}, u32[]{:S(2)}) collective-permute-start(f32[40,8,512]{2,1,0:T(8,128)} %get-tuple-element.46), channel_id=1, source_target_pairs={{2,1},{1,0},{4,2},{3,5},{6,7},{5,6},{10,9},{9,8},{12,10},{11,13},{... | collective-permute-start | bytes 1966088 | tf_op jit(solution)/shard_map/ppermute | solution.py:789
  105.6 12.4 %copy-start.2 = (f32[72,8,512]{2,1,0:T(8,128)}, f32[72,8,512]{2,1,0:T(8,128)S(1)}, u32[]{:S(2)}) copy-start(f32[72,8,512]{2,1,0:T(8,128)S(1)} %collective-permute-done.9.refs_5_.refs_0_.refs_1_) | copy-start | bytes 3538948
  118.0 61.1 %collective-permute-start.14 = (f32[72,8,512]{2,1,0:T(8,128)}, f32[72,8,512]{2,1,0:T(8,128)S(1)}, u32[]{:S(2)}, u32[]{:S(2)}) collective-permute-start(f32[72,8,512]{2,1,0:T(8,128)} %hold.10), channel_id=1, source_target_pairs={{0,1},{3,2},{2,3},{5,4},{4,5},{7,6},{8,9},{11,10},{10,11},{13,12},... | collective-permute-start | bytes 3538952 | tf_op jit(solution)/shard_map/ppermute | solution.py:789
  140.7 23.8 %collective-permute-start.10 = (f32[40,8,512]{2,1,0:T(8,128)}, f32[40,8,512]{2,1,0:T(8,128)}, u32[]{:S(2)}, u32[]{:S(2)}) collective-permute-start(f32[40,8,512]{2,1,0:T(8,128)} %hold.7), channel_id=1, source_target_pairs={{1,1},{0,2},{5,3},{2,4},{7,5},{6,6},{9,9},{8,10},{13,11},{10,12},{... | collective-permute-start | bytes 1966088 | tf_op jit(solution)/shard_map/ppermute | solution.py:789
  154.8 16.8 %collective-permute-start.12 = (f32[40,8,512]{2,1,0:T(8,128)}, f32[40,8,512]{2,1,0:T(8,128)S(1)}, u32[]{:S(2)}, u32[]{:S(2)}) collective-permute-start(f32[40,8,512]{2,1,0:T(8,128)} %hold.8), channel_id=1, source_target_pairs={{1,1},{0,2},{2,3},{5,4},{7,5},{6,6},{9,9},{8,10},{10,11},{13,12},{... | collective-permute-start | bytes 1966088 | tf_op jit(solution)/shard_map/ppermute | solution.py:789
  156.3 1.4 copy-start
  171.5 0.8 copy-start.4
  179.1 1.0 copy-start.3

commit v5 on v4

--- a/solution.py
+++ b/solution.py
@@ -26,9 +26,9 @@
 LANES = 128
 VMEM_BYTES = 56 * 1024 * 1024
 ROW_UNROLL = 9
-TURN_UNROLL = 3
-DELTA_UNROLL = 4
-SOURCE_UNROLL = 4
+TURN_UNROLL = 12
+DELTA_UNROLL = 6
+SOURCE_UNROLL = 6
 SOURCE_LANES = 256
 SPARE = 4
 COST = pl.CostEstimate(flops=1024, bytes_accessed=1024, transcendentals=0)
@@ -705,6 +705,14 @@
     return first, second
 
 
+def by_tile(count, tiles, even, odd):
+    steps = ([], [])
+    for tile in range(tiles):
+        for step, pairs in zip(steps, odd if tile % 2 else even):
+            step.extend((tile * count + source, tile * count + goal) for source, goal in pairs)
+    return steps
+
+
 def along_pairs(count):
     first, second = [], []
     for low in range(1, count - 1, 2):
@@ -798,14 +806,16 @@
         others = [send(sums, [(i, i ^ k) for i in range(spec_count)]) for k in (2, 4, 6)]
         sums = (sums + others[0]) + (others[1] + others[2])
         far_3 = send(hold(outer_sends[2], sums), along[0])
-        far_0 = [send(value, pairs[0]) for value, pairs in zip(outer_sends[:2], (some, most))]
+        mixed = by_tile(spec_count, geo_count, some, relay_pairs(spec_count, lambda rank: rank != 3))
+        far_0 = [lax.ppermute(outer_sends[0], ("geo", "spec"), mixed[0]), send(outer_sends[1], most[0])]
         far_1 = send(far_1, across[1])
         far_3 = send(hold(far_3, far_1), along[1])
         halo = members([far_1], near_1, 0)
         total_far = unpack(halo[:2], dir_count, back[1], None, land_sea)
         total_near = unpack(halo[2:], dir_count, back[1], None, land_sea)
         result, _ = finish(1, halo, None, None, True)
-        far_0 = [send(hold(value, result, total_far, total_near), pairs[1]) for value, pairs in zip(far_0, (some, most))]
+        far_0 = [hold(value, result, total_far, total_near) for value in far_0]
+        far_0 = [lax.ppermute(far_0[0], ("geo", "spec"), mixed[1]), send(far_0[1], most[1])]
         halo = {0: members(far_0, near, 0), 3: members([far_3], near, 2)}
         for s in (0, 3):
             total_near = unpack(halo[s][2:], dir_count, back[s], total_near, result)

time: 196 us -> 194 us (0.990)
    ppermute x14 -> x12, waiting for transfers between devices: 65 us -> 46.5 us  [send(): return lax.ppermute(value, 'spec', pairs)]
    ppermute x0 -> x2, waiting for transfers between devices: none -> 18 us  [the longest x1 10.8 us: shards(): lax.ppermute(outer_sends[0], ('geo', 'spec'), mixed[0])]
    ppermute x14 -> x12, starting transfers between devices: 27.3 us -> 24.5 us  [send(): return lax.ppermute(value, 'spec', pairs)]
    ppermute x0 -> x2, starting transfers between devices: none -> 2.79 us  [the longest x1 1.5 us: shards(): lax.ppermute(far_0[0], ('geo', 'spec'), mixed[1])]
  transfers between devices with their start and end apart: 16 -> 16, of which waited for: 9 -> 8; matrix products, arithmetic and copies ran while one was open for 3% -> 3% of each run, Pallas kernels for 31% -> 30%
where the time goes in v5:
time: 194 us; the launch traced here: 191 us
  Pallas kernels  83.1 us (43%)
  waiting for transfers between devices  66.2 us (34%)
  starting transfers between devices  30.1 us (16%)
  local copies, waits for them, and re-layouts  6.8 us (4%)
  other arithmetic  4.86 us (3%)
    ppermute x12, waiting for transfers between devices, send(): return lax.ppermute(value, 'spec', pairs)  46.5 us
    pallas_call x3, Pallas kernels, propagate(): pl.pallas_call(functools.partial(propagate_kernel, strips, dests, sends,...  40 us
    ppermute x12, starting transfers between devices, send(): return lax.ppermute(value, 'spec', pairs)  24.5 us
    pallas_call x4, Pallas kernels, unpack(): pl.pallas_call(functools.partial(unpack_kernel, places, len(extra)), grid...  13.3 us
    pallas_call x1, Pallas kernels, last_sources(): pl.pallas_call(functools.partial(last_kernel, dir_count, local_bands, hal...  12.6 us
    ppermute x1, waiting for transfers between devices, shards(): lax.ppermute(outer_sends[0], ('geo', 'spec'), mixed[0])  10.8 us
    pallas_call x2, Pallas kernels, source(): pl.pallas_call(functools.partial(source_kernel, dir_count, local_bands, p...  9.63 us
    pallas_call x3, Pallas kernels, plan(): pl.pallas_call(functools.partial(plan_kernel, kept, spill, wanted, back),...  7.67 us
  transfers between devices with their start and end apart: 16, of which 8 were waited for; matrix products, arithmetic and copies ran while one was open for 3% of the time, Pallas kernels for 30%

profile of v5, /device:TPU:0, one launch (start us, length us, event | category | flops | bytes accessed | tf_op | source)
XLA Modules:
  0.0 191.5 jit_solution(4655931744224033107)
XLA Ops:
  0.0 2.2 %plan.2.refs_6_.refs_9_ = bf16[512,512]{1,0:T(8,128)(2,1)} custom-call(s32[32,512]{1,0:T(8,128)} %refs_2_.15), custom_call_target="tpu_custom_call" | custom-call | tf_op jit(solution)/shard_map/plan/pallas_call | solution.py:112
  2.2 0.6 pad_add_fusion.refs_0_
  2.8 10.1 %propagate_inner.2 = (f32[2,36,8,512]{3,2,1,0:T(8,128)}, f32[2,36,8,512]{3,2,1,0:T(8,128)}, f32[72,8,512]{2,1,0:T(8,128)}, f32[2,32,512]{2,1,0:T(8,128)}, f32[4,...) custom-call(s32[2]{0:T(128)} %pad_add_fusion.refs_0_, f32[248]{0:T(256)} %constant.21.clone.refs_1_, ...), custom_call_target="tpu_custom_call" | custom-call | flops 1024 | bytes 1024 | tf_op jit(solution)/shard_map/propagate_inner/pallas_call | solution.py:355
  12.9 3.0 %collective-permute-start.2 = (f32[72,8,512]{2,1,0:T(8,128)}, f32[72,8,512]{2,1,0:T(8,128)S(1)}, u32[]{:S(2)}, u32[]{:S(2)}) collective-permute-start(f32[72,8,512]{2,1,0:T(8,128)} %get-tuple-element.40), channel_id=1, source_target_pairs={{0,1},{1,0},{2,3},{3,2},{4,5},{5,4},{6,7},{7,6},{8,9},{9,8},{10,11... | collective-permute-start | bytes 3538952 | tf_op jit(solution)/shard_map/ppermute | solution.py:797
  15.9 10.5 %propagate_inner.3 = (f32[2,36,8,512]{3,2,1,0:T(8,128)}, f32[2,36,8,512]{3,2,1,0:T(8,128)}, f32[72,8,512]{2,1,0:T(8,128)}, f32[2,32,512]{2,1,0:T(8,128)}, f32[4,...) custom-call(s32[2]{0:T(128)} %pad_add_fusion.refs_0_, f32[248]{0:T(256)} %constant.21.clone.refs_1_, ...), custom_call_target="tpu_custom_call" | custom-call | flops 1024 | bytes 1024 | tf_op jit(solution)/shard_map/propagate_inner/pallas_call | solution.py:355
  26.4 1.3 collective-permute-start.8
  27.7 1.5 collective-permute-start
  29.2 1.3 collective-permute-start.1
  30.5 2.6 %plan.3 = (bf16[512,512]{1,0:T(8,128)(2,1)}, bf16[512,512]{1,0:T(8,128)(2,1)}) custom-call(s32[32,512]{1,0:T(8,128)} %refs_2_.15), custom_call_target="tpu_custom_call" | custom-call | tf_op jit(solution)/shard_map/plan/pallas_call | solution.py:112
  33.1 1.8 collective-permute-done.1.refs_8_
  34.9 0.9 copy-done.6
  35.7 19.4 %propagate_edge.1 = (f32[4,36,8,512]{3,2,1,0:T(8,128)}, f32[4,36,8,512]{3,2,1,0:T(8,128)}, f32[40,8,512]{2,1,0:T(8,128)}, f32[40,8,512]{2,1,0:T(8,128)}, f32[72,...) custom-call(s32[2]{0:T(128)} %pad_add_fusion.refs_0_, f32[248]{0:T(256)} %constant.21.clone.refs_1_, ...), custom_call_target="tpu_custom_call" | custom-call | flops 1024 | bytes 1024 | tf_op jit(solution)/shard_map/propagate_edge/pallas_call | solution.py:355
  55.1 1.6 copy.16.refs_0_
  56.7 1.0 copy-done.1
  57.8 3.7 %collective-permute-start.3 = (f32[2,32,512]{2,1,0:T(8,128)}, f32[2,32,512]{2,1,0:T(8,128)S(1)}, u32[]{:S(2)}, u32[]{:S(2)}) collective-permute-start(f32[2,32,512]{2,1,0:T(8,128)} %hold.6), channel_id=1, source_target_pairs={{0,1},{1,0},{2,3},{3,2},{4,5},{5,4},{6,7},{7,6},{8,9},{9,8},{10,11... | collective-permute-start | bytes 393224 | tf_op jit(solution)/shard_map/ppermute | solution.py:797
  61.5 7.3 %collective-permute-done.3 = f32[2,32,512]{2,1,0:T(8,128)S(1)} collective-permute-done((f32[2,32,512]{2,1,0:T(8,128)}, f32[2,32,512]{2,1,0:T(8,128)S(1)}, u32[]{:S(2)}, u32[]{:S(2)}) %collective-permute-start.3) | collective-permute-done | bytes 131104 | tf_op jit(solution)/shard_map/ppermute | solution.py:797
  68.8 0.7 add.17
  69.5 3.0 %collective-permute-start.6 = (f32[2,32,512]{2,1,0:T(8,128)}, f32[2,32,512]{2,1,0:T(8,128)}, u32[]{:S(2)}, u32[]{:S(2)}) collective-permute-start(f32[2,32,512]{2,1,0:T(8,128)} %add.17), channel_id=1, source_target_pairs={{0,6},{1,7},{2,4},{3,5},{4,2},{5,3},{6,0},{7,1},{8,14},{9,15},{10,... | collective-permute-start | bytes 393224 | tf_op jit(solution)/shard_map/ppermute | solution.py:797
  72.4 0.3 collective-permute-start.5
  72.7 1.1 collective-permute-start.4
  73.9 1.5 collective-permute-start.15
  75.4 3.4 %collective-permute-start.9 = (f32[72,8,512]{2,1,0:T(8,128)}, f32[72,8,512]{2,1,0:T(8,128)S(1)}, u32[]{:S(2)}, u32[]{:S(2)}) collective-permute-start(f32[72,8,512]{2,1,0:T(8,128)} %collective-permute-done.8), channel_id=1, source_target_pairs={{3,1},{0,2},{5,3},{2,4},{7,5},{4,6},{11,9},{8,10},{13,11},{10,12},... | collective-permute-start | bytes 3538952 | tf_op jit(solution)/shard_map/ppermute | solution.py:797
  78.8 6.3 %collective-permute-done.5 = f32[2,32,512]{2,1,0:T(8,128)} collective-permute-done((f32[2,32,512]{2,1,0:T(8,128)}, f32[2,32,512]{2,1,0:T(8,128)}, u32[]{:S(2)}, u32[]{:S(2)}) %collective-permute-start.5) | collective-permute-done | bytes 131104 | tf_op jit(solution)/shard_map/ppermute | solution.py:797
  85.1 1.8 add_add_fusion.refs_4_.refs_1_
  86.9 1.3 collective-permute-start.13
  88.2 1.3 collective-permute-start.7
  89.5 1.3 collective-permute-start.11
  90.8 14.7 %collective-permute-done.9.refs_5_.refs_0_.refs_1_ = f32[72,8,512]{2,1,0:T(8,128)S(1)} collective-permute-done((f32[72,8,512]{2,1,0:T(8,128)}, f32[72,8,512]{2,1,0:T(8,128)S(1)}, u32[]{:S(2)}, u32[]{:S(2)}) %collective-permute-start.9) | collective-permute-done | bytes 1179680 | tf_op jit(solution)/shard_map/ppermute | solution.py:797
  105.5 12.4 %collective-permute-done.13.refs_0_ = f32[72,8,512]{2,1,0:T(8,128)} collective-permute-done((f32[72,8,512]{2,1,0:T(8,128)}, f32[72,8,512]{2,1,0:T(8,128)}, u32[]{:S(2)}, u32[]{:S(2)}) %collective-permute-start.13) | collective-permute-done | bytes 1179680 | tf_op jit(solution)/shard_map/ppermute | solution.py:797
  117.9 1.4 collective-permute-start.14
  119.3 2.9 %plan_back.1 = (bf16[512,512]{1,0:T(8,128)(2,1)}, bf16[512,512]{1,0:T(8,128)(2,1)}, bf16[512,512]{1,0:T(8,128)(2,1)}) custom-call(s32[32,512]{1,0:T(8,128)} %refs_2_.15), custom_call_target="tpu_custom_call" | custom-call | tf_op jit(solution)/shard_map/plan_back/pallas_call | solution.py:112
  122.2 1.1 multiply_bitcast_fusion.1
  123.3 0.7 pad_maximum_fusion.refs_3_
  124.0 3.2 %unpack.5.refs_3_.refs_2_ = f32[2,36,8,512]{3,2,1,0:T(8,128)} custom-call(f32[72,8,512]{2,1,0:T(8,128)} %copy-done.1, bf16[512,512]{1,0:T(8,128)(2,1)} %get-tuple-element.45.refs_1_, s32[32,512]{1,0:T(8,128)} %refs_2_.15), custom_call_target="tpu_custom_call" | custom-call | flops 1024 | bytes 1024 | tf_op jit(solution)/shard_map/unpack/pallas_call | solution.py:440
  127.2 3.3 %unpack.4.refs_2_ = f32[2,36,8,512]{3,2,1,0:T(8,128)} custom-call(f32[72,8,512]{2,1,0:T(8,128)} %copy-done.2, bf16[512,512]{1,0:T(8,128)(2,1)} %get-tuple-element.45.refs_1_, s32[32,512]{1,0:T(8,128)} %refs_2_.15), custom_call_target="tpu_custom_call" | custom-call | flops 1024 | bytes 1024 | tf_op jit(solution)/shard_map/unpack/pallas_call | solution.py:440
  130.5 4.8 %source.2.refs_1_.refs_3_.refs_9_ = f32[4,36,32,512]{3,2,1,0:T(8,128)} custom-call(s32[2]{0:T(128)} %pad_add_fusion.refs_0_, f32[248]{0:T(256)} %constant.21.clone.refs_1_, s32[32,512]{1,0:T(8,128)} %refs_2_.15, f32[2,32,512]{2,1,0:T(8,128)} %pad_maximum_fusion.refs_3_, f32[2,32,512]{2,1,0:T(8,128)} %add_add_fusion.refs_4_.refs_1_, f32[72,8,512]{2,1,0:T(8,128)} %copy-done.2, ...), custom_call_target="tpu_custom_call" | custom-call | flops 1024 | bytes 1024 | tf_op jit(solution)/shard_map/source/pallas_call | solution.py:669
  135.3 5.8 %collective-permute-done.7.refs_0_ = f32[40,8,512]{2,1,0:T(8,128)} collective-permute-done((f32[40,8,512]{2,1,0:T(8,128)}, f32[40,8,512]{2,1,0:T(8,128)}, u32[]{:S(2)}, u32[]{:S(2)}) %collective-permute-start.7) | collective-permute-done | bytes 655392 | tf_op jit(solution)/shard_map/ppermute | solution.py:797
  141.1 3.2 %collective-permute-start.10 = (f32[40,8,512]{2,1,0:T(8,128)}, f32[40,8,512]{2,1,0:T(8,128)}, u32[]{:S(2)}, u32[]{:S(2)}) collective-permute-start(f32[40,8,512]{2,1,0:T(8,128)} %hold.7), channel_id=1, source_target_pairs={{1,1},{0,2},{5,3},{2,4},{7,5},{6,6},{9,9},{8,10},{13,11},{10,12},{... | collective-permute-start | bytes 1966088 | tf_op jit(solution)/shard_map/ppermute | solution.py:797
  144.3 10.8 %collective-permute-done.11.refs_0_ = f32[40,8,512]{2,1,0:T(8,128)} collective-permute-done((f32[40,8,512]{2,1,0:T(8,128)}, f32[40,8,512]{2,1,0:T(8,128)}, u32[]{:S(2)}, u32[]{:S(2)}) %collective-permute-start.11) | collective-permute-done | bytes 655392 | tf_op jit(solution)/shard_map/ppermute | solution.py:810
  155.1 1.5 collective-permute-start.12
  156.6 1.4 copy-done
  158.1 3.4 %unpack.6.refs_2_ = f32[2,36,8,512]{3,2,1,0:T(8,128)} custom-call(f32[144,8,512]{2,1,0:T(8,128)} %copy-done, bf16[512,512]{1,0:T(8,128)(2,1)} %get-tuple-element.48.refs_1_.refs_9_, f32[2,36,8,512]{3,2,1,0:T(8,128)} %unpack.5.refs_3_.refs_2_, f32[4,36,32,512]{3,2,1,0:T(8,128)} %source.2.refs_1_.refs_3_.refs_9_), custom_call_target="tpu_custom_call" | custom-call | flops 1024 | bytes 1024 | tf_op jit(solution)/shard_map/unpack/pallas_call | solution.py:440
  161.5 3.4 %unpack.7 = f32[2,36,8,512]{3,2,1,0:T(8,128)} custom-call(f32[144,8,512]{2,1,0:T(8,128)} %copy-done, bf16[512,512]{1,0:T(8,128)(2,1)} %get-tuple-element.49.refs_1_.refs_10_, f32[2,36,8,512]{3,2,1,0:T(8,128)} %unpack.6.refs_2_, f32[4,36,32,512]{3,2,1,0:T(8,128)} %source.2.refs_1_.refs_3_.refs_9_), custom_call_target="tpu_custom_call" | custom-call | flops 1024 | bytes 1024 | tf_op jit(solution)/shard_map/unpack/pallas_call | solution.py:440
  164.9 7.2 %collective-permute-done.12.refs_6_ = f32[40,8,512]{2,1,0:T(8,128)S(1)} collective-permute-done((f32[40,8,512]{2,1,0:T(8,128)}, f32[40,8,512]{2,1,0:T(8,128)S(1)}, u32[]{:S(2)}, u32[]{:S(2)}) %collective-permute-start.12) | collective-permute-done | bytes 655392 | tf_op jit(solution)/shard_map/ppermute | solution.py:818
  172.1 0.8 copy-done.4
  172.9 4.8 %source.3.refs_17_ = f32[4,36,32,512]{3,2,1,0:T(8,128)} custom-call(s32[2]{0:T(128)} %pad_add_fusion.refs_0_, f32[248]{0:T(256)} %constant.21.clone.refs_1_, s32[32,512]{1,0:T(8,128)} %refs_2_.15, f32[2,32,512]{2,1,0:T(8,128)} %pad_maximum_fusion.refs_3_, f32[2,32,512]{2,1,0:T(8,128)} %add_add_fusion.refs_4_.refs_1_, ...), custom_call_target="tpu_custom_call", output_to_operand_aliasing={{}: (9, {})} | custom-call | flops 1024 | bytes 1024 | tf_op jit(solution)/shard_map/source/pallas_call | solution.py:669
  177.7 1.0 copy-done.3
  178.7 12.6 %last_sources.1 = f32[4,36,32,512]{3,2,1,0:T(8,128)} custom-call(s32[2]{0:T(128)} %pad_add_fusion.refs_0_, f32[248]{0:T(256)} %constant.21.clone.refs_1_, s32[32,512]{1,0:T(8,128)} %refs_2_.15, f32[2,32,512]{2,1,0:T(8,128)} %pad_maximum_fusion.refs_3_, f32[2,32,512]{2,1,0:T(8,128)} %add_add_fusion.refs_4_.refs_1_, ...), custom_call_target="tpu_custom_call", output_to_operand_aliasing={{}: (17, {})} | custom-call | flops 1024 | bytes 1024 | tf_op jit(solution)/shard_map/last_sources/pallas_call | solution.py:634
  (25 shorter events, 0.0 us)
Async XLA Ops:
  12.9 43.8 %collective-permute-start.2 = (f32[72,8,512]{2,1,0:T(8,128)}, f32[72,8,512]{2,1,0:T(8,128)S(1)}, u32[]{:S(2)}, u32[]{:S(2)}) collective-permute-start(f32[72,8,512]{2,1,0:T(8,128)} %get-tuple-element.40), channel_id=1, source_target_pairs={{0,1},{1,0},{2,3},{3,2},{4,5},{5,4},{6,7},{7,6},{8,9},{9,8},{10,11... | collective-permute-start | bytes 3538952 | tf_op jit(solution)/shard_map/ppermute | solution.py:797
  26.4 49.0 %collective-permute-start.8 = (f32[72,8,512]{2,1,0:T(8,128)}, f32[72,8,512]{2,1,0:T(8,128)}, u32[]{:S(2)}, u32[]{:S(2)}) collective-permute-start(f32[72,8,512]{2,1,0:T(8,128)} %get-tuple-element.42), channel_id=1, source_target_pairs={{2,3},{1,0},{4,5},{3,2},{6,7},{5,4},{10,11},{9,8},{12,13},{11,10},... | collective-permute-start | bytes 3538952 | tf_op jit(solution)/shard_map/ppermute | solution.py:797
  27.7 5.4 %collective-permute-start = (f32[4,36,2,512]{3,2,1,0:T(2,128)}, f32[4,36,2,512]{3,2,1,0:T(2,128)S(1)}, u32[]{:S(2)}, u32[]{:S(2)}) collective-permute-start(f32[4,36,2,512]{3,2,1,0:T(2,128)} %get-tuple-element.33), channel_id=1, source_target_pairs={{0,8},{8,16},{16,24},{1,9},{9,17},{17,25},{2,10},{10,18},{18,26},{... | collective-permute-start | bytes 1769480 | tf_op jit(solution)/shard_map/ppermute | solution.py:765
  29.2 5.6 %collective-permute-start.1 = (f32[4,36,2,512]{3,2,1,0:T(2,128)}, f32[4,36,2,512]{3,2,1,0:T(2,128)S(1)}, u32[]{:S(2)}, u32[]{:S(2)}) collective-permute-start(f32[4,36,2,512]{3,2,1,0:T(2,128)} %get-tuple-element.34), channel_id=1, source_target_pairs={{8,0},{16,8},{24,16},{9,1},{17,9},{25,17},{10,2},{18,10},{26,18},{... | collective-permute-start | bytes 1769480 | tf_op jit(solution)/shard_map/ppermute | solution.py:765
  33.1 1.8 copy-start.5
  34.8 0.9 copy-start.6
  55.1 13.7 %copy-start.7 = (f32[2,32,512]{2,1,0:T(8,128)S(1)}, f32[2,32,512]{2,1,0:T(8,128)}, u32[]{:S(2)}) copy-start(f32[2,32,512]{2,1,0:T(8,128)} %get-tuple-element.39) | copy-start | bytes 393220
  56.7 1.0 copy-start.1
  57.8 11.0 %collective-permute-start.3 = (f32[2,32,512]{2,1,0:T(8,128)}, f32[2,32,512]{2,1,0:T(8,128)S(1)}, u32[]{:S(2)}, u32[]{:S(2)}) collective-permute-start(f32[2,32,512]{2,1,0:T(8,128)} %hold.6), channel_id=1, source_target_pairs={{0,1},{1,0},{2,3},{3,2},{4,5},{5,4},{6,7},{7,6},{8,9},{9,8},{10,11... | collective-permute-start | bytes 393224 | tf_op jit(solution)/shard_map/ppermute | solution.py:797
  69.5 9.4 %collective-permute-start.6 = (f32[2,32,512]{2,1,0:T(8,128)}, f32[2,32,512]{2,1,0:T(8,128)}, u32[]{:S(2)}, u32[]{:S(2)}) collective-permute-start(f32[2,32,512]{2,1,0:T(8,128)} %add.17), channel_id=1, source_target_pairs={{0,6},{1,7},{2,4},{3,5},{4,2},{5,3},{6,0},{7,1},{8,14},{9,15},{10,... | collective-permute-start | bytes 393224 | tf_op jit(solution)/shard_map/ppermute | solution.py:797
  72.4 12.7 %collective-permute-start.5 = (f32[2,32,512]{2,1,0:T(8,128)}, f32[2,32,512]{2,1,0:T(8,128)}, u32[]{:S(2)}, u32[]{:S(2)}) collective-permute-start(f32[2,32,512]{2,1,0:T(8,128)} %add.17), channel_id=1, source_target_pairs={{0,4},{1,5},{2,6},{3,7},{4,0},{5,1},{6,2},{7,3},{8,12},{9,13},{10,... | collective-permute-start | bytes 393224 | tf_op jit(solution)/shard_map/ppermute | solution.py:797
  72.7 12.4 %collective-permute-start.4 = (f32[2,32,512]{2,1,0:T(8,128)}, f32[2,32,512]{2,1,0:T(8,128)}, u32[]{:S(2)}, u32[]{:S(2)}) collective-permute-start(f32[2,32,512]{2,1,0:T(8,128)} %add.17), channel_id=1, source_target_pairs={{0,2},{1,3},{2,0},{3,1},{4,6},{5,7},{6,4},{7,5},{8,10},{9,11},{10,... | collective-permute-start | bytes 393224 | tf_op jit(solution)/shard_map/ppermute | solution.py:797
  73.9 82.8 %collective-permute-start.15 = (f32[144,8,512]{2,1,0:T(8,128)}, f32[144,8,512]{2,1,0:T(8,128)S(1)}, u32[]{:S(2)}, u32[]{:S(2)}) collective-permute-start(f32[144,8,512]{2,1,0:T(8,128)} %hold.11), channel_id=1, source_target_pairs={{0,1},{1,0},{2,3},{3,2},{4,5},{5,4},{6,7},{7,6},{8,9},{9,8},{10,11... | collective-permute-start | bytes 7077896 | tf_op jit(solution)/shard_map/ppermute | solution.py:797
  75.4 30.1 %collective-permute-start.9 = (f32[72,8,512]{2,1,0:T(8,128)}, f32[72,8,512]{2,1,0:T(8,128)S(1)}, u32[]{:S(2)}, u32[]{:S(2)}) collective-permute-start(f32[72,8,512]{2,1,0:T(8,128)} %collective-permute-done.8), channel_id=1, source_target_pairs={{3,1},{0,2},{5,3},{2,4},{7,5},{4,6},{11,9},{8,10},{13,11},{10,12},... | collective-permute-start | bytes 3538952 | tf_op jit(solution)/shard_map/ppermute | solution.py:797
  86.9 31.0 %collective-permute-start.13 = (f32[72,8,512]{2,1,0:T(8,128)}, f32[72,8,512]{2,1,0:T(8,128)}, u32[]{:S(2)}, u32[]{:S(2)}) collective-permute-start(f32[72,8,512]{2,1,0:T(8,128)} %hold.9), channel_id=1, source_target_pairs={{2,0},{1,3},{4,2},{3,5},{6,4},{5,7},{10,8},{9,11},{12,10},{11,13},... | collective-permute-start | bytes 3538952 | tf_op jit(solution)/shard_map/ppermute | solution.py:797
  88.2 52.8 %collective-permute-start.7 = (f32[40,8,512]{2,1,0:T(8,128)}, f32[40,8,512]{2,1,0:T(8,128)}, u32[]{:S(2)}, u32[]{:S(2)}) collective-permute-start(f32[40,8,512]{2,1,0:T(8,128)} %get-tuple-element.41), channel_id=1, source_target_pairs={{2,1},{1,0},{4,5},{3,2},{6,7},{5,6},{10,9},{9,8},{12,13},{11,10},{... | collective-permute-start | bytes 1966088 | tf_op jit(solution)/shard_map/ppermute | solution.py:797
  89.5 65.6 %collective-permute-start.11 = (f32[40,8,512]{2,1,0:T(8,128)}, f32[40,8,512]{2,1,0:T(8,128)}, u32[]{:S(2)}, u32[]{:S(2)}) collective-permute-start(f32[40,8,512]{2,1,0:T(8,128)} %get-tuple-element.46), channel_id=1, source_target_pairs={{2,1},{1,0},{4,2},{3,5},{6,7},{5,6},{10,11},{9,8},{12,10},{11,13},... | collective-permute-start | bytes 1966088 | tf_op jit(solution)/shard_map/ppermute | solution.py:810
  105.5 12.4 %copy-start.2 = (f32[72,8,512]{2,1,0:T(8,128)}, f32[72,8,512]{2,1,0:T(8,128)S(1)}, u32[]{:S(2)}) copy-start(f32[72,8,512]{2,1,0:T(8,128)S(1)} %collective-permute-done.9.refs_5_.refs_0_.refs_1_) | copy-start | bytes 3538948
  117.9 59.8 %collective-permute-start.14 = (f32[72,8,512]{2,1,0:T(8,128)}, f32[72,8,512]{2,1,0:T(8,128)S(1)}, u32[]{:S(2)}, u32[]{:S(2)}) collective-permute-start(f32[72,8,512]{2,1,0:T(8,128)} %hold.10), channel_id=1, source_target_pairs={{0,1},{3,2},{2,3},{5,4},{4,5},{7,6},{8,9},{11,10},{10,11},{13,12},... | collective-permute-start | bytes 3538952 | tf_op jit(solution)/shard_map/ppermute | solution.py:797
  141.1 23.8 %collective-permute-start.10 = (f32[40,8,512]{2,1,0:T(8,128)}, f32[40,8,512]{2,1,0:T(8,128)}, u32[]{:S(2)}, u32[]{:S(2)}) collective-permute-start(f32[40,8,512]{2,1,0:T(8,128)} %hold.7), channel_id=1, source_target_pairs={{1,1},{0,2},{5,3},{2,4},{7,5},{6,6},{9,9},{8,10},{13,11},{10,12},{... | collective-permute-start | bytes 1966088 | tf_op jit(solution)/shard_map/ppermute | solution.py:797
  155.1 17.0 %collective-permute-start.12 = (f32[40,8,512]{2,1,0:T(8,128)}, f32[40,8,512]{2,1,0:T(8,128)S(1)}, u32[]{:S(2)}, u32[]{:S(2)}) collective-permute-start(f32[40,8,512]{2,1,0:T(8,128)} %hold.8), channel_id=1, source_target_pairs={{1,1},{0,2},{2,3},{5,4},{7,5},{6,6},{11,9},{8,10},{10,11},{13,12},... | collective-permute-start | bytes 1966088 | tf_op jit(solution)/shard_map/ppermute | solution.py:818
  156.6 1.4 copy-start
  172.1 0.8 copy-start.4
  177.7 1.0 copy-start.3
